TPU v7x, 32 devices: a whole 2x2x4 slice. The times are simulated.
32 devices in a mesh: doc: 16 (over z, x, core), pair: 2 (over y).
Axes of the slice: x: 2, y: 2, z: 4, core: 2. Of those that a mesh axis runs over, the one named last changes fastest.
Arguments:
- hidden_in: bfloat16 [16384, 768], P(('doc', 'pair')), may hold values from -6 to 6
- cotangent: bfloat16 [16384, 768], P(('doc', 'pair')), may hold values from -6 to 6
- span_lengths: int32 [128], P(('doc', 'pair')), may hold values from 32 to 128, as said below
- partner_span: int32 [16, 4], P('doc'), may hold values from 0 to 3, each once within a row
- query_weight: bfloat16 [768, 768], P(('doc', 'pair')), may hold values from -0.21875 to 0.21875
- query_bias: bfloat16 [768], P(('doc', 'pair')), may hold values from -3 to 3
- key_weight: bfloat16 [768, 768], P(('doc', 'pair')), may hold values from -0.21875 to 0.21875
- value_weight: bfloat16 [768, 768], P(('doc', 'pair')), may hold values from -0.21875 to 0.21875
- value_bias: bfloat16 [768], P(('doc', 'pair')), may hold values from -3 to 3
- output_weight: bfloat16 [768, 768], P(('doc', 'pair')), may hold values from -0.625 to 0.625
- output_bias: bfloat16 [768], P(('doc', 'pair')), may hold values from -3 to 3
- first_gain: bfloat16 [768], P(('doc', 'pair')), may hold values from 0.5 to 1.5
- first_shift: bfloat16 [768], P(('doc', 'pair')), may hold values from -2 to 2
- inner_weight: bfloat16 [768, 3072], P(('doc', 'pair')), may hold values from -0.21875 to 0.21875
- inner_bias: bfloat16 [3072], P(('doc', 'pair')), may hold values from -3 to 3
- outer_weight: bfloat16 [3072, 768], P(('doc', 'pair')), may hold values from -0.109375 to 0.109375
- outer_bias: bfloat16 [768], P(('doc', 'pair')), may hold values from -3 to 3
- second_gain: bfloat16 [768], P(('doc', 'pair')), may hold values from 0.5 to 1.5
- second_shift: bfloat16 [768], P(('doc', 'pair')), may hold values from -3 to 3
Outputs:
- layer_out: bfloat16 [16384, 768], P(('doc', 'pair'))
- input_gradient: bfloat16 [16384, 768], P(('doc', 'pair'))
- span_loss: float32 [128], P(('doc', 'pair'))
- query_weight_gradient: float32 [768, 768], P(('doc', 'pair'))
- query_bias_gradient: float32 [768], P(('doc', 'pair'))
- key_weight_gradient: float32 [768, 768], P(('doc', 'pair'))
- value_weight_gradient: float32 [768, 768], P(('doc', 'pair'))
- value_bias_gradient: float32 [768], P(('doc', 'pair'))
- output_weight_gradient: float32 [768, 768], P(('doc', 'pair'))
- output_bias_gradient: float32 [768], P(('doc', 'pair'))
- first_gain_gradient: float32 [768], P(('doc', 'pair'))
- first_shift_gradient: float32 [768], P(('doc', 'pair'))
- inner_weight_gradient: float32 [768, 3072], P(('doc', 'pair'))
- inner_bias_gradient: float32 [3072], P(('doc', 'pair'))
- outer_weight_gradient: float32 [3072, 768], P(('doc', 'pair'))
- outer_bias_gradient: float32 [768], P(('doc', 'pair'))
- second_gain_gradient: float32 [768], P(('doc', 'pair'))
- second_shift_gradient: float32 [768], P(('doc', 'pair'))
Inputs may be any that keep to these rules, and one draw needn't show every extreme that they name: A span's live tokens fill the first span_lengths of its 128 slots; the rest is padding. `partner_span`: each row is a permutation of the 4 spans of a document's second partner.
All inputs are finite; a program needn't handle non-finite values.
Results may differ from a plain program's by a relative error of at most 0.014.
Values may be sent and summed in bfloat16 or wider, within the bound.
No kernel may reach another device: no remote copies, remote signals or barrier semaphores. Data moves between devices by JAX's collectives and lax.ppermute only.
A program may use at most 192 MiB of HBM per device.

v0:
```python
from functools import partial
import math

import jax
import jax.numpy as jnp
from jax import lax
from jax.experimental import pallas as pl
from jax.experimental.pallas import tpu as pltpu
from jax.sharding import PartitionSpec as P

D = 768
HEAD_DIM = 64
SPAN = 128
SPANS_ROW = 4


epsilon = 1e-06
masked_out = -1000000000.0
highest = lax.Precision.HIGHEST


def across(block, mask):
    count = lax.axis_size("doc")
    return lax.ppermute(block, "doc", [(at, at ^ mask) for at in range(count)])


def mate(block):
    return lax.ppermute(block, "pair", [(0, 1), (1, 0)])


def far_groups():
    bits = lax.axis_size("doc").bit_length() - 1
    far = [1 << at for at in range(2, bits)]
    return [far[at : at + 2] for at in range(0, len(far), 2)]


def is_upper(mask):
    return (lax.axis_index("doc") & mask) != 0


def joined(own, other, upper):
    return jnp.where(upper, jnp.stack([other, own]), jnp.stack([own, other]))


def gather_rows(block):
    rows, columns = block.shape
    total = block[None]
    for masks in far_groups():
        low = masks[0]
        near = joined(total, across(total, low), is_upper(low))
        if len(masks) == 2:
            high = masks[1]
            straight, crossed = across(total, high), across(total, high | low)
            far = joined(straight, crossed, is_upper(low))
            near = joined(near, far, is_upper(high)).reshape((4,) + total.shape)
        total = near.reshape((-1, rows, columns))
    half = columns // 2
    left, right = total[..., :half], total[..., half:]
    on_pair = lax.axis_index("pair") == 1
    left_x, right_y = across(left, 2), mate(right)
    left, right = joined(left, left_x, is_upper(2)), joined(right, right_y, on_pair)
    left_y, right_x = mate(left), across(right, 2)
    left, right = joined(left, left_y, on_pair), joined(right, right_x, is_upper(2))
    left = joined(left, across(left, 1), is_upper(1))
    right = joined(right, across(right, 1), is_upper(1))
    left = jnp.transpose(left, (3, 2, 0, 1, 4, 5))
    right = jnp.transpose(right, (3, 1, 0, 2, 4, 5))
    return jnp.concatenate([left, right], axis=-1).reshape(-1, rows, columns)


def halves(blocks, axis, upper):
    lower = lax.index_in_dim(blocks, 0, axis, keepdims=False)
    higher = lax.index_in_dim(blocks, 1, axis, keepdims=False)
    return (jnp.where(upper, higher, lower), jnp.where(upper, lower, higher))


def plus(kept, received):
    return kept.astype(jnp.float32) + received.astype(jnp.float32)


def scatter_rows(blocks):
    rows, columns = blocks.shape[1:]
    on_pair = lax.axis_index("pair") == 1
    blocks = blocks.astype(jnp.bfloat16).reshape(-1, 2, 2, 2, rows, columns)
    kept, sent = halves(blocks, 2, is_upper(1))
    total = plus(kept, across(sent, 1)).astype(jnp.bfloat16)
    half = columns // 2
    left, right = total[..., :half], total[..., half:]
    left_kept, left_sent = halves(left, 2, on_pair)
    right_kept, right_sent = halves(right, 1, is_upper(2))
    left = plus(left_kept, mate(left_sent)).astype(jnp.bfloat16)
    right = plus(right_kept, across(right_sent, 2)).astype(jnp.bfloat16)
    left_kept, left_sent = halves(left, 1, is_upper(2))
    right_kept, right_sent = halves(right, 1, on_pair)
    left = plus(left_kept, across(left_sent, 2))
    right = plus(right_kept, mate(right_sent))
    total = jnp.concatenate([left, right], axis=-1)
    for masks in far_groups()[::-1]:
        total = total.astype(jnp.bfloat16).reshape(2 ** len(masks), -1, rows, columns)
        place = (lax.axis_index("doc") // masks[0]) % 2 ** len(masks)
        summed = lax.dynamic_index_in_dim(total, place, 0, keepdims=False).astype(jnp.float32)
        for step in range(1, 2 ** len(masks)):
            sent = lax.dynamic_index_in_dim(total, place ^ step, 0, keepdims=False)
            summed = plus(summed, across(sent, masks[0] * step))
        total = summed
    return total.reshape(rows, columns)


VECTORS = (1, 4, 6, 7, 8, 10, 12, 13, 14)


def pack_vectors(pieces):
    flat = jnp.concatenate(pieces, axis=-1)
    width = -(-flat.shape[-1] // D) * D
    flat = jnp.pad(flat, [(0, 0)] * (flat.ndim - 1) + [(0, width - flat.shape[-1])])
    return flat.reshape(flat.shape[:-1] + (-1, D))


def fold(matrix):
    return jnp.concatenate([matrix[:, at : at + D] for at in range(0, matrix.shape[1], D)])


def collect(shards):
    rows = shards[0].shape[0]
    devices = lax.axis_size("doc") * lax.axis_size("pair")
    small = pack_vectors([shards[at] for at in VECTORS])
    first = gather_rows(jnp.concatenate([shards[0], shards[2], shards[3], small]))
    second = gather_rows(jnp.concatenate([shards[5], fold(shards[9])]))
    outer = lax.all_gather(shards[11], ("doc", "pair"), axis=0, tiled=True)
    whole = {
        0: first[:, :rows].reshape(-1, D),
        2: first[:, rows : 2 * rows].reshape(-1, D),
        3: first[:, 2 * rows : 3 * rows].reshape(-1, D),
        5: second[:, :rows].reshape(-1, D),
        9: jnp.concatenate(
            [
                second[:, at : at + rows].reshape(-1, D)
                for at in range(rows, second.shape[1], rows)
            ],
            axis=1,
        ),
        11: outer,
    }
    vectors, start = first[:, 3 * rows :].reshape(devices, -1), 0
    for at in VECTORS:
        size = shards[at].shape[0]
        whole[at] = vectors[:, start : start + size].reshape(-1).astype(jnp.float32)
        start += size
    return tuple(whole[at] for at in range(15))


def spread(gradients):
    devices = lax.axis_size("doc") * lax.axis_size("pair")
    by_device = [
        piece.reshape((devices, -1) + piece.shape[1:]) for piece in gradients
    ]
    rows = by_device[0].shape[1]
    outer = scatter_rows(by_device[11])
    inner = by_device[9]
    parts = [inner[..., at : at + D] for at in range(0, inner.shape[-1], D)]
    second = scatter_rows(jnp.concatenate([by_device[5]] + parts, axis=1))
    small = pack_vectors([by_device[at] for at in VECTORS])
    first = scatter_rows(
        jnp.concatenate([by_device[0], by_device[2], by_device[3], small], axis=1)
    )
    own = {
        0: first[:rows],
        2: first[rows : 2 * rows],
        3: first[2 * rows : 3 * rows],
        5: second[:rows],
        9: jnp.concatenate(
            [second[at : at + rows] for at in range(rows, second.shape[0], rows)], axis=1
        ),
        11: outer,
    }
    vectors, start = first[3 * rows :].reshape(-1), 0
    for at in VECTORS:
        size = by_device[at].shape[1]
        own[at] = vectors[start : start + size]
        start += size
    return tuple(own[at] for at in range(15))


def normalize(hidden, gain, shift):
    average = jnp.mean(hidden, axis=-1, keepdims=True)
    centred = hidden - average
    factor = lax.rsqrt(jnp.mean(centred * centred, axis=-1, keepdims=True) + epsilon)
    normed = centred * factor
    return (normed * gain + shift, normed, factor)


def normalize_back(upstream, normed, factor, gain):
    scaled = upstream * gain
    hidden_grad = factor * (
        scaled
        - jnp.mean(scaled, axis=-1, keepdims=True)
        - normed * jnp.mean(scaled * normed, axis=-1, keepdims=True)
    )
    return (hidden_grad, jnp.sum(upstream * normed, axis=0), jnp.sum(upstream, axis=0))


def head_scores(query_row, key_row, live_row):
    product = jnp.einsum("sqhd,skhd->shqk", query_row, key_row, preferred_element_type=jnp.float32)
    return jnp.where(live_row[:, None, None, :], product * HEAD_DIM ** (-0.5), masked_out)


def encode(hidden_in, allowed, gathered):
    (
        query_mat,
        query_add,
        key_mat,
        value_mat,
        value_add,
        output_mat,
        output_add,
        gain_one,
        shift_one,
        inner_mat,
        inner_add,
        outer_mat,
        outer_add,
        gain_two,
        shift_two,
    ) = gathered
    row_count = allowed.shape[0]
    shaped = (row_count, SPANS_ROW, SPAN, D // HEAD_DIM, HEAD_DIM)
    queries = (
        jnp.dot(hidden_in, query_mat, preferred_element_type=jnp.float32) + query_add
    ).astype(jnp.bfloat16)
    key_rows = jnp.dot(hidden_in, key_mat, preferred_element_type=jnp.float32).astype(jnp.bfloat16)
    value_rows = (
        jnp.dot(hidden_in, value_mat, preferred_element_type=jnp.float32) + value_add
    ).astype(jnp.bfloat16)

    def attend(element):
        query_row, key_row, value_row, live_row = element
        scores = head_scores(query_row, key_row, live_row)
        highest_score = jnp.max(scores, axis=-1, keepdims=True)
        exponent = jnp.exp(scores - highest_score)
        totals = jnp.sum(exponent, axis=-1, keepdims=True)
        attention = (exponent / totals).astype(jnp.bfloat16)
        context_row = jnp.einsum(
            "shqk,skhd->sqhd", attention, value_row, preferred_element_type=jnp.float32
        )
        return (context_row.astype(jnp.bfloat16), (highest_score + jnp.log(totals))[..., 0])

    context, logsum = lax.map(
        attend,
        (queries.reshape(shaped), key_rows.reshape(shaped), value_rows.reshape(shaped), allowed),
    )
    context = context.reshape(-1, D)
    residual = (
        hidden_in.astype(jnp.float32)
        + jnp.dot(context, output_mat, preferred_element_type=jnp.float32)
        + output_add
    )
    first_out, first_normed, first_factor = normalize(residual, gain_one, shift_one)
    first16 = first_out.astype(jnp.bfloat16)
    preact = jnp.dot(first16, inner_mat, preferred_element_type=jnp.float32) + inner_add
    active = jax.nn.gelu(preact, approximate=False).astype(jnp.bfloat16)
    second = first_out + jnp.dot(active, outer_mat, preferred_element_type=jnp.float32) + outer_add
    encoded, second_normed, second_factor = normalize(second, gain_two, shift_two)
    stored = (
        queries,
        key_rows,
        value_rows,
        logsum,
        context,
        first_normed,
        first_factor,
        first16,
        preact,
        active,
        second_normed,
        second_factor,
    )
    return (encoded, stored)


def backward(hidden_in, allowed, gathered, stored, out_gradient):
    (
        query_mat,
        query_add,
        key_mat,
        value_mat,
        value_add,
        output_mat,
        output_add,
        gain_one,
        shift_one,
        inner_mat,
        inner_add,
        outer_mat,
        outer_add,
        gain_two,
        shift_two,
    ) = gathered
    (
        queries,
        key_rows,
        value_rows,
        logsum,
        context,
        first_normed,
        first_factor,
        first16,
        preact,
        active,
        second_normed,
        second_factor,
    ) = stored
    row_count = allowed.shape[0]
    shaped = (row_count, SPANS_ROW, SPAN, D // HEAD_DIM, HEAD_DIM)
    second_grad, gain_two_grad, shift_two_grad = normalize_back(
        out_gradient, second_normed, second_factor, gain_two
    )
    outer_add_grad = jnp.sum(second_grad, axis=0)
    second16 = second_grad.astype(jnp.bfloat16)
    outer_mat_grad = jnp.dot(active.T, second16, preferred_element_type=jnp.float32)
    active_grad = jnp.dot(second16, outer_mat.T, preferred_element_type=jnp.float32)
    unused, gelu_back = jax.vjp(partial(jax.nn.gelu, approximate=False), preact)
    preact_grad = gelu_back(active_grad)[0]
    inner_add_grad = jnp.sum(preact_grad, axis=0)
    preact16 = preact_grad.astype(jnp.bfloat16)
    inner_mat_grad = jnp.dot(first16.T, preact16, preferred_element_type=jnp.float32)
    first_grad = second_grad + jnp.dot(preact16, inner_mat.T, preferred_element_type=jnp.float32)
    residual_grad, gain_one_grad, shift_one_grad = normalize_back(
        first_grad, first_normed, first_factor, gain_one
    )
    output_add_grad = jnp.sum(residual_grad, axis=0)
    residual16 = residual_grad.astype(jnp.bfloat16)
    output_mat_grad = jnp.dot(context.T, residual16, preferred_element_type=jnp.float32)
    context_grad = jnp.dot(residual16, output_mat.T, preferred_element_type=jnp.float32).astype(
        jnp.bfloat16
    )

    def attend_back(element):
        query_row, key_row, value_row, live_row, logsum_row, context_row = element
        scores = head_scores(query_row, key_row, live_row)
        attention = jnp.exp(scores - logsum_row[..., None])
        attention16 = attention.astype(jnp.bfloat16)
        value_grad = jnp.einsum(
            "shqk,sqhd->skhd", attention16, context_row, preferred_element_type=jnp.float32
        )
        attention_grad = jnp.einsum(
            "sqhd,skhd->shqk", context_row, value_row, preferred_element_type=jnp.float32
        )
        weighted = jnp.sum(attention * attention_grad, axis=-1, keepdims=True)
        scores_grad = (attention * (attention_grad - weighted)).astype(jnp.bfloat16)
        query_grad = jnp.einsum(
            "shqk,skhd->sqhd", scores_grad, key_row, preferred_element_type=jnp.float32
        ) * HEAD_DIM ** (-0.5)
        key_grad = jnp.einsum(
            "shqk,sqhd->skhd", scores_grad, query_row, preferred_element_type=jnp.float32
        ) * HEAD_DIM ** (-0.5)
        return (
            query_grad.astype(jnp.bfloat16),
            key_grad.astype(jnp.bfloat16),
            value_grad.astype(jnp.bfloat16),
        )

    query_grad, key_grad, value_grad = lax.map(
        attend_back,
        (
            queries.reshape(shaped),
            key_rows.reshape(shaped),
            value_rows.reshape(shaped),
            allowed,
            logsum,
            context_grad.reshape(shaped),
        ),
    )
    query_grad = query_grad.reshape(-1, D)
    key_grad = key_grad.reshape(-1, D)
    value_grad = value_grad.reshape(-1, D)
    query_add_grad = jnp.sum(query_grad.astype(jnp.float32), axis=0)
    value_add_grad = jnp.sum(value_grad.astype(jnp.float32), axis=0)
    query_mat_grad = jnp.dot(hidden_in.T, query_grad, preferred_element_type=jnp.float32)
    key_mat_grad = jnp.dot(hidden_in.T, key_grad, preferred_element_type=jnp.float32)
    value_mat_grad = jnp.dot(hidden_in.T, value_grad, preferred_element_type=jnp.float32)
    input_grad = (
        residual_grad
        + jnp.dot(query_grad, query_mat.T, preferred_element_type=jnp.float32)
        + jnp.dot(key_grad, key_mat.T, preferred_element_type=jnp.float32)
        + jnp.dot(value_grad, value_mat.T, preferred_element_type=jnp.float32)
    )
    gradients = (
        query_mat_grad,
        query_add_grad,
        key_mat_grad,
        value_mat_grad,
        value_add_grad,
        output_mat_grad,
        output_add_grad,
        gain_one_grad,
        shift_one_grad,
        inner_mat_grad,
        inner_add_grad,
        outer_mat_grad,
        outer_add_grad,
        gain_two_grad,
        shift_two_grad,
    )
    return (input_grad, gradients)


def per_device(
    hidden_in,
    cotangent,
    span_lengths,
    partner_span,
    query_weight,
    query_bias,
    key_weight,
    value_weight,
    value_bias,
    output_weight,
    output_bias,
    first_gain,
    first_shift,
    inner_weight,
    inner_bias,
    outer_weight,
    outer_bias,
    second_gain,
    second_shift,
):
    shards = (
        query_weight,
        query_bias,
        key_weight,
        value_weight,
        value_bias,
        output_weight,
        output_bias,
        first_gain,
        first_shift,
        inner_weight,
        inner_bias,
        outer_weight,
        outer_bias,
        second_gain,
        second_shift,
    )
    length = SPAN * SPANS_ROW
    row_count = hidden_in.shape[0] // length
    allowed = jnp.arange(SPAN)[None, None, :] < span_lengths.reshape(row_count, SPANS_ROW, 1)
    gathered = collect(shards)
    encoded, stored = encode(hidden_in, allowed, gathered)
    cls_rows = (
        encoded.reshape(row_count, SPANS_ROW, SPAN, D)[:, :, 0, :]
        .reshape(-1, D)
        .astype(jnp.bfloat16)
    )
    other_rows = mate(cls_rows)
    logits = jnp.dot(cls_rows, other_rows.T, preferred_element_type=jnp.float32) / math.sqrt(D)
    span_count = cls_rows.shape[0]
    matches = (partner_span.reshape(span_count, 1) == jnp.arange(span_count)[None, :]).astype(
        jnp.float32
    )
    target = jnp.where(lax.axis_index("pair") == 0, matches, matches.T)
    highest_logit = jnp.max(logits, axis=-1, keepdims=True)
    exponent = jnp.exp(logits - highest_logit)
    totals = jnp.sum(exponent, axis=-1, keepdims=True)
    span_loss = highest_logit[:, 0] + jnp.log(totals[:, 0]) - jnp.sum(target * logits, axis=-1)
    softened = exponent / totals - target
    own_grad = jnp.dot(softened, other_rows.astype(jnp.float32), precision=highest)
    other_logits = logits.T
    other_highest = jnp.max(other_logits, axis=-1, keepdims=True)
    other_exponent = jnp.exp(other_logits - other_highest)
    other_softened = (
        other_exponent / jnp.sum(other_exponent, axis=-1, keepdims=True) - target.T
    )
    back_grad = jnp.dot(
        other_softened.T, other_rows.astype(jnp.float32), precision=highest
    ).astype(jnp.bfloat16)
    cls_gradient = (own_grad + back_grad.astype(jnp.float32)).reshape(row_count, SPANS_ROW, 1, D)
    placed = jnp.concatenate(
        [cls_gradient, jnp.zeros((row_count, SPANS_ROW, SPAN - 1, D), jnp.float32)], axis=2
    )
    out_gradient = cotangent.astype(jnp.float32) + placed.reshape(-1, D)
    input_grad, gradients = backward(hidden_in, allowed, gathered, stored, out_gradient)
    reduced = spread(gradients)
    return (encoded.astype(jnp.bfloat16), input_grad.astype(jnp.bfloat16), span_loss) + tuple(
        reduced
    )


ROW = 24
PLACES = 8


def coordinates():
    doc = lax.axis_index("doc")
    return (doc & 1, (doc >> 1) & 1, doc >> 2, lax.axis_index("pair"))


def permutations():
    core, x_at, z_at, y_at = coordinates()
    row = jnp.arange(D, dtype=jnp.int32)
    block, inside = row // ROW, row % ROW
    y_off, x_off = (block & 1) ^ y_at, ((block >> 2) & 1) ^ x_at
    block_core, z_off = (block >> 1) & 1, (block >> 3) ^ z_at
    arrived = ((((block_core ^ core) * 2 + y_off) * 2 + x_off) * 4 + z_off) * ROW + inside
    leaving = ((y_off * 2 + x_off) * 4 + z_off) * 2 * ROW + block_core * ROW + inside
    restore = (arrived[:, None] == row[None, :]).astype(jnp.bfloat16)
    arrange = (leaving[None, :] == row[:, None]).astype(jnp.bfloat16)
    return (restore, arrange)


def after(value, *others):
    return lax.optimization_barrier((value,) + others)[0]


def z_exchange(block):
    return [across(block, mask) for mask in (4, 8, 12)]


def tied(values, *others):
    return lax.optimization_barrier(tuple(values) + others)[: len(values)]


def near_exchange(block):
    return across(block[0], 2), mate(block[1])


def stack_near(block, received):
    return stack_pair(block[0], received[0], block[1], received[1])


def far_exchange(block):
    return mate(block[0]), across(block[1], 2)


def core_exchange(block):
    return across(block[0], 1), across(block[1], 1)


def pieces_of(near, far, core, far_core):
    return [near[0], far[0], near[1], far[1], core[0], far_core[0], core[1], far_core[1]]


VMEM = pl.BlockSpec(memory_space=pltpu.VMEM)
SMEM = pl.BlockSpec(memory_space=pltpu.SMEM)


def full(shape):
    return pl.BlockSpec(shape, lambda *at: (0,) * len(shape))


class Fetched:
    def __init__(self, source, held, semaphore):
        self.copy, self.held, self.waiting = pltpu.make_async_copy(source, held, semaphore), held, True
        self.shape = held.shape
        self.copy.start()

    def ready(self):
        if self.waiting:
            self.copy.wait()
            self.waiting = False
        return self.held

    def __getitem__(self, at):
        return self.ready()[at]


class Stored:
    def __init__(self, target, held, semaphores):
        self.target, self.held, self.semaphores, self.copies = target, held, semaphores, []
        self.shape = held.shape

    def __getitem__(self, at):
        return self.held[at]

    def __setitem__(self, at, value):
        self.held[at] = value

    def done(self, at=None):
        semaphore = self.semaphores.at[len(self.copies)]
        held, target = (self.held, self.target) if at is None else (self.held.at[at], self.target.at[at])
        self.copies.append(pltpu.make_async_copy(held, target, semaphore))
        self.copies[-1].start()


PARTS = 8


def run(kernel, name, operands, results, flops, scratch=(), mib=12):
    in_hbm = pl.BlockSpec(memory_space=pltpu.HBM)
    spaces = {"S": SMEM, "V": VMEM, "H": in_hbm, "A": in_hbm}
    in_places = [place for _, place in operands]
    out_places = [place for _, _, place in results]
    staged = [pltpu.VMEM(array.shape, array.dtype) for array, place in operands if place == "H"]
    made = [pltpu.VMEM(shape, dtype) for shape, dtype, place in results if place == "H"]
    semaphores = [pltpu.SemaphoreType.DMA((max(1, len(staged)),))]
    semaphores += [pltpu.SemaphoreType.DMA((max(1, len(made)), PARTS))]

    def body(*refs):
        ins, refs = refs[: len(operands)], refs[len(operands) :]
        outs, refs = refs[: len(results)], refs[len(results) :]
        held_in, refs = refs[: len(staged)], refs[len(staged) :]
        held_out, refs = refs[: len(made)], refs[len(made) :]
        fetching, storing, own = refs[0], refs[1], refs[2:]
        arguments, at = [], 0
        for ref, place in zip(ins, in_places):
            if place == "H":
                ref, at = Fetched(ref, held_in[at], fetching.at[at]), at + 1
            arguments.append(ref)
        inputs, at = list(arguments), 0
        for ref, place in zip(outs, out_places):
            if place == "H":
                ref, at = Stored(ref, held_out[at], storing.at[at]), at + 1
            arguments.append(ref)
        kernel(*arguments, *own)
        for ref in inputs:
            if isinstance(ref, Fetched):
                ref.ready()
        made_here = [ref for ref in arguments if isinstance(ref, Stored)]
        for ref in made_here:
            if not ref.copies:
                ref.done()
        for ref in made_here:
            for copy in ref.copies:
                copy.wait()

    size = lambda shape, dtype: math.prod(shape) * jnp.dtype(dtype).itemsize
    inside = sum(size(array.shape, array.dtype) for array, place in operands if place == "H")
    inside += sum(size(shape, dtype) for shape, dtype, place in results if place == "H")
    mib = mib + inside // 2**20
    return pl.pallas_call(
        body,
        in_specs=[spaces[place] for place in in_places],
        out_specs=[spaces[place] for place in out_places],
        out_shape=[jax.ShapeDtypeStruct(shape, dtype) for shape, dtype, _ in results],
        scratch_shapes=staged + made + semaphores + list(scratch),
        compiler_params=params(mib),
        cost_estimate=cost(1, 1),
        name=name,
    )(*[array for array, _ in operands])


def placed_at(place, *arrays):
    return [(array, place) for array in arrays]


bf16, f32 = jnp.bfloat16, jnp.float32


def params(mib=16):
    return pltpu.CompilerParams(vmem_limit_bytes=mib << 20)


def cost(flops, moved):
    return pl.CostEstimate(flops=int(flops), bytes_accessed=int(moved), transcendentals=0)


def dot(left, right):
    return jnp.dot(left, right, preferred_element_type=jnp.float32)


def dot_nt(left, right):
    return lax.dot_general(
        left, right, (((1,), (1,)), ((), ())), preferred_element_type=jnp.float32
    )


def dot_tn(left, right):
    return lax.dot_general(
        left, right, (((0,), (0,)), ((), ())), preferred_element_type=jnp.float32
    )


def pack_kernel(*refs):
    query, key, value, output, inner, inner_bias = refs[:6]
    vectors, (first, second, turned) = refs[6:-3], refs[-3:]
    turned[...] = jnp.zeros_like(turned)
    for at, vector in enumerate(vectors):
        turned[at : at + 1, :ROW] = vector[...].astype(jnp.float32)
    bias = inner_bias[...].astype(jnp.float32)
    for at in range(4):
        turned[8 + at : 9 + at, :ROW] = bias[:, at * ROW : (at + 1) * ROW]
    small = jnp.transpose(turned[...])[:ROW].astype(jnp.bfloat16)
    first[:, :D] = query[...]
    first[:, D : D + 512] = key[:, :512]
    first[:, D + 512 : D + 640] = small
    first[:, D + 640 : D + 768] = jnp.zeros_like(small)
    first[:, D + 768 : D + 1024] = key[:, 512:]
    first[:, D + 1024 :] = value[...]
    second[:, :D] = output[...]
    second[:, D:] = inner[...]


def pack(query, key, value, output, inner, inner_bias, vectors):
    rows = [vector.reshape(1, -1) for vector in (inner_bias, *vectors)]
    return run(
        pack_kernel,
        "pack",
        placed_at("H", query, key, value, output, inner, *rows),
        [((ROW, 2 * FIRST_HALF), bf16, "V"), ((ROW, D + inner.shape[1]), bf16, "V")],
        1e6,
        [pltpu.VMEM((128, 128), f32)],
        mib=58,
    )


def stack_z_kernel(split, first, second, third, fourth, left, right):
    blocks = [ref[...].astype(jnp.float32) for ref in (first, second, third, fourth)]
    whole = jnp.concatenate(blocks).astype(jnp.bfloat16)
    left[...] = whole[:, :split]
    right[...] = whole[:, split:]


def stack_z(block, received, split):
    rows, columns = block.shape
    return pl.pallas_call(
        partial(stack_z_kernel, split),
        in_specs=[VMEM] * 4,
        out_specs=[VMEM] * 2,
        out_shape=[
            jax.ShapeDtypeStruct((4 * rows, split), jnp.bfloat16),
            jax.ShapeDtypeStruct((4 * rows, columns - split), jnp.bfloat16),
        ],
        compiler_params=params(),
        cost_estimate=cost(1, 1),
        name="stack_z",
    )(block, *received)


def stack_pair_kernel(left, left_in, right, right_in, left_out, right_out):
    for own, received, out in ((left, left_in, left_out), (right, right_in, right_out)):
        rows = own.shape[0]
        out[:rows, :] = own[...]
        out[rows:, :] = received[...]


def stack_pair(left, left_in, right, right_in):
    double = lambda block: jax.ShapeDtypeStruct((2 * block.shape[0], block.shape[1]), block.dtype)
    return pl.pallas_call(
        stack_pair_kernel,
        in_specs=[VMEM] * 4,
        out_specs=[VMEM] * 2,
        out_shape=[double(left), double(right)],
        compiler_params=params(),
        cost_estimate=cost(1, 1),
        name="stack_pair",
    )(left, left_in, right, right_in)


def left_tile(refs, columns):
    return jnp.concatenate([ref[:, columns] for ref in refs])


def right_tile(refs, columns):
    near, far, other_near, other_far = refs
    rows = near.shape[0] // 2
    order = [(near, 0), (far, 0), (near, 1), (far, 1)]
    order += [(other_near, 0), (other_far, 0), (other_near, 1), (other_far, 1)]
    return jnp.concatenate([ref[at * rows : (at + 1) * rows, columns] for ref, at in order])


def in_order(pieces):
    left, left_far, right, right_far, c_left, c_left_far, c_right, c_right_far = pieces
    return (left, left_far, c_left, c_left_far, right, right_far, c_right, c_right_far)


FIRST_HALF = 1280
SECOND_HALF = 1792
def head_pair(pair, low):
    nothing = jnp.zeros_like(pair)
    return jnp.concatenate([jnp.where(low, pair, nothing), jnp.where(low, nothing, pair)])


def key_columns(left_rows, right_rows, rows, at):
    if at < 512:
        return left_rows[rows, D + at : D + at + 128]
    return right_rows[rows, at - 256 : at - 128]


def front_kernel(
    lengths,
    hidden,
    restore,
    arrange,
    l0,
    l1,
    l2,
    l3,
    r0,
    r1,
    r2,
    r3,
    left_rows,
    right_rows,
    vectors,
    attention_out,
    context_arrived,
    hidden_t,
    context_t,
    context,
):
    tokens = hidden.shape[0]
    hidden_t[...] = dot_nt(arrange[...], hidden[...]).astype(jnp.bfloat16)
    moved = dot(hidden[...], restore[...]).astype(jnp.bfloat16)
    small = dot(restore[...], right_tile((r0, r1, r2, r3), slice(0, 128)))
    turned = jnp.transpose(small)[:16]
    vectors[...] = turned
    for at in range(0, FIRST_HALF, 256):
        columns = slice(at, at + 256)
        rows = dot(moved, left_tile((l0, l1, l2, l3), columns))
        if at < D:
            rows += turned[0:1, columns]
        left_rows[:, columns] = rows.astype(jnp.bfloat16)
        if at == 0:
            right_rows[:, columns] = jnp.zeros((tokens, 256), jnp.bfloat16)
            continue
        rows = dot(moved, right_tile((r0, r1, r2, r3), columns))
        if at >= 512:
            rows += turned[1:2, at - 512 : at - 256]
        right_rows[:, columns] = rows.astype(jnp.bfloat16)
    low = lax.broadcasted_iota(jnp.int32, (SPAN, 128), 1) < HEAD_DIM

    def attend(span, carry):
        rows = pl.ds(pl.multiple_of(span * SPAN, SPAN), SPAN)
        live = lax.broadcasted_iota(jnp.int32, (SPAN, SPAN), 1) < lengths[span]
        for at in range(0, D, 128):
            query = left_rows[rows, at : at + 128]
            keys = head_pair(key_columns(left_rows, right_rows, rows, at), low)
            values = head_pair(right_rows[rows, 512 + at : 640 + at], low)
            scores = dot_nt(query, keys) * HEAD_DIM ** (-0.5)
            parts = []
            for head in range(2):
                part = jnp.where(live, scores[:, head * SPAN : (head + 1) * SPAN], masked_out)
                exponent = jnp.exp(part - jnp.max(part, axis=-1, keepdims=True))
                parts.append(
                    (exponent * (1.0 / jnp.sum(exponent, axis=-1, keepdims=True))).astype(jnp.bfloat16)
                )
            attention = jnp.concatenate(parts, axis=1)
            attention_out[rows, 2 * at : 2 * at + 256] = attention
            context[rows, at : at + 128] = dot(attention, values).astype(jnp.bfloat16)
        return carry

    lax.fori_loop(0, tokens // SPAN, attend, 0)
    context_arrived[...] = dot(context[...], restore[...]).astype(jnp.bfloat16)
    context_t[...] = dot_nt(arrange[...], context[...]).astype(jnp.bfloat16)


def front(lengths, hidden, restore, arrange, pieces):
    tokens = hidden.shape[0]
    return run(
        front_kernel,
        "front",
        [(lengths, "S")] + placed_at("H", hidden, restore, arrange, *in_order(pieces)),
        [
            ((tokens, FIRST_HALF), bf16, "H"),
            ((tokens, FIRST_HALF), bf16, "H"),
            ((16, D), f32, "V"),
            ((tokens, 2 * D), bf16, "H"),
            ((tokens, D), bf16, "H"),
            ((D, tokens), bf16, "H"),
            ((D, tokens), bf16, "H"),
        ],
        9e9,
        [pltpu.VMEM((tokens, D), bf16)],
    )


def gelu_parts(preact):
    scaled = jnp.abs(preact) * (0.5**0.5)
    near = 1.0 / (1.0 + 0.3275911 * scaled)
    poly = near * (
        0.254829592
        + near * (-0.284496736 + near * (1.421413741 + near * (-1.453152027 + near * 1.061405429)))
    )
    bell = jnp.exp(-0.5 * preact * preact)
    tail = 0.5 * poly * bell
    below = jnp.where(preact < 0.0, tail, 1.0 - tail)
    return (preact * below, below + preact * bell * (0.5 / math.pi) ** 0.5)


FF_TILE = 512


def second_tiles(left, right):
    for at in range(D, SECOND_HALF, FF_TILE):
        yield at - D, left_tile(left, slice(at, at + FF_TILE))
    for at in range(0, right[0].shape[1], FF_TILE):
        yield SECOND_HALF - D + at, right_tile(right, slice(at, at + FF_TILE))


def vector_places():
    for device in range(D // ROW):
        for part in range(4):
            yield (8 + part, device * ROW), (device * 4 + part) * ROW


def middle_kernel(
    hidden,
    context_arrived,
    restore,
    arrange,
    vectors,
    l0,
    l1,
    l2,
    l3,
    r0,
    r1,
    r2,
    r3,
    active,
    active_t,
    slope,
    normed_out,
    factor_out,
    first_t,
    inner_bias,
):
    for at, column in vector_places():
        inner_bias[:, column : column + ROW] = vectors[at[0] : at[0] + 1, at[1] : at[1] + ROW]
    left, right = (l0, l1, l2, l3), (r0, r1, r2, r3)
    residual = hidden[...].astype(jnp.float32) + vectors[2:3, :]
    residual += dot(context_arrived[...], left_tile(left, slice(0, D)))
    first_out, normed, factor = normalize(residual, vectors[3:4, :], vectors[4:5, :])
    normed_out[...] = normed
    factor_out[...] = factor
    first16 = first_out.astype(jnp.bfloat16)
    first_t[...] = dot_nt(arrange[...], first16).astype(jnp.bfloat16)
    normed_out.done()
    first_t.done()
    moved = dot(first16, restore[...]).astype(jnp.bfloat16)
    for at, tile in second_tiles(left, right):
        columns = slice(at, at + FF_TILE)
        value, derivative = gelu_parts(dot(moved, tile) + inner_bias[:, columns])
        value16 = value.astype(jnp.bfloat16)
        active[:, columns] = value16
        active_t[columns, :] = jnp.transpose(value16)
        slope[:, columns] = derivative.astype(jnp.bfloat16)
        active.done((slice(None), columns))
        active_t.done((columns, slice(None)))
        slope.done((slice(None), columns))


def middle(hidden, context_arrived, restore, arrange, vectors, ff, pieces):
    tokens = hidden.shape[0]
    return run(
        middle_kernel,
        "middle",
        placed_at("H", hidden, context_arrived, restore, arrange)
        + placed_at("V", vectors)
        + placed_at("H", *in_order(pieces)),
        [
            ((tokens, ff), bf16, "H"),
            ((ff, tokens), bf16, "H"),
            ((tokens, ff), bf16, "H"),
            ((tokens, D), f32, "H"),
            ((tokens, 1), f32, "V"),
            ((D, tokens), bf16, "H"),
        ],
        8e9,
        [pltpu.VMEM((1, ff), f32)],
    )


def natural_rows(place, pieces, target, semaphore):
    rows = 4 * ROW
    for at, piece in enumerate(pieces):
        half = piece.shape[1]
        is_right, core_off, far_off = at // 4, at // 2 % 2, at % 2
        for near_off in range(2):
            for z_off in range(4):
                x_off, y_off = (far_off, near_off) if is_right else (near_off, far_off)
                block = ((z_off ^ place[3]) * 2 + (x_off ^ place[2])) * 2 + (core_off ^ place[0])
                block = block * 2 + (y_off ^ place[1])
                to = pl.ds(pl.multiple_of(block * rows, rows), rows)
                pltpu.make_async_copy(
                    piece.at[pl.ds((near_off * 4 + z_off) * rows, rows), :],
                    target.at[to, pl.ds(is_right * half, half)],
                    semaphore,
                ).start()
    pltpu.make_async_copy(target, target, semaphore).wait()


def last_kernel(
    place,
    active,
    first_normed,
    vectors,
    l0,
    l1,
    l2,
    l3,
    r0,
    r1,
    r2,
    r3,
    layer_out,
    normed_out,
    factor_out,
    cls_rows,
    outer_mat,
    semaphore,
):
    natural_rows(place, (l0, l1, l2, l3, r0, r1, r2, r3), outer_mat, semaphore)
    total = first_normed[...] * vectors[3:4, :] + vectors[4:5, :] + vectors[5:6, :]
    total += dot(active[...], outer_mat[...])
    encoded, normed, factor = normalize(total, vectors[6:7, :], vectors[7:8, :])
    layer_out[...] = encoded.astype(jnp.bfloat16)
    normed_out[...] = normed
    factor_out[...] = factor
    for span in range(encoded.shape[0] // SPAN):
        cls_rows[span : span + 1, :] = encoded[span * SPAN : span * SPAN + 1].astype(jnp.bfloat16)


def last(place, active, first_normed, vectors, pieces):
    tokens, ff = active.shape
    return run(
        last_kernel,
        "last",
        [(place, "S")]
        + placed_at("H", active, first_normed)
        + [(vectors, "V")]
        + placed_at("A", *in_order(pieces)),
        [
            ((tokens, D), bf16, "H"),
            ((tokens, D), f32, "V"),
            ((tokens, 1), f32, "V"),
            ((tokens // SPAN, D), bf16, "V"),
            ((ff, D), bf16, "V"),
        ],
        2.5e9,
        [pltpu.SemaphoreType.DMA],
    )


def pick(place, first, second):
    return jnp.where(place == 0, first, second)


def turn_kernel(
    place,
    partner_span,
    cotangent,
    normed,
    factor,
    vectors,
    own_rows,
    other_rows,
    second_grad,
    kept,
    sent,
    sums,
    loss,
):
    spans = own_rows.shape[0]
    own, other = own_rows[...].astype(jnp.float32), other_rows[...].astype(jnp.float32)
    logits = dot_nt(own_rows[...], other_rows[...]) / math.sqrt(D)
    row = lax.broadcasted_iota(jnp.int32, (spans, spans), 0)
    column = lax.broadcasted_iota(jnp.int32, (spans, spans), 1)
    first_place = place[1] == 0
    target = jnp.zeros((spans, spans), jnp.float32)
    for span in range(spans):
        match = partner_span[0, span]
        hit_row = jnp.where(first_place, span, match)
        hit_column = jnp.where(first_place, match, span)
        target += ((row == hit_row) & (column == hit_column)).astype(jnp.float32)
    highest_logit = jnp.max(logits, axis=1, keepdims=True)
    exponent = jnp.exp(logits - highest_logit)
    totals = jnp.sum(exponent, axis=1, keepdims=True)
    losses = highest_logit + jnp.log(totals) - jnp.sum(target * logits, axis=1, keepdims=True)
    loss[...] = jnp.sum(jnp.where(row == column, losses, 0.0), axis=0, keepdims=True)
    soft = exponent / totals - target
    exponent = jnp.exp(logits - jnp.max(logits, axis=0, keepdims=True))
    back = exponent / jnp.sum(exponent, axis=0, keepdims=True) - target
    own_term, back_term = jnp.zeros_like(own), jnp.zeros_like(own)
    for span in range(spans):
        own_term += soft[:, span : span + 1] * other[span : span + 1]
        back_term += back[:, span : span + 1] * other[span : span + 1]
    cls_gradient = own_term + back_term.astype(jnp.bfloat16).astype(jnp.float32)
    start = lax.broadcasted_iota(jnp.int32, (SPAN, 1), 0) == 0
    gain = vectors[6:7, :]
    gain_sum = jnp.zeros((1, D), jnp.float32)
    shift_sum, bias_sum = gain_sum, gain_sum
    for span in range(spans):
        rows = slice(span * SPAN, (span + 1) * SPAN)
        upstream = cotangent[rows, :].astype(jnp.float32)
        upstream += jnp.where(start, cls_gradient[span : span + 1], 0.0)
        grad, gain_part, shift_part = normalize_back(upstream, normed[rows, :], factor[rows, :], gain)
        second_grad[rows, :] = grad
        gain_sum += gain_part[None]
        shift_sum += shift_part[None]
        bias_sum += jnp.sum(grad, axis=0, keepdims=True)
        grad16 = grad.astype(jnp.bfloat16)
        kept[rows, :] = pick(place[0], grad16[:, : D // 2], grad16[:, D // 2 :])
        sent[rows, :] = pick(place[0], grad16[:, D // 2 :], grad16[:, : D // 2])
    sums[0:1, :] = bias_sum
    sums[1:2, :] = gain_sum
    sums[2:3, :] = shift_sum


def turn(place, partner_span, cotangent, normed, factor, vectors, own_rows, other_rows):
    tokens = cotangent.shape[0]
    return run(
        turn_kernel,
        "turn",
        placed_at("S", place, partner_span)
        + [(cotangent, "H")]
        + placed_at("V", normed, factor, vectors, own_rows, other_rows),
        [
            ((tokens, D), f32, "H"),
            ((tokens, D // 2), bf16, "V"),
            ((tokens, D // 2), bf16, "V"),
            ((3, D), f32, "V"),
            ((1, own_rows.shape[0]), f32, "V"),
        ],
        1e8,
    )


def both_halves(place, kept, sent):
    return jnp.concatenate([pick(place, kept, sent), pick(place, sent, kept)], axis=1)


def slope_kernel(place, second_kept, second_sent, outer_mat, slope, kept, sent, sums):
    second16 = both_halves(place[0], second_kept[...], second_sent[...])
    half = kept.shape[1]
    for at in range(0, 2 * half, D):
        columns, inside = slice(at, at + D), slice(at % half, at % half + D)
        grad = dot_nt(second16, outer_mat[columns, :]) * slope[:, columns].astype(jnp.float32)
        sums[:, columns] = jnp.sum(grad, axis=0, keepdims=True)
        grad16 = grad.astype(jnp.bfloat16)
        mine = place[0] == at // half

        @pl.when(mine)
        def keep():
            kept[:, inside] = grad16

        @pl.when(jnp.logical_not(mine))
        def send():
            sent[:, inside] = grad16


def slope_back(place, second_kept, second_sent, outer_mat, slope):
    tokens, ff = slope.shape
    half = ((tokens, ff // 2), bf16, "V")
    return run(
        slope_kernel,
        "slope_back",
        [(place, "S")] + placed_at("V", second_kept, second_sent, outer_mat) + [(slope, "H")],
        [half, half, ((1, ff), f32, "V")],
        2.5e9,
    )


def outer_kernel(place, active_t, other_active_t, kept, received, left_kept, left_sent, right_kept, right_sent):
    rows = 2 * ROW
    active_t, other_active_t = active_t.ready(), other_active_t.ready()

    def chip_rows(chip, carry):
        x_off, z_off = (chip & 1) ^ place[2], (chip >> 1) ^ place[3]
        tile = pl.ds(pl.multiple_of(chip * 8 * rows, 8 * rows), 8 * rows)
        grad = dot(active_t[tile, :], kept[...]) + dot(other_active_t[tile, :], received[...])
        grad = grad.astype(jnp.bfloat16)
        for core in range(2):
            for y_at in range(2):
                start = (core * 2 + y_at) * 2 * rows
                left, right = grad[start : start + rows], grad[start + rows : start + 2 * rows]
                y_off = place[1] ^ y_at
                left_at = (x_off * 4 + z_off) * 2 + core
                right_at = (y_off * 4 + z_off) * 2 + core

                @pl.when(y_off == 0)
                def left_here():
                    left_kept[left_at] = left

                @pl.when(y_off == 1)
                def left_there():
                    left_sent[left_at] = left

                @pl.when(x_off == 0)
                def right_here():
                    right_kept[right_at] = right

                @pl.when(x_off == 1)
                def right_there():
                    right_sent[right_at] = right

        return carry

    lax.fori_loop(0, PLACES, chip_rows, 0)


def outer_gradient(place, active_t, other_active_t, kept, received):
    piece = ((2 * PLACES, 2 * ROW, kept.shape[1]), bf16, "V")
    return run(
        outer_kernel,
        "outer_gradient",
        [(place, "S")] + placed_at("H", active_t, other_active_t) + placed_at("V", kept, received),
        [piece] * 4,
        2.5e9,
    )


def whole_precision(left, right):
    high = left.astype(jnp.bfloat16)
    rest = (left - high.astype(jnp.float32)).astype(jnp.bfloat16)
    return dot_nt(high, right) + dot_nt(rest, right)


def first_kernel(
    place,
    preact_kept,
    preact_sent,
    second_grad,
    normed,
    factor,
    vectors,
    restore,
    l0,
    l1,
    l2,
    l3,
    r0,
    r1,
    r2,
    r3,
    residual_grad,
    kept,
    sent,
    context_grad,
    sums,
):
    left, right = (l0, l1, l2, l3), (r0, r1, r2, r3)
    total = jnp.zeros(second_grad.shape, jnp.float32)
    half = preact_kept.shape[1]
    for at, tile in second_tiles(left, right):
        columns = slice(at % half, at % half + FF_TILE)
        kept_part, sent_part = preact_kept[:, columns], preact_sent[:, columns]
        if at >= half:
            kept_part, sent_part = sent_part, kept_part
        total += dot_nt(pick(place[0], kept_part, sent_part), tile)
    first_grad = second_grad[...] + whole_precision(total, restore[...])
    grad, gain_sum, shift_sum = normalize_back(first_grad, normed[...], factor[...], vectors[3:4, :])
    residual_grad[...] = grad
    sums[0:1, :] = jnp.sum(grad, axis=0, keepdims=True)
    sums[1:2, :] = gain_sum[None]
    sums[2:3, :] = shift_sum[None]
    grad16 = grad.astype(jnp.bfloat16)
    kept[...] = pick(place[0], grad16[:, : D // 2], grad16[:, D // 2 :])
    sent[...] = pick(place[0], grad16[:, D // 2 :], grad16[:, : D // 2])
    moved = dot_nt(grad16, left_tile(left, slice(0, D))).astype(jnp.bfloat16)
    context_grad[...] = dot_nt(moved, restore[...]).astype(jnp.bfloat16)


def first_back(place, preact_kept, preact_sent, second_grad, normed, factor, vectors, restore, pieces):
    tokens = second_grad.shape[0]
    half = ((tokens, D // 2), bf16, "V")
    return run(
        first_kernel,
        "first_back",
        [(place, "S")]
        + placed_at("V", preact_kept, preact_sent)
        + placed_at("H", second_grad, normed)
        + placed_at("V", factor, vectors)
        + placed_at("H", restore, *in_order(pieces)),
        [((tokens, D), f32, "H"), half, half, ((tokens, D), bf16, "V"), ((3, D), f32, "V")],
        4.9e9,
    )


def part_rows(grad, left_kept, left_sent, right_kept, right_sent, is_left):
    quarter = D // 4
    if is_left:
        left_kept[...] = grad[: 2 * quarter]
        left_sent[...] = grad[2 * quarter :]
    else:
        right_kept[:quarter, :] = grad[:quarter]
        right_sent[:quarter, :] = grad[quarter : 2 * quarter]
        right_kept[quarter:, :] = grad[2 * quarter : 3 * quarter]
        right_sent[quarter:, :] = grad[3 * quarter :]


def inner_kernel(first_t, other_first_t, kept, received, left_kept, left_sent, right_kept, right_sent):
    for is_left in (True, False):
        columns = slice(0, D) if is_left else slice(D, 2 * D)
        grad = dot(first_t[...], kept[:, columns]) + dot(other_first_t[...], received[:, columns])
        part_rows(grad.astype(jnp.bfloat16), left_kept, left_sent, right_kept, right_sent, is_left)


def inner_gradient(first_t, other_first_t, kept, received):
    piece = ((D // 2, kept.shape[1] // 2), bf16, "V")
    return run(
        inner_kernel,
        "inner_gradient",
        placed_at("H", first_t, other_first_t) + placed_at("V", kept, received),
        [piece] * 4,
        2.5e9,
    )


def attend_kernel(
    place,
    context_grad,
    left_rows,
    right_rows,
    attention_in,
    first_sums,
    second_sums,
    inner_sums,
    kept,
    sent,
    sums,
    grads,
):
    tokens = context_grad.shape[0]
    low = lax.broadcasted_iota(jnp.int32, (SPAN, 128), 1) < HEAD_DIM
    scale = HEAD_DIM ** (-0.5)
    left_rows, right_rows, attention_in = [ref.ready() for ref in (left_rows, right_rows, attention_in)]

    def attend(span, carry):
        rows = pl.ds(pl.multiple_of(span * SPAN, SPAN), SPAN)
        for at in range(0, D, 128):
            query = left_rows[rows, at : at + 128]
            keys = head_pair(key_columns(left_rows, right_rows, rows, at), low)
            values = head_pair(right_rows[rows, 512 + at : 640 + at], low)
            upstream = context_grad[rows, at : at + 128]
            attention16 = attention_in[rows, 2 * at : 2 * at + 256]
            attention_grad = dot_nt(upstream, values)
            parts = []
            for head in range(2):
                columns = slice(head * SPAN, (head + 1) * SPAN)
                attention = attention16[:, columns].astype(jnp.float32)
                part = attention_grad[:, columns]
                weighted = jnp.sum(attention * part, axis=-1, keepdims=True)
                parts.append((attention * (part - weighted)).astype(jnp.bfloat16))
            scores_grad = jnp.concatenate(parts, axis=1)
            grads[0, rows, at : at + 128] = (dot(scores_grad, keys) * scale).astype(jnp.bfloat16)
            both = dot_tn(scores_grad, query)
            both = jnp.where(low, both[:SPAN], both[SPAN:])
            grads[1, rows, at : at + 128] = (both * scale).astype(jnp.bfloat16)
            both = dot_tn(attention16, upstream)
            both = jnp.where(low, both[:SPAN], both[SPAN:])
            grads[2, rows, at : at + 128] = both.astype(jnp.bfloat16)
        return carry

    lax.fori_loop(0, tokens // SPAN, attend, 0)
    query_grad, key_grad, value_grad = grads[0], grads[1], grads[2]
    half = D // 2
    for at, grad in enumerate((query_grad, key_grad, value_grad)):
        columns = slice(at * half, (at + 1) * half)
        kept[:, columns] = pick(place[0], grad[:, :half], grad[:, half:])
        sent[:, columns] = pick(place[0], grad[:, half:], grad[:, :half])
    sums[0:1, :] = jnp.sum(query_grad.astype(jnp.float32), axis=0, keepdims=True)
    sums[1:2, :] = jnp.sum(value_grad.astype(jnp.float32), axis=0, keepdims=True)
    sums[2:5, :] = first_sums[...]
    sums[5:8, :] = second_sums[...]
    for at, column in vector_places():
        sums[at[0] : at[0] + 1, at[1] : at[1] + ROW] = inner_sums[:, column : column + ROW]
    sums[12:16, :] = jnp.zeros((4, D), jnp.float32)


def attend_back(place, context_grad, left_rows, right_rows, attention, first_sums, second_sums, inner_sums):
    tokens = context_grad.shape[0]
    part = ((tokens, 3 * D // 2), bf16, "V")
    return run(
        attend_kernel,
        "attend_back",
        placed_at("S", place)
        + placed_at("V", context_grad)
        + placed_at("H", left_rows, right_rows, attention)
        + placed_at("V", first_sums, second_sums, inner_sums),
        [part, part, ((16, D), f32, "V")],
        4e9,
        [pltpu.VMEM((3, tokens, D), bf16)],
    )


def attention_gradient_kernel(
    arrange,
    sums,
    other_sums,
    hidden_t,
    other_hidden_t,
    context_t,
    other_context_t,
    grads,
    other_grads,
    residual,
    other_residual,
    left_kept,
    left_sent,
    right_kept,
    right_sent,
):
    half = D // 2
    grad = dot(hidden_t[...], grads[:, :D]) + dot(other_hidden_t[...], other_grads[:, :D])
    grad = grad.astype(jnp.bfloat16)
    left_kept[:, :D] = grad[:half]
    left_sent[:, :D] = grad[half:]
    total = (sums[...] + other_sums[...]).astype(jnp.bfloat16)
    total = jnp.concatenate([total, jnp.zeros((112, D), jnp.bfloat16)])
    small = dot_nt(arrange[...], total).astype(jnp.bfloat16)
    left_kept[:, D:] = small[:half]
    left_sent[:, D:] = small[half:]
    value = dot(hidden_t[...], grads[:, D:]) + dot(other_hidden_t[...], other_grads[:, D:])
    output = dot(context_t[...], residual[...]) + dot(other_context_t[...], other_residual[...])
    grad = jnp.concatenate([value, output], axis=1).astype(jnp.bfloat16)
    part_rows(grad, left_kept, left_sent, right_kept, right_sent, False)


def attention_gradient(*operands):
    left, right = ((D // 2, D + 128), bf16, "V"), ((D // 2, D), bf16, "V")
    places = ["H"] + ["V"] * 2 + ["H"] * 4 + ["V"] * 4
    return run(
        attention_gradient_kernel,
        "attention_gradient",
        list(zip(operands, places)),
        [left, left, right, right],
        2.5e9,
    )


def input_kernel(place, residual_grad, kept, sent, restore, l0, l1, l2, l3, r0, r1, r2, r3, input_grad):
    left, right = (l0, l1, l2, l3), (r0, r1, r2, r3)
    half = D // 2
    parts = []
    for at in range(3):
        columns = slice(at * half, (at + 1) * half)
        parts.append(both_halves(place[0], kept[:, columns], sent[:, columns]))
    query_grad, key_grad, value_grad = parts
    total = dot_nt(query_grad, left_tile(left, slice(0, D)))
    total += dot_nt(key_grad[:, :512], left_tile(left, slice(D, FIRST_HALF)))
    total += dot_nt(key_grad[:, 512:], right_tile(right, slice(256, 512)))
    total += dot_nt(value_grad, right_tile(right, slice(512, FIRST_HALF)))
    total = residual_grad[...] + whole_precision(total, restore[...])
    input_grad[...] = total.astype(jnp.bfloat16)


def input_back(place, residual_grad, kept, sent, restore, pieces):
    return run(
        input_kernel,
        "input_back",
        [(place, "S"), (residual_grad, "H")]
        + placed_at("V", kept, sent)
        + placed_at("H", restore, *in_order(pieces)),
        [(residual_grad.shape, bf16, "H")],
        3e9,
    )[0]


def add_kernel(left, left_in, right, right_in, left_kept, left_sent, right_kept, right_sent):
    for own, received, kept, sent in (
        (left, left_in, left_kept, left_sent),
        (right, right_in, right_kept, right_sent),
    ):
        total = (own[...].astype(jnp.float32) + received[...].astype(jnp.float32)).astype(jnp.bfloat16)
        half = total.shape[0] // 2
        kept[...] = total[:half]
        sent[...] = total[half:]


def add_parts(left, left_in, right, right_in):
    shapes = [(part.shape[0] // 2,) + part.shape[1:] for part in (left, left, right, right)]
    return pl.pallas_call(
        add_kernel,
        in_specs=[VMEM] * 4,
        out_specs=[VMEM] * 4,
        out_shape=[jax.ShapeDtypeStruct(shape, jnp.bfloat16) for shape in shapes],
        compiler_params=params(),
        cost_estimate=cost(1, 1),
        name="add_parts",
    )(left, left_in, right, right_in)


def add_z_kernel(left, left_in, right, right_in, own, first, second, third):
    width = left.shape[-1]
    for part, received, columns in (
        (left, left_in, slice(0, width)),
        (right, right_in, slice(width, width + right.shape[-1])),
    ):
        rows = part.shape[0] // 4
        total = part[...].astype(jnp.float32) + received[...].astype(jnp.float32)
        own[..., columns] = total[:rows]
        for at, sent in enumerate((first, second, third)):
            sent[..., columns] = total[(at + 1) * rows : (at + 2) * rows].astype(jnp.bfloat16)


def add_z(left, left_in, right, right_in):
    shape = (left.shape[0] // 4,) + left.shape[1:-1] + (left.shape[-1] + right.shape[-1],)
    return pl.pallas_call(
        add_z_kernel,
        in_specs=[VMEM] * 4,
        out_specs=[VMEM] * 4,
        out_shape=[jax.ShapeDtypeStruct(shape, jnp.float32)]
        + [jax.ShapeDtypeStruct(shape, jnp.bfloat16)] * 3,
        compiler_params=params(),
        cost_estimate=cost(1, 1),
        name="add_z",
    )(left, left_in, right, right_in)


def finish_kernel(place, own, first, second, third, mine, other):
    total = own[...]
    for received in (first, second, third):
        total = total + received[...].astype(jnp.float32)
    if len(total.shape) == 3:
        low, high = total[0], total[1]
    else:
        low, high = total[:ROW], total[ROW:]
    mine[...] = pick(place[0], low, high)
    other[...] = pick(place[0], high, low)


def finish(place, own, received):
    rows = own.shape[1] if own.ndim == 3 else ROW
    return pl.pallas_call(
        finish_kernel,
        in_specs=[SMEM] + [VMEM] * 4,
        out_specs=[VMEM] * 2,
        out_shape=[jax.ShapeDtypeStruct((rows, own.shape[-1]), jnp.float32)] * 2,
        compiler_params=params(),
        cost_estimate=cost(1, 1),
        name="finish",
    )(place, own, *received)


def put(place, out, mine, received):
    half = mine.shape[1]
    out[:, :half] = pick(place[0], mine, received)
    out[:, half:] = pick(place[0], received, mine)


def outer_out_kernel(place, mine, received, out):
    rows, half = mine.shape[0], mine.shape[1] // 2
    for at in range(2):
        columns = slice(at * half, (at + 1) * half)
        put(place, out.at[at * rows : (at + 1) * rows], mine[:, columns], received[:, columns])


def inner_out_kernel(place, mine, received, out):
    put(place, out, mine[...], received[...])


def rest_out_kernel(place, mine, received, query, key, value, output, inner_bias, *vectors):
    half = D // 2
    for out, at in ((query, 0), (key, half), (value, D + 128), (output, D + 128 + half)):
        columns = slice(at, at + half)
        put(place, out, mine[:, columns], received[:, columns])
    turned = jnp.transpose(mine[:, D : D + 128])
    for at, out in enumerate(vectors):
        out[...] = turned[at : at + 1]
    for at in range(4):
        inner_bias[:, at * ROW : (at + 1) * ROW] = turned[8 + at : 9 + at]


def placed(kernel, name, place, mine, received, shapes):
    return pl.pallas_call(
        kernel,
        in_specs=[SMEM, VMEM, VMEM],
        out_specs=[VMEM] * len(shapes),
        out_shape=[jax.ShapeDtypeStruct(shape, jnp.float32) for shape in shapes],
        compiler_params=params(),
        cost_estimate=cost(1, 1),
        name=name,
    )(place, mine, received)


def first_transfers(pieces):
    return [mate(pieces[1]), across(pieces[3], 2)]


def add_first(pieces, received):
    return add_parts(pieces[0], received[0], pieces[2], received[1])


def second_transfers(pieces):
    return [across(pieces[1], 2), mate(pieces[3])]


def add_second(pieces, received):
    return add_z(pieces[0], received[0], pieces[2], received[1])


def third_transfers(parts):
    return [across(sent, mask) for sent, mask in zip(parts[1:], (4, 8, 12))]


def fast_device(
    hidden_in,
    cotangent,
    span_lengths,
    partner_span,
    query_weight,
    query_bias,
    key_weight,
    value_weight,
    value_bias,
    output_weight,
    output_bias,
    first_gain,
    first_shift,
    inner_weight,
    inner_bias,
    outer_weight,
    outer_bias,
    second_gain,
    second_shift,
):
    core, x_at, z_at, y_at = coordinates()
    place = jnp.stack([core, y_at, x_at, z_at]).astype(jnp.int32)
    restore, arrange = permutations()
    first_block, second_block = pack(
        query_weight,
        key_weight,
        value_weight,
        output_weight,
        inner_weight,
        inner_bias,
        (
            query_bias,
            value_bias,
            output_bias,
            first_gain,
            first_shift,
            outer_bias,
            second_gain,
            second_shift,
        ),
    )
    ff = inner_weight.shape[1]
    first_z = z_exchange(first_block)
    first = stack_z(first_block, first_z, FIRST_HALF)
    first_in = near_exchange(first)
    second_z = z_exchange(after(second_block, *first))
    first = stack_near(first, first_in)
    first_far = far_exchange(first)
    first_core = core_exchange(first)
    second = stack_z(after(second_block, *first_far), second_z, SECOND_HALF)
    second_in = near_exchange(second)
    third_z = z_exchange(after(outer_weight, *second))
    first_far_core = core_exchange(tied(first_far, *second))
    second = stack_near(second, second_in)
    second_far = far_exchange(second)
    second_core = core_exchange(second)
    first_pieces = pieces_of(first, first_far, first_core, tied(first_far_core, *second))
    left_rows, right_rows, vectors, attention, context_arrived, hidden_t, context_t = front(
        span_lengths, hidden_in, restore, arrange, first_pieces
    )
    third = stack_z(after(outer_weight, vectors, *second_far), third_z, D // 2)
    third_in = near_exchange(third)
    second_far_core = core_exchange(tied(second_far, *third))
    third = stack_near(third, third_in)
    third_far = far_exchange(third)
    third_core = core_exchange(third)
    second_pieces = pieces_of(second, second_far, second_core, tied(second_far_core, *third))
    active, active_t, slope, first_normed, first_factor, first_t = middle(
        hidden_in, context_arrived, restore, arrange, vectors, ff, second_pieces
    )
    third_far_core = core_exchange(tied(third_far, first_factor))
    third_pieces = pieces_of(third, third_far, third_core, third_far_core)
    layer_out, second_normed, second_factor, cls_rows, outer_mat = last(
        place, active, first_normed, vectors, third_pieces
    )
    other_rows = mate(cls_rows)
    hidden_t, context_t, first_t, active_t = tied((hidden_t, context_t, first_t, active_t), cls_rows)
    other_hidden_t, other_context_t = across(hidden_t, 1), across(context_t, 1)
    other_first_t, other_active_t = across(first_t, 1), across(active_t, 1)
    second_grad, second_kept, second_sent, second_sums, span_loss = turn(
        place, partner_span, cotangent, second_normed, second_factor, vectors, cls_rows, other_rows
    )
    second_received = across(second_sent, 1)
    preact_kept, preact_sent, inner_sums = slope_back(
        place, second_kept, second_sent, outer_mat, slope
    )
    preact_received = across(preact_sent, 1)
    outer_parts = outer_gradient(
        place, active_t, other_active_t, after(second_kept, preact_kept), second_received
    )
    outer_in = first_transfers(outer_parts)
    residual_grad, residual_kept, residual_sent, context_grad, first_sums = first_back(
        place,
        after(preact_kept, outer_parts[0]),
        preact_sent,
        second_grad,
        first_normed,
        first_factor,
        vectors,
        restore,
        second_pieces,
    )
    outer_parts = add_first(outer_parts, tied(outer_in, context_grad))
    outer_in = second_transfers(outer_parts)
    residual_received = across(after(residual_sent, outer_parts[0]), 1)
    inner_parts = inner_gradient(
        first_t, other_first_t, after(preact_kept, outer_parts[0]), preact_received
    )
    outer_parts = add_second(outer_parts, tied(outer_in, inner_parts[0]))
    outer_in = third_transfers(outer_parts)
    inner_in = first_transfers(tied(inner_parts, outer_parts[0]))
    grads_kept, grads_sent, sums = attend_back(
        place,
        after(context_grad, inner_parts[0], outer_parts[0]),
        left_rows,
        right_rows,
        attention,
        first_sums,
        second_sums,
        inner_sums,
    )
    inner_parts = add_first(inner_parts, tied(inner_in, sums))
    inner_in = second_transfers(inner_parts)
    grads_received = across(after(grads_sent, inner_parts[0]), 1)
    other_sums = across(after(sums, inner_parts[0]), 1)
    outer_mine, outer_other = finish(place, outer_parts[0], tied(outer_in, inner_parts[0]))
    outer_other = across(outer_other, 1)
    rest_parts = attention_gradient(
        arrange,
        sums,
        other_sums,
        hidden_t,
        other_hidden_t,
        context_t,
        other_context_t,
        after(grads_kept, outer_mine),
        grads_received,
        residual_kept,
        residual_received,
    )
    inner_parts = add_second(inner_parts, tied(inner_in, rest_parts[0]))
    rest_in = first_transfers(tied(rest_parts, inner_parts[0]))
    inner_in = third_transfers(inner_parts)
    input_grad = input_back(
        place,
        residual_grad,
        after(grads_kept, rest_parts[0], inner_parts[0]),
        grads_sent,
        restore,
        first_pieces,
    )
    rest_parts = add_first(rest_parts, tied(rest_in, input_grad))
    rest_in = second_transfers(rest_parts)
    inner_mine, inner_other = finish(place, inner_parts[0], tied(inner_in, rest_parts[0]))
    inner_other = across(inner_other, 1)
    (outer_grad,) = placed(
        outer_out_kernel, "outer_out", place, outer_mine, after(outer_other, inner_mine), [(4 * ROW, D)]
    )
    rest_parts = add_second(rest_parts, tied(rest_in, outer_grad))
    rest_in = third_transfers(rest_parts)
    (inner_grad,) = placed(
        inner_out_kernel, "inner_out", place, inner_mine, after(inner_other, rest_parts[0]), [(ROW, ff)]
    )
    rest_mine, rest_other = finish(place, rest_parts[0], tied(rest_in, inner_grad))
    rest_other = across(rest_other, 1)
    query_grad, key_grad, value_grad, output_grad, inner_bias_grad, *vector_grads = placed(
        rest_out_kernel,
        "rest_out",
        place,
        rest_mine,
        rest_other,
        [(ROW, D)] * 4 + [(1, 4 * ROW)] + [(1, ROW)] * 8,
    )
    vector_grads = [grad.reshape(-1) for grad in vector_grads]
    return (
        layer_out,
        input_grad,
        span_loss.reshape(-1),
        query_grad,
        vector_grads[0],
        key_grad,
        value_grad,
        vector_grads[1],
        output_grad,
        vector_grads[2],
        vector_grads[3],
        vector_grads[4],
        inner_grad,
        inner_bias_grad.reshape(-1),
        outer_grad,
        vector_grads[5],
        vector_grads[6],
        vector_grads[7],
    )


def solution(mesh):
    is_block = mesh.shape["doc"] == 2 * PLACES and mesh.shape["pair"] == 2
    return jax.shard_map(
        fast_device if is_block else per_device,
        mesh=mesh,
        in_specs=(
            P(("doc", "pair"), None),
            P(("doc", "pair"), None),
            P(("doc", "pair")),
            P("doc", None),
            P(("doc", "pair"), None),
            P(("doc", "pair")),
            P(("doc", "pair"), None),
            P(("doc", "pair"), None),
            P(("doc", "pair")),
            P(("doc", "pair"), None),
            P(("doc", "pair")),
            P(("doc", "pair")),
            P(("doc", "pair")),
            P(("doc", "pair"), None),
            P(("doc", "pair")),
            P(("doc", "pair"), None),
            P(("doc", "pair")),
            P(("doc", "pair")),
            P(("doc", "pair")),
        ),
        out_specs=(
            P(("doc", "pair"), None),
            P(("doc", "pair"), None),
            P(("doc", "pair")),
            P(("doc", "pair"), None),
            P(("doc", "pair")),
            P(("doc", "pair"), None),
            P(("doc", "pair"), None),
            P(("doc", "pair")),
            P(("doc", "pair"), None),
            P(("doc", "pair")),
            P(("doc", "pair")),
            P(("doc", "pair")),
            P(("doc", "pair"), None),
            P(("doc", "pair")),
            P(("doc", "pair"), None),
            P(("doc", "pair")),
            P(("doc", "pair")),
            P(("doc", "pair")),
        ),
        check_vma=False,
    )
```

profile of v0, /device:TPU:0, one launch (start us, length us, event | category | flops | bytes accessed | tf_op | source)
XLA Modules:
  0.0 265.2 jit_solution(18391737812153842490)
XLA Ops:
  0.7 1.9 pack.1
  2.6 5.1 %collective-permute-start.2 = (bf16[24,2560]{1,0:T(8,128)(2,1)}, bf16[24,2560]{1,0:T(8,128)(2,1)S(1)}, u32[]{:S(2)}, u32[]{:S(2)}) collective-permute-start(bf16[24,2560]{1,0:T(8,128)(2,1)} %get-tuple-element.175.first), channel_id=1, source_target_pairs={{0,24},{2,26},{4,28},{6,30},{8,16},{10,18},{12,20},{14,22},{16,8},... | collective-permute-start | bytes 368648 | tf_op jit(solution)/shard_map/ppermute | solution.py:24
  8.4 3.8 %collective-permute-done.2.fourth = bf16[24,2560]{1,0:T(8,128)(2,1)S(1)} collective-permute-done((bf16[24,2560]{1,0:T(8,128)(2,1)}, bf16[24,2560]{1,0:T(8,128)(2,1)S(1)}, u32[]{:S(2)}, u32[]{:S(2)}) %collective-permute-start.2) | collective-permute-done | bytes 122912 | tf_op jit(solution)/shard_map/ppermute | solution.py:24
  12.2 6.1 %collective-permute-done.1.third = bf16[24,2560]{1,0:T(8,128)(2,1)S(1)} collective-permute-done((bf16[24,2560]{1,0:T(8,128)(2,1)}, bf16[24,2560]{1,0:T(8,128)(2,1)S(1)}, u32[]{:S(2)}, u32[]{:S(2)}) %collective-permute-start.1) | collective-permute-done | bytes 122912 | tf_op jit(solution)/shard_map/ppermute | solution.py:24
  19.3 1.6 collective-permute-start.3
  20.8 1.5 collective-permute-start.4
  22.3 4.0 %collective-permute-done.3.left_in = bf16[96,1280]{1,0:T(8,128)(2,1)S(1)} collective-permute-done((bf16[96,1280]{1,0:T(8,128)(2,1)S(1)}, bf16[96,1280]{1,0:T(8,128)(2,1)S(1)}, u32[]{:S(2)}, u32[]{:S(2)}) %collective-permute-start.3) | collective-permute-done | bytes 245792 | tf_op jit(solution)/shard_map/ppermute | solution.py:24
  28.4 1.5 collective-permute-start.5
  30.4 2.3 collective-permute-start.10
  32.7 2.1 collective-permute-start.8
  34.8 4.7 %collective-permute-done.5.refs_5_.refs_6_ = bf16[192,1280]{1,0:T(8,128)(2,1)} collective-permute-done((bf16[192,1280]{1,0:T(8,128)(2,1)S(1)}, bf16[192,1280]{1,0:T(8,128)(2,1)}, u32[]{:S(2)}, u32[]{:S(2)}) %collective-permute-start.5) | collective-permute-done | bytes 491552 | tf_op jit(solution)/shard_map/ppermute | solution.py:28
  41.0 5.3 %collective-permute-done.9.third = bf16[24,3840]{1,0:T(8,128)(2,1)S(1)} collective-permute-done((bf16[24,3840]{1,0:T(8,128)(2,1)}, bf16[24,3840]{1,0:T(8,128)(2,1)S(1)}, u32[]{:S(2)}, u32[]{:S(2)}) %collective-permute-start.9) | collective-permute-done | bytes 184352 | tf_op jit(solution)/shard_map/ppermute | solution.py:24
  48.4 9.0 %collective-permute-done.13.left_in = bf16[96,1792]{1,0:T(8,128)(2,1)S(1)} collective-permute-done((bf16[96,1792]{1,0:T(8,128)(2,1)S(1)}, bf16[96,1792]{1,0:T(8,128)(2,1)S(1)}, u32[]{:S(2)}, u32[]{:S(2)}) %collective-permute-start.13) | collective-permute-done | bytes 344096 | tf_op jit(solution)/shard_map/ppermute | solution.py:24
  57.5 1.5 collective-permute-start.18
  60.3 1.5 collective-permute-start.16
  62.3 2.2 collective-permute-start.21
  64.5 2.3 collective-permute-start.19
  67.1 13.3 %front.1 = (bf16[512,1280]{1,0:T(8,128)(2,1)S(1)}, bf16[512,1280]{1,0:T(8,128)(2,1)S(1)}, f32[16,768]{1,0:T(8,128)S(1)}, bf16[512,1536]{1,0:T(8,128)(2,1)S(1)}, ...) custom-call(s32[4]{0:T(128)S(1)} %copy-done.17, ...), custom_call_target="tpu_custom_call" | custom-call | flops 1 | bytes 1 | tf_op jit(solution)/shard_map/front/pallas_call | solution.py:630
  84.2 7.8 %collective-permute-done.24.left_in = bf16[384,384]{1,0:T(8,128)(2,1)S(1)} collective-permute-done((bf16[384,384]{1,0:T(8,128)(2,1)S(1)}, bf16[384,384]{1,0:T(8,128)(2,1)S(1)}, u32[]{:S(2)}, u32[]{:S(2)}) %collective-permute-start.24) | collective-permute-done | bytes 294944 | tf_op jit(solution)/shard_map/ppermute | solution.py:24
  95.0 16.2 %middle.1 = (bf16[512,3072]{1,0:T(8,128)(2,1)S(1)}, bf16[3072,512]{1,0:T(8,128)(2,1)S(1)}, bf16[512,3072]{1,0:T(8,128)(2,1)S(1)}, f32[512,768]{1,0:T(8,128)S(1)}...) custom-call(bf16[512,768]{1,0:T(8,128)(2,1)S(1)} %copy-done, bf16[512,768]{1,0:T(8,128)(2,1)S(1)} %get-tuple-element.191.refs_1_, ...), custom_call_target="tpu_custom_call" | custom-call | flops 1 | bytes 1 | tf_op jit(solution)/shard_map/middle/pallas_call | solution.py:630
  114.1 6.3 %last.1 = (bf16[512,768]{1,0:T(8,128)(2,1)}, f32[512,768]{1,0:T(8,128)S(1)}, f32[512,1]{1,0:T(8,128)S(1)}, bf16[4,768]{1,0:T(4,128)(2,1)S(1)}, bf16[3072,768]{1,0:T(8,128)(2,1)S(1)}) custom-call(s32[4]{0:T(128)S(1)} %pad_add_fusion.refs_0_.place, bf16[512,3072]{1,0:T(8,128)(2,1)S(1)} %get-tuple-element.203.refs_1_, ...), custom_call_target="tpu_custom_call" | custom-call | flops 1 | bytes 1 | tf_op jit(solution)/shard_map/last/pallas_call | solution.py:630
  120.6 1.5 collective-permute-start.33
  122.2 2.1 collective-permute-done.33.refs_7_
  124.3 2.8 %turn.1 = (f32[512,768]{1,0:T(8,128)S(1)}, bf16[512,384]{1,0:T(8,128)(2,1)S(1)}, bf16[512,384]{1,0:T(8,128)(2,1)S(1)}, f32[3,768]{1,0:T(4,128)S(1)}, f32[1,4]{1,0:T(1,128)}) custom-call(s32[4]{0:T(128)S(1)} %pad_add_fusion.refs_0_.place, s32[1,4]{1,0:T(1,128)S(1)} %copy-done.18, bf16[512,768]{1,0:T(8,128)(2,1)S(1)} %copy-done.9, ...), custom_call_target="tpu_custom_call" | custom-call | flops 1 | bytes 1 | tf_op jit(solution)/shard_map/turn/pallas_call | solution.py:630
  127.1 5.7 %slope_back.1 = (bf16[512,1536]{1,0:T(8,128)(2,1)S(1)}, bf16[512,1536]{1,0:T(8,128)(2,1)S(1)}, f32[1,3072]{1,0:T(1,128)S(1)}) custom-call(s32[4]{0:T(128)S(1)} %pad_add_fusion.refs_0_.place, bf16[512,384]{1,0:T(8,128)(2,1)S(1)} %get-tuple-element.222.refs_1_.refs_3_, bf16[512,384]{1,0:T(8,128)(2,1)S(1)} %get-tuple-element.213.refs_2_, ...), custom_call_target="tpu_custom_call" | custom-call | flops 1 | bytes 1 | tf_op jit(solution)/shard_map/slope_back/pallas_call | solution.py:630
  133.3 3.5 %collective-permute-done.35.refs_4_ = bf16[512,384]{1,0:T(8,128)(2,1)S(1)} collective-permute-done((bf16[512,384]{1,0:T(8,128)(2,1)S(1)}, bf16[512,384]{1,0:T(8,128)(2,1)S(1)}, u32[]{:S(2)}, u32[]{:S(2)}) %collective-permute-start.35) | collective-permute-done | bytes 393248 | tf_op jit(solution)/shard_map/ppermute | solution.py:24
  136.8 6.4 %outer_gradient.1 = (bf16[16,48,384]{2,1,0:T(8,128)(2,1)S(1)}, bf16[16,48,384]{2,1,0:T(8,128)(2,1)S(1)}, bf16[16,48,384]{2,1,0:T(8,128)(2,1)S(1)}, bf16[16,48,384]{2,1,0:T(8,128)(2,1)S(1)}) custom-call(s32[4]{0:T(128)S(1)} %pad_add_fusion.refs_0_.place, bf16[3072,512]{1,0:T(8,128)(2,1)S(1)} %get-tuple-element.221.refs_1_, ...), custom_call_target="tpu_custom_call" | custom-call | flops 1 | bytes 1 | tf_op jit(solution)/shard_map/outer_gradient/pallas_call | solution.py:630
  143.1 1.6 collective-permute-start.37
  145.3 11.5 %first_back.1 = (f32[512,768]{1,0:T(8,128)S(1)}, bf16[512,384]{1,0:T(8,128)(2,1)S(1)}, bf16[512,384]{1,0:T(8,128)(2,1)S(1)}, bf16[512,768]{1,0:T(8,128)(2,1)S(1)}, f32[3,768]{1,0:T(4,128)S(1)}) custom-call(s32[4]{0:T(128)S(1)} %pad_add_fusion.refs_0_.place, bf16[512,1536]{1,0:T(8,128)(2,1)S(1)} %get-tuple-element.236.refs_1_.refs_2_, ...), custom_call_target="tpu_custom_call" | custom-call | flops 1 | bytes 1 | tf_op jit(solution)/shard_map/first_back/pallas_call | solution.py:630
  156.8 1.8 collective-permute-done.37.left_in
  161.3 2.9 %inner_gradient.1 = (bf16[384,768]{1,0:T(8,128)(2,1)S(1)}, bf16[384,768]{1,0:T(8,128)(2,1)S(1)}, bf16[384,768]{1,0:T(8,128)(2,1)S(1)}, bf16[384,768]{1,0:T(8,128)(2,1)S(1)}) custom-call(bf16[768,512]{1,0:T(8,128)(2,1)S(1)} %get-tuple-element.229.refs_0_, bf16[768,512]{1,0:T(8,128)(2,1)S(1)} %collective-permute-done.36.refs_1_, ...), custom_call_target="tpu_custom_call" | custom-call | flops 1 | bytes 1 | tf_op jit(solution)/shard_map/inner_gradient/pallas_call | solution.py:630
  164.2 3.9 %collective-permute-done.40.left_in = bf16[8,48,384]{2,1,0:T(8,128)(2,1)S(1)} collective-permute-done((bf16[8,48,384]{2,1,0:T(8,128)(2,1)S(1)}, bf16[8,48,384]{2,1,0:T(8,128)(2,1)S(1)}, u32[]{:S(2)}, u32[]{:S(2)}) %collective-permute-start.40) | collective-permute-done | bytes 294944 | tf_op jit(solution)/shard_map/ppermute | solution.py:24
  169.2 1.5 collective-permute-start.43
  170.6 10.1 %attend_back.1 = (bf16[512,1152]{1,0:T(8,128)(2,1)S(1)}, bf16[512,1152]{1,0:T(8,128)(2,1)S(1)}, f32[16,768]{1,0:T(8,128)S(1)}) custom-call(s32[4]{0:T(128)S(1)} %pad_add_fusion.refs_0_.place, bf16[512,768]{1,0:T(8,128)(2,1)S(1)} %get-tuple-element.244.refs_1_, bf16[512,1280]{1,0:T(8,128)(2,1)S(1)} %copy-done.6, bf16[512,1280]{1,0:T(8,128)(2,1)S(1)} %copy-done.8, ...), custom_call_target="tpu_custom_call" | custom-call | flops 1 | bytes 1 | tf_op jit(solution)/shard_map/attend_back/pallas_call | solution.py:630
  183.4 2.9 %collective-permute-done.45.refs_4_ = bf16[768,512]{1,0:T(8,128)(2,1)S(1)} collective-permute-done((bf16[768,512]{1,0:T(8,128)(2,1)S(1)}, bf16[768,512]{1,0:T(8,128)(2,1)S(1)}, u32[]{:S(2)}, u32[]{:S(2)}) %collective-permute-start.45) | collective-permute-done | bytes 786464 | tf_op jit(solution)/shard_map/ppermute | solution.py:24
  190.5 5.3 %collective-permute-done.48.second = bf16[2,48,768]{2,1,0:T(8,128)(2,1)S(1)} collective-permute-done((bf16[2,48,768]{2,1,0:T(8,128)(2,1)S(1)}, bf16[2,48,768]{2,1,0:T(8,128)(2,1)S(1)}, u32[]{:S(2)}, u32[]{:S(2)}) %collective-permute-start.48) | collective-permute-done | bytes 147488 | tf_op jit(solution)/shard_map/ppermute | solution.py:24
  195.8 2.0 collective-permute-start.49
  197.8 5.6 %collective-permute-done.49.third = bf16[2,48,768]{2,1,0:T(8,128)(2,1)S(1)} collective-permute-done((bf16[2,48,768]{2,1,0:T(8,128)(2,1)S(1)}, bf16[2,48,768]{2,1,0:T(8,128)(2,1)S(1)}, u32[]{:S(2)}, u32[]{:S(2)}) %collective-permute-start.49) | collective-permute-done | bytes 147488 | tf_op jit(solution)/shard_map/ppermute | solution.py:24
  204.6 5.0 %attention_gradient.1 = (bf16[384,896]{1,0:T(8,128)(2,1)S(1)}, bf16[384,896]{1,0:T(8,128)(2,1)S(1)}, bf16[384,768]{1,0:T(8,128)(2,1)S(1)}, bf16[384,768]{1,0:T(8,128)(2,1)S(1)}) custom-call(bf16[768,768]{1,0:T(8,128)(2,1)S(1)} %fusion.1.refs_3_.refs_0_, f32[16,768]{1,0:T(8,128)S(1)} %get-tuple-element.261.refs_1_, ...), custom_call_target="tpu_custom_call" | custom-call | flops 1 | bytes 1 | tf_op jit(solution)/shard_map/attention_gradient/pallas_call | solution.py:630
  212.7 9.8 %input_back.1 = bf16[512,768]{1,0:T(8,128)(2,1)} custom-call(s32[4]{0:T(128)S(1)} %pad_add_fusion.refs_0_.place, f32[512,768]{1,0:T(8,128)S(1)} %get-tuple-element.227.refs_1_, bf16[512,1152]{1,0:T(8,128)(2,1)S(1)} %get-tuple-element.284.refs_7_.refs_2_, bf16[512,1152]{1,0:T(8,128)(2,1)S(1)} %get-tuple-element.273.refs_3_, ...), custom_call_target="tpu_custom_call" | custom-call | flops 1 | bytes 1 | tf_op jit(solution)/shard_map/input_back/pallas_call | solution.py:630
  222.4 3.9 %collective-permute-done.55.right_in = bf16[384,768]{1,0:T(8,128)(2,1)S(1)} collective-permute-done((bf16[384,768]{1,0:T(8,128)(2,1)S(1)}, bf16[384,768]{1,0:T(8,128)(2,1)S(1)}, u32[]{:S(2)}, u32[]{:S(2)}) %collective-permute-start.55) | collective-permute-done | bytes 589856 | tf_op jit(solution)/shard_map/ppermute | solution.py:24
  227.6 1.5 collective-permute-start.56
  230.5 2.6 collective-permute-start.60
  233.1 1.8 collective-permute-start.61
  235.9 8.0 %collective-permute-done.60.second = bf16[48,1536]{1,0:T(8,128)(2,1)S(1)} collective-permute-done((bf16[48,1536]{1,0:T(8,128)(2,1)S(1)}, bf16[48,1536]{1,0:T(8,128)(2,1)S(1)}, u32[]{:S(2)}, u32[]{:S(2)}) %collective-permute-start.60) | collective-permute-done | bytes 147488 | tf_op jit(solution)/shard_map/ppermute | solution.py:24
  246.0 2.2 collective-permute-start.62
  248.8 1.8 collective-permute-start.64
  253.3 8.3 %collective-permute-done.63.second = bf16[48,1664]{1,0:T(8,128)(2,1)S(1)} collective-permute-done((bf16[48,1664]{1,0:T(8,128)(2,1)S(1)}, bf16[48,1664]{1,0:T(8,128)(2,1)S(1)}, u32[]{:S(2)}, u32[]{:S(2)}) %collective-permute-start.63) | collective-permute-done | bytes 159776 | tf_op jit(solution)/shard_map/ppermute | solution.py:24
  (158 shorter events, 47.9 us)
Async XLA Ops:
  2.6 9.6 %collective-permute-start.2 = (bf16[24,2560]{1,0:T(8,128)(2,1)}, bf16[24,2560]{1,0:T(8,128)(2,1)S(1)}, u32[]{:S(2)}, u32[]{:S(2)}) collective-permute-start(bf16[24,2560]{1,0:T(8,128)(2,1)} %get-tuple-element.175.first), channel_id=1, source_target_pairs={{0,24},{2,26},{4,28},{6,30},{8,16},{10,18},{12,20},{14,22},{16,8},... | collective-permute-start | bytes 368648 | tf_op jit(solution)/shard_map/ppermute | solution.py:24
  7.7 10.6 %collective-permute-start.1 = (bf16[24,2560]{1,0:T(8,128)(2,1)}, bf16[24,2560]{1,0:T(8,128)(2,1)S(1)}, u32[]{:S(2)}, u32[]{:S(2)}) collective-permute-start(bf16[24,2560]{1,0:T(8,128)(2,1)} %get-tuple-element.175.first), channel_id=1, source_target_pairs={{0,16},{2,18},{4,20},{6,22},{8,24},{10,26},{12,28},{14,30},{16,0},... | collective-permute-start | bytes 368648 | tf_op jit(solution)/shard_map/ppermute | solution.py:24
  7.7 10.6 %collective-permute-start = (bf16[24,2560]{1,0:T(8,128)(2,1)}, bf16[24,2560]{1,0:T(8,128)(2,1)S(1)}, u32[]{:S(2)}, u32[]{:S(2)}) collective-permute-start(bf16[24,2560]{1,0:T(8,128)(2,1)} %get-tuple-element.175.first), channel_id=1, source_target_pairs={{0,8},{2,10},{4,12},{6,14},{8,0},{10,2},{12,4},{14,6},{16,24},{18,... | collective-permute-start | bytes 368648 | tf_op jit(solution)/shard_map/ppermute | solution.py:24
  28.4 11.2 %collective-permute-start.5 = (bf16[192,1280]{1,0:T(8,128)(2,1)S(1)}, bf16[192,1280]{1,0:T(8,128)(2,1)}, u32[]{:S(2)}, u32[]{:S(2)}) collective-permute-start(bf16[192,1280]{1,0:T(8,128)(2,1)S(1)} %get-tuple-element.178.refs_4_.refs_5_), channel_id=1, source_target_pairs={{0,1},{1,0},{2,3},{3,2},{4,5},{5,4},{6,7},{7,6},{8,9},{9,8},{10,11... | collective-permute-start | bytes 1474568 | tf_op jit(solution)/shard_map/ppermute | solution.py:28
  29.9 11.1 %collective-permute-start.7 = (bf16[192,1280]{1,0:T(8,128)(2,1)}, bf16[192,1280]{1,0:T(8,128)(2,1)}, u32[]{:S(2)}, u32[]{:S(2)}) collective-permute-start(bf16[192,1280]{1,0:T(8,128)(2,1)} %get-tuple-element.179.refs_8_.refs_9_), channel_id=1, source_target_pairs={{0,4},{2,6},{4,0},{6,2},{8,12},{10,14},{12,8},{14,10},{16,20},{18,... | collective-permute-start | bytes 1474568 | tf_op jit(solution)/shard_map/ppermute | solution.py:24
  30.4 10.6 %collective-permute-start.10 = (bf16[24,3840]{1,0:T(8,128)(2,1)}, bf16[24,3840]{1,0:T(8,128)(2,1)S(1)}, u32[]{:S(2)}, u32[]{:S(2)}) collective-permute-start(bf16[24,3840]{1,0:T(8,128)(2,1)} %get-tuple-element.182.first), channel_id=1, source_target_pairs={{0,24},{2,26},{4,28},{6,30},{8,16},{10,18},{12,20},{14,22},{16,8},... | collective-permute-start | bytes 552968 | tf_op jit(solution)/shard_map/ppermute | solution.py:24
  32.7 13.6 %collective-permute-start.9 = (bf16[24,3840]{1,0:T(8,128)(2,1)}, bf16[24,3840]{1,0:T(8,128)(2,1)S(1)}, u32[]{:S(2)}, u32[]{:S(2)}) collective-permute-start(bf16[24,3840]{1,0:T(8,128)(2,1)} %get-tuple-element.182.first), channel_id=1, source_target_pairs={{0,16},{2,18},{4,20},{6,22},{8,24},{10,26},{12,28},{14,30},{16,0},... | collective-permute-start | bytes 552968 | tf_op jit(solution)/shard_map/ppermute | solution.py:24
  32.7 13.6 %collective-permute-start.8 = (bf16[24,3840]{1,0:T(8,128)(2,1)}, bf16[24,3840]{1,0:T(8,128)(2,1)S(1)}, u32[]{:S(2)}, u32[]{:S(2)}) collective-permute-start(bf16[24,3840]{1,0:T(8,128)(2,1)} %get-tuple-element.182.first), channel_id=1, source_target_pairs={{0,8},{2,10},{4,12},{6,14},{8,0},{10,2},{12,4},{14,6},{16,24},{18,... | collective-permute-start | bytes 552968 | tf_op jit(solution)/shard_map/ppermute | solution.py:24
  46.4 11.1 %collective-permute-start.14 = (bf16[96,2048]{1,0:T(8,128)(2,1)S(1)}, bf16[96,2048]{1,0:T(8,128)(2,1)S(1)}, u32[]{:S(2)}, u32[]{:S(2)}) collective-permute-start(bf16[96,2048]{1,0:T(8,128)(2,1)S(1)} %get-tuple-element.184.right), channel_id=1, source_target_pairs={{0,1},{1,0},{2,3},{3,2},{4,5},{5,4},{6,7},{7,6},{8,9},{9,8},{10,11... | collective-permute-start | bytes 1179656 | tf_op jit(solution)/shard_map/ppermute | solution.py:28
  46.9 12.6 %collective-permute-start.6 = (bf16[192,1280]{1,0:T(8,128)(2,1)S(1)}, bf16[192,1280]{1,0:T(8,128)(2,1)S(1)}, u32[]{:S(2)}, u32[]{:S(2)}) collective-permute-start(bf16[192,1280]{1,0:T(8,128)(2,1)S(1)} %get-tuple-element.178.refs_4_.refs_5_), channel_id=1, source_target_pairs={{0,2},{2,0},{4,6},{6,4},{8,10},{10,8},{12,14},{14,12},{16,18},{18,... | collective-permute-start | bytes 1474568 | tf_op jit(solution)/shard_map/ppermute | solution.py:24
  46.9 10.5 %collective-permute-start.13 = (bf16[96,1792]{1,0:T(8,128)(2,1)S(1)}, bf16[96,1792]{1,0:T(8,128)(2,1)S(1)}, u32[]{:S(2)}, u32[]{:S(2)}) collective-permute-start(bf16[96,1792]{1,0:T(8,128)(2,1)S(1)} %get-tuple-element.183.left), channel_id=1, source_target_pairs={{0,4},{2,6},{4,0},{6,2},{8,12},{10,14},{12,8},{14,10},{16,20},{18,... | collective-permute-start | bytes 1032200 | tf_op jit(solution)/shard_map/ppermute | solution.py:24
  57.5 24.9 %collective-permute-start.18 = (bf16[192,2048]{1,0:T(8,128)(2,1)S(1)}, bf16[192,2048]{1,0:T(8,128)(2,1)S(1)}, u32[]{:S(2)}, u32[]{:S(2)}) collective-permute-start(bf16[192,2048]{1,0:T(8,128)(2,1)S(1)} %get-tuple-element.188.refs_9_.refs_12_), channel_id=1, source_target_pairs={{0,4},{2,6},{4,0},{6,2},{8,12},{10,14},{12,8},{14,10},{16,20},{18,... | collective-permute-start | bytes 2359304 | tf_op jit(solution)/shard_map/ppermute | solution.py:24
  60.3 22.0 %collective-permute-start.16 = (bf16[192,1792]{1,0:T(8,128)(2,1)S(1)}, bf16[192,1792]{1,0:T(8,128)(2,1)}, u32[]{:S(2)}, u32[]{:S(2)}) collective-permute-start(bf16[192,1792]{1,0:T(8,128)(2,1)S(1)} %get-tuple-element.187.refs_5_.refs_8_), channel_id=1, source_target_pairs={{0,1},{1,0},{2,3},{3,2},{4,5},{5,4},{6,7},{7,6},{8,9},{9,8},{10,11... | collective-permute-start | bytes 2064392 | tf_op jit(solution)/shard_map/ppermute | solution.py:28
  62.3 20.1 %collective-permute-start.21 = (bf16[96,768]{1,0:T(8,128)(2,1)}, bf16[96,768]{1,0:T(8,128)(2,1)S(1)}, u32[]{:S(2)}, u32[]{:S(2)}) collective-permute-start(bf16[96,768]{1,0:T(8,128)(2,1)} %first), channel_id=1, source_target_pairs={{0,24},{2,26},{4,28},{6,30},{8,16},{10,18},{12,20},{14,22},{16,8},... | collective-permute-start | bytes 442376 | tf_op jit(solution)/shard_map/ppermute | solution.py:24
  64.5 17.9 %collective-permute-start.20 = (bf16[96,768]{1,0:T(8,128)(2,1)}, bf16[96,768]{1,0:T(8,128)(2,1)S(1)}, u32[]{:S(2)}, u32[]{:S(2)}) collective-permute-start(bf16[96,768]{1,0:T(8,128)(2,1)} %first), channel_id=1, source_target_pairs={{0,16},{2,18},{4,20},{6,22},{8,24},{10,26},{12,28},{14,30},{16,0},... | collective-permute-start | bytes 442376 | tf_op jit(solution)/shard_map/ppermute | solution.py:24
  64.5 17.9 %collective-permute-start.19 = (bf16[96,768]{1,0:T(8,128)(2,1)}, bf16[96,768]{1,0:T(8,128)(2,1)S(1)}, u32[]{:S(2)}, u32[]{:S(2)}) collective-permute-start(bf16[96,768]{1,0:T(8,128)(2,1)} %first), channel_id=1, source_target_pairs={{0,8},{2,10},{4,12},{6,14},{8,0},{10,2},{12,4},{14,6},{16,24},{18,... | collective-permute-start | bytes 442376 | tf_op jit(solution)/shard_map/ppermute | solution.py:24
  82.5 10.5 %collective-permute-start.22 = (bf16[192,1792]{1,0:T(8,128)(2,1)}, bf16[192,1792]{1,0:T(8,128)(2,1)S(1)}, u32[]{:S(2)}, u32[]{:S(2)}) collective-permute-start(bf16[192,1792]{1,0:T(8,128)(2,1)} %collective-permute-done.16.refs_6_.refs_9_), channel_id=1, source_target_pairs={{0,2},{2,0},{4,6},{6,4},{8,10},{10,8},{12,14},{14,12},{16,18},{18,... | collective-permute-start | bytes 2064392 | tf_op jit(solution)/shard_map/ppermute | solution.py:24
  82.6 9.4 %collective-permute-start.24 = (bf16[384,384]{1,0:T(8,128)(2,1)S(1)}, bf16[384,384]{1,0:T(8,128)(2,1)S(1)}, u32[]{:S(2)}, u32[]{:S(2)}) collective-permute-start(bf16[384,384]{1,0:T(8,128)(2,1)S(1)} %get-tuple-element.195.left), channel_id=1, source_target_pairs={{0,4},{2,6},{4,0},{6,2},{8,12},{10,14},{12,8},{14,10},{16,20},{18,... | collective-permute-start | bytes 884744 | tf_op jit(solution)/shard_map/ppermute | solution.py:24
  83.2 9.1 %collective-permute-start.25 = (bf16[384,384]{1,0:T(8,128)(2,1)S(1)}, bf16[384,384]{1,0:T(8,128)(2,1)S(1)}, u32[]{:S(2)}, u32[]{:S(2)}) collective-permute-start(bf16[384,384]{1,0:T(8,128)(2,1)S(1)} %get-tuple-element.196.right), channel_id=1, source_target_pairs={{0,1},{1,0},{2,3},{3,2},{4,5},{5,4},{6,7},{7,6},{8,9},{9,8},{10,11... | collective-permute-start | bytes 884744 | tf_op jit(solution)/shard_map/ppermute | solution.py:28
  83.7 10.7 %collective-permute-start.23 = (bf16[192,2048]{1,0:T(8,128)(2,1)S(1)}, bf16[192,2048]{1,0:T(8,128)(2,1)S(1)}, u32[]{:S(2)}, u32[]{:S(2)}) collective-permute-start(bf16[192,2048]{1,0:T(8,128)(2,1)S(1)} %collective-permute-done.18.refs_10_.refs_13_), channel_id=1, source_target_pairs={{0,2},{2,0},{4,6},{6,4},{8,10},{10,8},{12,14},{14,12},{16,18},{18,... | collective-permute-start | bytes 2359304 | tf_op jit(solution)/shard_map/ppermute | solution.py:24
  83.7 11.2 %collective-permute-start.26 = (bf16[192,2048]{1,0:T(8,128)(2,1)S(1)}, bf16[192,2048]{1,0:T(8,128)(2,1)S(1)}, u32[]{:S(2)}, u32[]{:S(2)}) collective-permute-start(bf16[192,2048]{1,0:T(8,128)(2,1)S(1)} %get-tuple-element.188.refs_9_.refs_12_), channel_id=1, source_target_pairs={{0,2},{2,0},{4,6},{6,4},{8,10},{10,8},{12,14},{14,12},{16,18},{18,... | collective-permute-start | bytes 2359304 | tf_op jit(solution)/shard_map/ppermute | solution.py:24
  92.4 18.8 %collective-permute-start.27 = (bf16[768,384]{1,0:T(8,128)(2,1)S(1)}, bf16[768,384]{1,0:T(8,128)(2,1)S(1)}, u32[]{:S(2)}, u32[]{:S(2)}) collective-permute-start(bf16[768,384]{1,0:T(8,128)(2,1)S(1)} %get-tuple-element.199.refs_4_), channel_id=1, source_target_pairs={{0,1},{1,0},{2,3},{3,2},{4,5},{5,4},{6,7},{7,6},{8,9},{9,8},{10,11... | collective-permute-start | bytes 1769480 | tf_op jit(solution)/shard_map/ppermute | solution.py:28
  93.0 18.2 %collective-permute-start.29 = (bf16[768,384]{1,0:T(8,128)(2,1)S(1)}, bf16[768,384]{1,0:T(8,128)(2,1)S(1)}, u32[]{:S(2)}, u32[]{:S(2)}) collective-permute-start(bf16[768,384]{1,0:T(8,128)(2,1)S(1)} %get-tuple-element.200.refs_8_), channel_id=1, source_target_pairs={{0,4},{2,6},{4,0},{6,2},{8,12},{10,14},{12,8},{14,10},{16,20},{18,... | collective-permute-start | bytes 1769480 | tf_op jit(solution)/shard_map/ppermute | solution.py:24
  94.4 17.4 %collective-permute-start.28 = (bf16[768,384]{1,0:T(8,128)(2,1)S(1)}, bf16[768,384]{1,0:T(8,128)(2,1)S(1)}, u32[]{:S(2)}, u32[]{:S(2)}) collective-permute-start(bf16[768,384]{1,0:T(8,128)(2,1)S(1)} %get-tuple-element.199.refs_4_), channel_id=1, source_target_pairs={{0,2},{2,0},{4,6},{6,4},{8,10},{10,8},{12,14},{14,12},{16,18},{18,... | collective-permute-start | bytes 1769480 | tf_op jit(solution)/shard_map/ppermute | solution.py:24
  94.4 17.4 %collective-permute-start.31 = (bf16[768,384]{1,0:T(8,128)(2,1)S(1)}, bf16[768,384]{1,0:T(8,128)(2,1)S(1)}, u32[]{:S(2)}, u32[]{:S(2)}) collective-permute-start(bf16[768,384]{1,0:T(8,128)(2,1)S(1)} %get-tuple-element.200.refs_8_), channel_id=1, source_target_pairs={{0,2},{2,0},{4,6},{6,4},{8,10},{10,8},{12,14},{14,12},{16,18},{18,... | collective-permute-start | bytes 1769480 | tf_op jit(solution)/shard_map/ppermute | solution.py:24
  120.4 16.3 %collective-permute-start.34 = (bf16[3072,512]{1,0:T(8,128)(2,1)S(1)}, bf16[3072,512]{1,0:T(8,128)(2,1)S(1)}, u32[]{:S(2)}, u32[]{:S(2)}) collective-permute-start(bf16[3072,512]{1,0:T(8,128)(2,1)S(1)} %get-tuple-element.221.refs_1_), channel_id=1, source_target_pairs={{0,2},{2,0},{4,6},{6,4},{8,10},{10,8},{12,14},{14,12},{16,18},{18,... | collective-permute-start | bytes 9437192 | tf_op jit(solution)/shard_map/ppermute | solution.py:24
  132.7 28.5 %collective-permute-start.39 = (bf16[512,1536]{1,0:T(8,128)(2,1)S(1)}, bf16[512,1536]{1,0:T(8,128)(2,1)S(1)}, u32[]{:S(2)}, u32[]{:S(2)}) collective-permute-start(bf16[512,1536]{1,0:T(8,128)(2,1)S(1)} %get-tuple-element.225.refs_2_), channel_id=1, source_target_pairs={{0,2},{2,0},{4,6},{6,4},{8,10},{10,8},{12,14},{14,12},{16,18},{18,... | collective-permute-start | bytes 4718600 | tf_op jit(solution)/shard_map/ppermute | solution.py:24
  143.1 15.4 %collective-permute-start.37 = (bf16[16,48,384]{2,1,0:T(8,128)(2,1)S(1)}, bf16[16,48,384]{2,1,0:T(8,128)(2,1)S(1)}, u32[]{:S(2)}, u32[]{:S(2)}) collective-permute-start(bf16[16,48,384]{2,1,0:T(8,128)(2,1)S(1)} %get-tuple-element.230), channel_id=1, source_target_pairs={{0,1},{1,0},{2,3},{3,2},{4,5},{5,4},{6,7},{7,6},{8,9},{9,8},{10,11... | collective-permute-start | bytes 1769480 | tf_op jit(solution)/shard_map/ppermute | solution.py:28
  144.7 15.1 %collective-permute-start.38 = (bf16[16,48,384]{2,1,0:T(8,128)(2,1)S(1)}, bf16[16,48,384]{2,1,0:T(8,128)(2,1)S(1)}, u32[]{:S(2)}, u32[]{:S(2)}) collective-permute-start(bf16[16,48,384]{2,1,0:T(8,128)(2,1)S(1)} %get-tuple-element.231), channel_id=1, source_target_pairs={{0,4},{2,6},{4,0},{6,2},{8,12},{10,14},{12,8},{14,10},{16,20},{18,... | collective-permute-start | bytes 1769480 | tf_op jit(solution)/shard_map/ppermute | solution.py:24
  145.3 16.0 %collective-permute-start.36 = (bf16[768,512]{1,0:T(8,128)(2,1)S(1)}, bf16[768,512]{1,0:T(8,128)(2,1)S(1)}, u32[]{:S(2)}, u32[]{:S(2)}) collective-permute-start(bf16[768,512]{1,0:T(8,128)(2,1)S(1)} %get-tuple-element.229.refs_0_), channel_id=1, source_target_pairs={{0,2},{2,0},{4,6},{6,4},{8,10},{10,8},{12,14},{14,12},{16,18},{18,... | collective-permute-start | bytes 2359304 | tf_op jit(solution)/shard_map/ppermute | solution.py:24
  160.1 8.0 %collective-permute-start.40 = (bf16[8,48,384]{2,1,0:T(8,128)(2,1)S(1)}, bf16[8,48,384]{2,1,0:T(8,128)(2,1)S(1)}, u32[]{:S(2)}, u32[]{:S(2)}) collective-permute-start(bf16[8,48,384]{2,1,0:T(8,128)(2,1)S(1)} %get-tuple-element.238), channel_id=1, source_target_pairs={{0,4},{2,6},{4,0},{6,2},{8,12},{10,14},{12,8},{14,10},{16,20},{18,... | collective-permute-start | bytes 884744 | tf_op jit(solution)/shard_map/ppermute | solution.py:24
  160.7 7.6 %collective-permute-start.41 = (bf16[8,48,384]{2,1,0:T(8,128)(2,1)S(1)}, bf16[8,48,384]{2,1,0:T(8,128)(2,1)S(1)}, u32[]{:S(2)}, u32[]{:S(2)}) collective-permute-start(bf16[8,48,384]{2,1,0:T(8,128)(2,1)S(1)} %get-tuple-element.239), channel_id=1, source_target_pairs={{0,1},{1,0},{2,3},{3,2},{4,5},{5,4},{6,7},{7,6},{8,9},{9,8},{10,11... | collective-permute-start | bytes 884744 | tf_op jit(solution)/shard_map/ppermute | solution.py:28
  168.5 13.1 %collective-permute-start.42 = (bf16[384,768]{1,0:T(8,128)(2,1)S(1)}, bf16[384,768]{1,0:T(8,128)(2,1)S(1)}, u32[]{:S(2)}, u32[]{:S(2)}) collective-permute-start(bf16[384,768]{1,0:T(8,128)(2,1)S(1)} %get-tuple-element.256), channel_id=1, source_target_pairs={{0,1},{1,0},{2,3},{3,2},{4,5},{5,4},{6,7},{7,6},{8,9},{9,8},{10,11... | collective-permute-start | bytes 1769480 | tf_op jit(solution)/shard_map/ppermute | solution.py:28
  169.2 12.8 %collective-permute-start.43 = (bf16[384,768]{1,0:T(8,128)(2,1)S(1)}, bf16[384,768]{1,0:T(8,128)(2,1)S(1)}, u32[]{:S(2)}, u32[]{:S(2)}) collective-permute-start(bf16[384,768]{1,0:T(8,128)(2,1)S(1)} %get-tuple-element.257), channel_id=1, source_target_pairs={{0,4},{2,6},{4,0},{6,2},{8,12},{10,14},{12,8},{14,10},{16,20},{18,... | collective-permute-start | bytes 1769480 | tf_op jit(solution)/shard_map/ppermute | solution.py:24
  182.3 22.3 %collective-permute-start.50 = (bf16[512,1152]{1,0:T(8,128)(2,1)S(1)}, bf16[512,1152]{1,0:T(8,128)(2,1)S(1)}, u32[]{:S(2)}, u32[]{:S(2)}) collective-permute-start(bf16[512,1152]{1,0:T(8,128)(2,1)S(1)} %get-tuple-element.273.refs_3_), channel_id=1, source_target_pairs={{0,2},{2,0},{4,6},{6,4},{8,10},{10,8},{12,14},{14,12},{16,18},{18,... | collective-permute-start | bytes 3538952 | tf_op jit(solution)/shard_map/ppermute | solution.py:24
  182.9 21.1 %collective-permute-start.51 = (bf16[512,384]{1,0:T(8,128)(2,1)S(1)}, bf16[512,384]{1,0:T(8,128)(2,1)S(1)}, u32[]{:S(2)}, u32[]{:S(2)}) collective-permute-start(bf16[512,384]{1,0:T(8,128)(2,1)S(1)} %get-tuple-element.276), channel_id=1, source_target_pairs={{0,2},{2,0},{4,6},{6,4},{8,10},{10,8},{12,14},{14,12},{16,18},{18,... | collective-permute-start | bytes 1179656 | tf_op jit(solution)/shard_map/ppermute | solution.py:24
  186.3 9.5 %collective-permute-start.48 = (bf16[2,48,768]{2,1,0:T(8,128)(2,1)S(1)}, bf16[2,48,768]{2,1,0:T(8,128)(2,1)S(1)}, u32[]{:S(2)}, u32[]{:S(2)}) collective-permute-start(bf16[2,48,768]{2,1,0:T(8,128)(2,1)S(1)} %get-tuple-element.265), channel_id=1, source_target_pairs={{0,16},{2,18},{4,20},{6,22},{8,24},{10,26},{12,28},{14,30},{16,0},... | collective-permute-start | bytes 442376 | tf_op jit(solution)/shard_map/ppermute | solution.py:24
  187.4 22.2 %collective-permute-start.52 = (bf16[192,768]{1,0:T(8,128)(2,1)S(1)}, bf16[192,768]{1,0:T(8,128)(2,1)S(1)}, u32[]{:S(2)}, u32[]{:S(2)}) collective-permute-start(bf16[192,768]{1,0:T(8,128)(2,1)S(1)} %get-tuple-element.278), channel_id=1, source_target_pairs={{0,4},{2,6},{4,0},{6,2},{8,12},{10,14},{12,8},{14,10},{16,20},{18,... | collective-permute-start | bytes 884744 | tf_op jit(solution)/shard_map/ppermute | solution.py:24
  189.1 20.5 %collective-permute-start.53 = (bf16[192,768]{1,0:T(8,128)(2,1)S(1)}, bf16[192,768]{1,0:T(8,128)(2,1)S(1)}, u32[]{:S(2)}, u32[]{:S(2)}) collective-permute-start(bf16[192,768]{1,0:T(8,128)(2,1)S(1)} %get-tuple-element.279), channel_id=1, source_target_pairs={{0,1},{1,0},{2,3},{3,2},{4,5},{5,4},{6,7},{7,6},{8,9},{9,8},{10,11... | collective-permute-start | bytes 884744 | tf_op jit(solution)/shard_map/ppermute | solution.py:28
  209.8 17.6 %collective-permute-start.54 = (bf16[384,896]{1,0:T(8,128)(2,1)S(1)}, bf16[384,896]{1,0:T(8,128)(2,1)S(1)}, u32[]{:S(2)}, u32[]{:S(2)}) collective-permute-start(bf16[384,896]{1,0:T(8,128)(2,1)S(1)} %get-tuple-element.289), channel_id=1, source_target_pairs={{0,1},{1,0},{2,3},{3,2},{4,5},{5,4},{6,7},{7,6},{8,9},{9,8},{10,11... | collective-permute-start | bytes 2064392 | tf_op jit(solution)/shard_map/ppermute | solution.py:28
  211.2 15.1 %collective-permute-start.55 = (bf16[384,768]{1,0:T(8,128)(2,1)S(1)}, bf16[384,768]{1,0:T(8,128)(2,1)S(1)}, u32[]{:S(2)}, u32[]{:S(2)}) collective-permute-start(bf16[384,768]{1,0:T(8,128)(2,1)S(1)} %get-tuple-element.290), channel_id=1, source_target_pairs={{0,4},{2,6},{4,0},{6,2},{8,12},{10,14},{12,8},{14,10},{16,20},{18,... | collective-permute-start | bytes 1769480 | tf_op jit(solution)/shard_map/ppermute | solution.py:24
  227.6 18.2 %collective-permute-start.56 = (bf16[192,896]{1,0:T(8,128)(2,1)S(1)}, bf16[192,896]{1,0:T(8,128)(2,1)S(1)}, u32[]{:S(2)}, u32[]{:S(2)}) collective-permute-start(bf16[192,896]{1,0:T(8,128)(2,1)S(1)} %get-tuple-element.294), channel_id=1, source_target_pairs={{0,4},{2,6},{4,0},{6,2},{8,12},{10,14},{12,8},{14,10},{16,20},{18,... | collective-permute-start | bytes 1032200 | tf_op jit(solution)/shard_map/ppermute | solution.py:24
  229.2 16.6 %collective-permute-start.57 = (bf16[192,768]{1,0:T(8,128)(2,1)S(1)}, bf16[192,768]{1,0:T(8,128)(2,1)S(1)}, u32[]{:S(2)}, u32[]{:S(2)}) collective-permute-start(bf16[192,768]{1,0:T(8,128)(2,1)S(1)} %get-tuple-element.295), channel_id=1, source_target_pairs={{0,1},{1,0},{2,3},{3,2},{4,5},{5,4},{6,7},{7,6},{8,9},{9,8},{10,11... | collective-permute-start | bytes 884744 | tf_op jit(solution)/shard_map/ppermute | solution.py:28
  230.5 13.4 %collective-permute-start.60 = (bf16[48,1536]{1,0:T(8,128)(2,1)S(1)}, bf16[48,1536]{1,0:T(8,128)(2,1)S(1)}, u32[]{:S(2)}, u32[]{:S(2)}) collective-permute-start(bf16[48,1536]{1,0:T(8,128)(2,1)S(1)} %get-tuple-element.298), channel_id=1, source_target_pairs={{0,16},{2,18},{4,20},{6,22},{8,24},{10,26},{12,28},{14,30},{16,0},... | collective-permute-start | bytes 442376 | tf_op jit(solution)/shard_map/ppermute | solution.py:24
  233.1 10.8 %collective-permute-start.61 = (bf16[48,1536]{1,0:T(8,128)(2,1)S(1)}, bf16[48,1536]{1,0:T(8,128)(2,1)S(1)}, u32[]{:S(2)}, u32[]{:S(2)}) collective-permute-start(bf16[48,1536]{1,0:T(8,128)(2,1)S(1)} %get-tuple-element.299), channel_id=1, source_target_pairs={{0,24},{2,26},{4,28},{6,30},{8,16},{10,18},{12,20},{14,22},{16,8},... | collective-permute-start | bytes 442376 | tf_op jit(solution)/shard_map/ppermute | solution.py:24
  235.9 8.6 %collective-permute-start.58 = (f32[48,768]{1,0:T(8,128)S(1)}, f32[48,768]{1,0:T(8,128)S(1)}, u32[]{:S(2)}, u32[]{:S(2)}) collective-permute-start(f32[48,768]{1,0:T(8,128)S(1)} %get-tuple-element.296), channel_id=1, source_target_pairs={{0,2},{2,0},{4,6},{6,4},{8,10},{10,8},{12,14},{14,12},{16,18},{18,... | collective-permute-start | bytes 442376 | tf_op jit(solution)/shard_map/ppermute | solution.py:24
  248.2 13.4 %collective-permute-start.63 = (bf16[48,1664]{1,0:T(8,128)(2,1)S(1)}, bf16[48,1664]{1,0:T(8,128)(2,1)S(1)}, u32[]{:S(2)}, u32[]{:S(2)}) collective-permute-start(bf16[48,1664]{1,0:T(8,128)(2,1)S(1)} %get-tuple-element.310), channel_id=1, source_target_pairs={{0,16},{2,18},{4,20},{6,22},{8,24},{10,26},{12,28},{14,30},{16,0},... | collective-permute-start | bytes 479240 | tf_op jit(solution)/shard_map/ppermute | solution.py:24
  248.8 12.8 %collective-permute-start.64 = (bf16[48,1664]{1,0:T(8,128)(2,1)S(1)}, bf16[48,1664]{1,0:T(8,128)(2,1)S(1)}, u32[]{:S(2)}, u32[]{:S(2)}) collective-permute-start(bf16[48,1664]{1,0:T(8,128)(2,1)S(1)} %get-tuple-element.311), channel_id=1, source_target_pairs={{0,24},{2,26},{4,28},{6,30},{8,16},{10,18},{12,20},{14,22},{16,8},... | collective-permute-start | bytes 479240 | tf_op jit(solution)/shard_map/ppermute | solution.py:24
  (38 other events, 313.1 us)
where the time goes:
time: 268 us; the launch traced here: 265 us
  Pallas kernels  100 us (37%)
  waiting for transfers between devices  100 us (37%)
  starting transfers between devices  59.2 us (22%)
  local copies, waits for them, and re-layouts  3.68 us (1%)
    pallas_call x12, Pallas kernels, run(): pl.pallas_call(body, in_specs=[spaces[place] for place in in_places], out...  91.9 us
    ppermute x54, waiting for transfers between devices, across(): return lax.ppermute(block, 'doc', [(at, at ^ mask) for at in range(count)])  87.8 us
    ppermute x54, starting transfers between devices, across(): return lax.ppermute(block, 'doc', [(at, at ^ mask) for at in range(count)])  44.6 us
    ppermute x13, starting transfers between devices, mate(): return lax.ppermute(block, 'pair', [(0, 1), (1, 0)])  14.6 us
    ppermute x13, waiting for transfers between devices, mate(): return lax.ppermute(block, 'pair', [(0, 1), (1, 0)])  12.2 us
  transfers between devices with their start and end apart: 67, of which 33 were waited for; matrix products, arithmetic and copies ran while one was open for 0% of the time, Pallas kernels for 33%

commit v1 on v0

--- a/solution.py
+++ b/solution.py
@@ -495,25 +495,35 @@
     return (doc & 1, (doc >> 1) & 1, doc >> 2, lax.axis_index("pair"))
 
 
-def permutations():
-    core, x_at, z_at, y_at = coordinates()
-    row = jnp.arange(D, dtype=jnp.int32)
-    block, inside = row // ROW, row % ROW
-    y_off, x_off = (block & 1) ^ y_at, ((block >> 2) & 1) ^ x_at
-    block_core, z_off = (block >> 1) & 1, (block >> 3) ^ z_at
-    arrived = ((((block_core ^ core) * 2 + y_off) * 2 + x_off) * 4 + z_off) * ROW + inside
-    leaving = ((y_off * 2 + x_off) * 4 + z_off) * 2 * ROW + block_core * ROW + inside
-    restore = (arrived[:, None] == row[None, :]).astype(jnp.bfloat16)
-    arrange = (leaving[None, :] == row[:, None]).astype(jnp.bfloat16)
-    return (restore, arrange)
+def blocks_of(row):
+    block = (row * 2731) >> 16
+    return (block >> 1) & 1, block & 1, (block >> 2) & 1, block >> 3, row - block * ROW
+
+
+def restore_from(place):
+    row = lax.broadcasted_iota(jnp.int32, (D, 1), 0)
+    core, y_at, x_at, z_at, inside = blocks_of(row)
+    offset = ((core ^ place[0]) * 2 + (y_at ^ place[1])) * 2 + (x_at ^ place[2])
+    arrived = (offset * 4 + (z_at ^ place[3])) * ROW + inside
+    hit = arrived == lax.broadcasted_iota(jnp.int32, (D, D), 1)
+    return jnp.where(hit, 1.0, 0.0).astype(jnp.bfloat16)
+
+
+def arrange_from(place):
+    row = lax.broadcasted_iota(jnp.int32, (1, D), 1)
+    core, y_at, x_at, z_at, inside = blocks_of(row)
+    offset = ((y_at ^ place[1]) * 2 + (x_at ^ place[2])) * 4 + (z_at ^ place[3])
+    leaving = offset * 2 * ROW + core * ROW + inside
+    hit = leaving == lax.broadcasted_iota(jnp.int32, (D, D), 0)
+    return jnp.where(hit, 1.0, 0.0).astype(jnp.bfloat16)
 
 
 def after(value, *others):
     return lax.optimization_barrier((value,) + others)[0]
 
 
-def z_exchange(block):
-    return [across(block, mask) for mask in (4, 8, 12)]
+def z_exchange(block, masks=(4, 8, 12)):
+    return [across(block, mask) for mask in masks]
 
 
 def tied(values, *others):
@@ -533,11 +543,11 @@
 
 
 def core_exchange(block):
-    return across(block[0], 1), across(block[1], 1)
+    return [across(part, 1) for part in block]
 
 
 def pieces_of(near, far, core, far_core):
-    return [near[0], far[0], near[1], far[1], core[0], far_core[0], core[1], far_core[1]]
+    return [near[0], far[0], near[1], far[1], core, far_core[0], far_core[1]]
 
 
 VMEM = pl.BlockSpec(memory_space=pltpu.VMEM)
@@ -585,9 +595,10 @@
 PARTS = 8
 
 
-def run(kernel, name, operands, results, flops, scratch=(), mib=12):
+def run(kernel, name, operands, results, flops, scratch=(), mib=12, total=None):
     in_hbm = pl.BlockSpec(memory_space=pltpu.HBM)
     spaces = {"S": SMEM, "V": VMEM, "H": in_hbm, "A": in_hbm}
+    spaces["K"] = VMEM
     in_places = [place for _, place in operands]
     out_places = [place for _, _, place in results]
     staged = [pltpu.VMEM(array.shape, array.dtype) for array, place in operands if place == "H"]
@@ -626,7 +637,7 @@
     size = lambda shape, dtype: math.prod(shape) * jnp.dtype(dtype).itemsize
     inside = sum(size(array.shape, array.dtype) for array, place in operands if place == "H")
     inside += sum(size(shape, dtype) for shape, dtype, place in results if place == "H")
-    mib = mib + inside // 2**20
+    mib = (mib + inside // 2**20) if total is None else total
     return pl.pallas_call(
         body,
         in_specs=[spaces[place] for place in in_places],
@@ -699,22 +710,64 @@
         [((ROW, 2 * FIRST_HALF), bf16, "V"), ((ROW, D + inner.shape[1]), bf16, "V")],
         1e6,
         [pltpu.VMEM((128, 128), f32)],
-        mib=58,
-    )
-
-
-def stack_z_kernel(split, first, second, third, fourth, left, right):
-    blocks = [ref[...].astype(jnp.float32) for ref in (first, second, third, fourth)]
+        total=58,
+    )
+
+
+def stack_two_kernel(first, second, left, right):
+    blocks = [first[...].astype(jnp.float32), second[...].astype(jnp.float32)]
     whole = jnp.concatenate(blocks).astype(jnp.bfloat16)
+    left[...] = whole[:, : left.shape[1]]
+    right[...] = whole[:, left.shape[1] :]
+
+
+def stack_two(block, received, split):
+    rows, columns = block.shape
+    return pl.pallas_call(
+        stack_two_kernel,
+        in_specs=[VMEM] * 2,
+        out_specs=[VMEM] * 2,
+        out_shape=[
+            jax.ShapeDtypeStruct((2 * rows, split), jnp.bfloat16),
+            jax.ShapeDtypeStruct((2 * rows, columns - split), jnp.bfloat16),
+        ],
+        compiler_params=params(),
+        cost_estimate=cost(1, 1),
+        name="stack_two",
+    )(block, received)
+
+
+def stack_z_two_kernel(first, second, out):
+    blocks = [first[...].astype(jnp.float32), second[...].astype(jnp.float32)]
+    out[...] = jnp.concatenate(blocks).astype(jnp.bfloat16)
+
+
+def stack_z_two(block, received):
+    rows, columns = block.shape
+    return pl.pallas_call(
+        stack_z_two_kernel,
+        in_specs=[VMEM] * 2,
+        out_specs=VMEM,
+        out_shape=jax.ShapeDtypeStruct((2 * rows, columns), jnp.bfloat16),
+        compiler_params=params(),
+        cost_estimate=cost(1, 1),
+        name="stack_z_two",
+    )(block, received)
+
+
+def stack_z_kernel(split, *refs):
+    blocks, (left, right) = refs[:-2], refs[-2:]
+    whole = jnp.concatenate([ref[...].astype(jnp.float32) for ref in blocks]).astype(jnp.bfloat16)
     left[...] = whole[:, :split]
     right[...] = whole[:, split:]
 
 
 def stack_z(block, received, split):
     rows, columns = block.shape
+    rows = rows * (1 + len(received)) // 4
     return pl.pallas_call(
         partial(stack_z_kernel, split),
-        in_specs=[VMEM] * 4,
+        in_specs=[VMEM] * (1 + len(received)),
         out_specs=[VMEM] * 2,
         out_shape=[
             jax.ShapeDtypeStruct((4 * rows, split), jnp.bfloat16),
@@ -726,20 +779,27 @@
     )(block, *received)
 
 
-def stack_pair_kernel(left, left_in, right, right_in, left_out, right_out):
-    for own, received, out in ((left, left_in, left_out), (right, right_in, right_out)):
+def stack_pair_kernel(left, left_in, right, right_in, left_out, right_out, both_out):
+    width = left.shape[1]
+    for own, received, out, columns in (
+        (left, left_in, left_out, slice(0, width)),
+        (right, right_in, right_out, slice(width, width + right.shape[1])),
+    ):
         rows = own.shape[0]
         out[:rows, :] = own[...]
         out[rows:, :] = received[...]
+        both_out[:rows, columns] = own[...]
+        both_out[rows:, columns] = received[...]
 
 
 def stack_pair(left, left_in, right, right_in):
     double = lambda block: jax.ShapeDtypeStruct((2 * block.shape[0], block.shape[1]), block.dtype)
+    both = jax.ShapeDtypeStruct((2 * left.shape[0], left.shape[1] + right.shape[1]), left.dtype)
     return pl.pallas_call(
         stack_pair_kernel,
         in_specs=[VMEM] * 4,
-        out_specs=[VMEM] * 2,
-        out_shape=[double(left), double(right)],
+        out_specs=[VMEM] * 3,
+        out_shape=[double(left), double(right), both],
         compiler_params=params(),
         cost_estimate=cost(1, 1),
         name="stack_pair",
@@ -759,8 +819,47 @@
 
 
 def in_order(pieces):
-    left, left_far, right, right_far, c_left, c_left_far, c_right, c_right_far = pieces
-    return (left, left_far, c_left, c_left_far, right, right_far, c_right, c_right_far)
+    left, left_far, right, right_far, c_both, c_left_far, c_right_far = pieces
+    return (left, left_far, c_left_far, c_both, right, right_far, c_right_far)
+
+
+class Side:
+    def __init__(self, ref, start, width):
+        self.ref, self.start, self.shape = ref, start, (ref.shape[0], width)
+
+    def __getitem__(self, at):
+        rows, columns = at
+        return self.ref[rows, columns.start + self.start : columns.stop + self.start]
+
+
+def sides(l0, l1, l3, both, r0, r1, r3):
+    left, right = l0.shape[1], r0.shape[1]
+    return (l0, l1, Side(both, 0, left), l3), (r0, r1, Side(both, left, right), r3)
+
+
+FIRST_PARTS = ((0, 0, 768), (0, 768, 512), (1, 256, 256), (1, 512, 768))
+SECOND_PARTS = ((0, 0, 768), (0, 768, 512), (0, 1280, 512)) + tuple((1, at, 512) for at in range(0, 2048, 512))
+
+
+def settle(sides_of, parts, mats, semaphore):
+    copies = []
+    for (side, start, width), mat in zip(parts, mats):
+        for at, piece in enumerate(sides_of[side]):
+            rows = piece.shape[0]
+            source, first = (piece.ref, piece.start) if isinstance(piece, Side) else (piece, 0)
+            columns = pl.ds(first + start, width)
+            if side == 0:
+                copies.append((source.at[:, columns], mat.at[pl.ds(at * rows, rows), :]))
+                continue
+            half = rows // 2
+            core, far = at // 2, at % 2
+            for near in range(2):
+                to = ((core * 2 + near) * 2 + far) * half
+                copies.append((source.at[pl.ds(near * half, half), columns], mat.at[pl.ds(to, half), :]))
+    copies = [pltpu.make_async_copy(*ends, semaphore.at[at]) for at, ends in enumerate(copies)]
+    for copy in copies:
+        copy.start()
+    return copies
 
 
 FIRST_HALF = 1280
@@ -776,47 +875,79 @@
     return right_rows[rows, at - 256 : at - 128]
 
 
-def front_kernel(
-    lengths,
+def project_kernel(
+    place,
     hidden,
-    restore,
-    arrange,
+    both,
+    r0,
+    r1,
+    r3,
     l0,
     l1,
-    l2,
     l3,
-    r0,
-    r1,
-    r2,
-    r3,
     left_rows,
     right_rows,
     vectors,
-    attention_out,
-    context_arrived,
     hidden_t,
-    context_t,
-    context,
+    query_mat,
+    low_key_mat,
+    high_key_mat,
+    value_mat,
+    settling,
 ):
     tokens = hidden.shape[0]
-    hidden_t[...] = dot_nt(arrange[...], hidden[...]).astype(jnp.bfloat16)
-    moved = dot(hidden[...], restore[...]).astype(jnp.bfloat16)
-    small = dot(restore[...], right_tile((r0, r1, r2, r3), slice(0, 128)))
+    lefts, rights = sides(l0, l1, l3, both, r0, r1, r3)
+    mats = (query_mat, low_key_mat, high_key_mat, value_mat)
+    copies = settle((lefts, rights), FIRST_PARTS, mats, settling)
+    restore = restore_from(place)
+    moved = dot(hidden[...], restore).astype(jnp.bfloat16)
+    small = dot(restore, right_tile(rights, slice(0, 128)))
     turned = jnp.transpose(small)[:16]
     vectors[...] = turned
     for at in range(0, FIRST_HALF, 256):
         columns = slice(at, at + 256)
-        rows = dot(moved, left_tile((l0, l1, l2, l3), columns))
+        rows = dot(moved, left_tile(lefts, columns))
         if at < D:
             rows += turned[0:1, columns]
         left_rows[:, columns] = rows.astype(jnp.bfloat16)
         if at == 0:
             right_rows[:, columns] = jnp.zeros((tokens, 256), jnp.bfloat16)
             continue
-        rows = dot(moved, right_tile((r0, r1, r2, r3), columns))
+        rows = dot(moved, right_tile(rights, columns))
         if at >= 512:
             rows += turned[1:2, at - 512 : at - 256]
         right_rows[:, columns] = rows.astype(jnp.bfloat16)
+    left_rows.done()
+    right_rows.done()
+    hidden_t[...] = dot_nt(arrange_from(place), hidden[...]).astype(jnp.bfloat16)
+    for copy in copies:
+        copy.wait()
+
+
+def project(place, hidden, pieces):
+    tokens, ordered = hidden.shape[0], in_order(pieces)
+    return run(
+        project_kernel,
+        "project",
+        [(place, "S"), (hidden, "H")] + placed_at("K", *ordered[3:], *ordered[:3]),
+        [
+            ((tokens, FIRST_HALF), bf16, "H"),
+            ((tokens, FIRST_HALF), bf16, "H"),
+            ((16, D), f32, "V"),
+            ((D, tokens), bf16, "H"),
+        ]
+        + [((D, width), bf16, "A") for _, _, width in FIRST_PARTS],
+        9e9,
+        [pltpu.SemaphoreType.DMA((24,))],
+        total=50,
+    )
+
+
+def attention_kernel(
+    place, lengths, left_rows, right_rows, attention_out, context_arrived, context_t, context
+):
+    tokens = context.shape[0]
+    left_rows, right_rows = left_rows.ready(), right_rows.ready()
     low = lax.broadcasted_iota(jnp.int32, (SPAN, 128), 1) < HEAD_DIM
 
     def attend(span, carry):
@@ -840,33 +971,29 @@
         return carry
 
     lax.fori_loop(0, tokens // SPAN, attend, 0)
-    context_arrived[...] = dot(context[...], restore[...]).astype(jnp.bfloat16)
-    context_t[...] = dot_nt(arrange[...], context[...]).astype(jnp.bfloat16)
-
-
-def front(lengths, hidden, restore, arrange, pieces):
-    tokens = hidden.shape[0]
+    attention_out.done()
+    context_arrived[...] = dot(context[...], restore_from(place)).astype(jnp.bfloat16)
+    context_t[...] = dot_nt(arrange_from(place), context[...]).astype(jnp.bfloat16)
+
+
+def attention_forward(place, lengths, left_rows, right_rows):
+    tokens = left_rows.shape[0]
     return run(
-        front_kernel,
-        "front",
-        [(lengths, "S")] + placed_at("H", hidden, restore, arrange, *in_order(pieces)),
-        [
-            ((tokens, FIRST_HALF), bf16, "H"),
-            ((tokens, FIRST_HALF), bf16, "H"),
-            ((16, D), f32, "V"),
-            ((tokens, 2 * D), bf16, "H"),
-            ((tokens, D), bf16, "H"),
-            ((D, tokens), bf16, "H"),
-            ((D, tokens), bf16, "H"),
-        ],
+        attention_kernel,
+        "attention_forward",
+        placed_at("S", place, lengths) + placed_at("H", left_rows, right_rows),
+        [((tokens, 2 * D), bf16, "H"), ((tokens, D), bf16, "V"), ((D, tokens), bf16, "H")],
         9e9,
         [pltpu.VMEM((tokens, D), bf16)],
+        total=28,
     )
 
 
 def gelu_parts(preact):
     scaled = jnp.abs(preact) * (0.5**0.5)
-    near = 1.0 / (1.0 + 0.3275911 * scaled)
+    below_one = 1.0 + 0.3275911 * scaled
+    near = pl.reciprocal(below_one, approx=True)
+    near = near * (2.0 - below_one * near)
     poly = near * (
         0.254829592
         + near * (-0.284496736 + near * (1.421413741 + near * (-1.453152027 + near * 1.061405429)))
@@ -893,79 +1020,99 @@
             yield (8 + part, device * ROW), (device * 4 + part) * ROW
 
 
-def middle_kernel(
-    hidden,
+def residual_kernel(
+    place,
+    vectors,
     context_arrived,
-    restore,
-    arrange,
-    vectors,
     l0,
     l1,
-    l2,
     l3,
-    r0,
-    r1,
-    r2,
-    r3,
-    active,
-    active_t,
-    slope,
+    both,
+    hidden,
+    moved,
     normed_out,
     factor_out,
     first_t,
-    inner_bias,
+    output_mat,
+    settling,
 ):
-    for at, column in vector_places():
-        inner_bias[:, column : column + ROW] = vectors[at[0] : at[0] + 1, at[1] : at[1] + ROW]
-    left, right = (l0, l1, l2, l3), (r0, r1, r2, r3)
-    residual = hidden[...].astype(jnp.float32) + vectors[2:3, :]
-    residual += dot(context_arrived[...], left_tile(left, slice(0, D)))
+    left = (l0, l1, Side(both, 0, l0.shape[1]), l3)
+    copies = settle((left, ()), SECOND_PARTS[:1], (output_mat,), settling)
+    residual = dot(context_arrived[...], left_tile(left, slice(0, D)))
+    residual += hidden[...].astype(jnp.float32) + vectors[2:3, :]
     first_out, normed, factor = normalize(residual, vectors[3:4, :], vectors[4:5, :])
     normed_out[...] = normed
     factor_out[...] = factor
     first16 = first_out.astype(jnp.bfloat16)
-    first_t[...] = dot_nt(arrange[...], first16).astype(jnp.bfloat16)
-    normed_out.done()
-    first_t.done()
-    moved = dot(first16, restore[...]).astype(jnp.bfloat16)
+    moved[...] = dot(first16, restore_from(place)).astype(jnp.bfloat16)
+    first_t[...] = dot_nt(arrange_from(place), first16).astype(jnp.bfloat16)
+    for copy in copies:
+        copy.wait()
+
+
+def residual_forward(place, hidden, context_arrived, vectors, pieces):
+    tokens, ordered = hidden.shape[0], in_order(pieces)
+    return run(
+        residual_kernel,
+        "residual",
+        [(place, "S")]
+        + placed_at("V", vectors, context_arrived, *ordered[:4])
+        + [(hidden, "H")],
+        [
+            ((tokens, D), bf16, "V"),
+            ((tokens, D), f32, "V"),
+            ((tokens, 1), f32, "V"),
+            ((D, tokens), bf16, "H"),
+            ((D, D), bf16, "A"),
+        ],
+        1e9,
+        [pltpu.SemaphoreType.DMA((4,))],
+        total=24,
+    )
+
+
+def feed_kernel(vectors, moved, l0, l1, l3, both, r0, r1, r3, active, active_t, slope, *rest):
+    mats, (inner_bias, settling) = rest[:-2], rest[-2:]
+    for at, column in vector_places():
+        inner_bias[:, column : column + ROW] = vectors[at[0] : at[0] + 1, at[1] : at[1] + ROW]
+    left, right = sides(l0, l1, l3, both, r0, r1, r3)
+    copies = settle((left, right), SECOND_PARTS[1:], mats, settling)
     for at, tile in second_tiles(left, right):
         columns = slice(at, at + FF_TILE)
-        value, derivative = gelu_parts(dot(moved, tile) + inner_bias[:, columns])
+        value, derivative = gelu_parts(dot(moved[...], tile) + inner_bias[:, columns])
         value16 = value.astype(jnp.bfloat16)
         active[:, columns] = value16
         active_t[columns, :] = jnp.transpose(value16)
         slope[:, columns] = derivative.astype(jnp.bfloat16)
-        active.done((slice(None), columns))
         active_t.done((columns, slice(None)))
         slope.done((slice(None), columns))
-
-
-def middle(hidden, context_arrived, restore, arrange, vectors, ff, pieces):
-    tokens = hidden.shape[0]
+    for copy in copies:
+        copy.wait()
+
+
+def feed_forward(moved, vectors, ff, pieces):
+    tokens = moved.shape[0]
     return run(
-        middle_kernel,
-        "middle",
-        placed_at("H", hidden, context_arrived, restore, arrange)
-        + placed_at("V", vectors)
-        + placed_at("H", *in_order(pieces)),
-        [
-            ((tokens, ff), bf16, "H"),
-            ((ff, tokens), bf16, "H"),
-            ((tokens, ff), bf16, "H"),
-            ((tokens, D), f32, "H"),
-            ((tokens, 1), f32, "V"),
-            ((D, tokens), bf16, "H"),
-        ],
+        feed_kernel,
+        "feed_forward",
+        placed_at("V", vectors, moved, *in_order(pieces)),
+        [((tokens, ff), bf16, "V"), ((ff, tokens), bf16, "H"), ((tokens, ff), bf16, "H")]
+        + [((D, width), bf16, "A") for _, _, width in SECOND_PARTS[1:]],
         8e9,
-        [pltpu.VMEM((1, ff), f32)],
+        [pltpu.VMEM((1, ff), f32), pltpu.SemaphoreType.DMA((44,))],
+        total=24,
     )
 
 
 def natural_rows(place, pieces, target, semaphore):
     rows = 4 * ROW
-    for at, piece in enumerate(pieces):
-        half = piece.shape[1]
-        is_right, core_off, far_off = at // 4, at // 2 % 2, at % 2
+    left, right = pieces[0].shape[1], pieces[4].shape[1]
+    near, far, far_core, near_core, right_near, right_far, right_far_core = pieces
+    places = [(near, 0, 0, 0, 0), (far, 0, 0, 1, 0), (near_core, 0, 1, 0, 0), (far_core, 0, 1, 1, 0)]
+    places += [(right_near, 1, 0, 0, 0), (right_far, 1, 0, 1, 0)]
+    places += [(near_core, 1, 1, 0, left), (right_far_core, 1, 1, 1, 0)]
+    for piece, is_right, core_off, far_off, start in places:
+        half = right if is_right else left
         for near_off in range(2):
             for z_off in range(4):
                 x_off, y_off = (far_off, near_off) if is_right else (near_off, far_off)
@@ -973,8 +1120,8 @@
                 block = block * 2 + (y_off ^ place[1])
                 to = pl.ds(pl.multiple_of(block * rows, rows), rows)
                 pltpu.make_async_copy(
-                    piece.at[pl.ds((near_off * 4 + z_off) * rows, rows), :],
-                    target.at[to, pl.ds(is_right * half, half)],
+                    piece.at[pl.ds((near_off * 4 + z_off) * rows, rows), pl.ds(start, half)],
+                    target.at[to, pl.ds(is_right * left, half)],
                     semaphore,
                 ).start()
     pltpu.make_async_copy(target, target, semaphore).wait()
@@ -987,11 +1134,10 @@
     vectors,
     l0,
     l1,
-    l2,
     l3,
+    both,
     r0,
     r1,
-    r2,
     r3,
     layer_out,
     normed_out,
@@ -1000,7 +1146,7 @@
     outer_mat,
     semaphore,
 ):
-    natural_rows(place, (l0, l1, l2, l3, r0, r1, r2, r3), outer_mat, semaphore)
+    natural_rows(place, (l0, l1, l3, both, r0, r1, r3), outer_mat, semaphore)
     total = first_normed[...] * vectors[3:4, :] + vectors[4:5, :] + vectors[5:6, :]
     total += dot(active[...], outer_mat[...])
     encoded, normed, factor = normalize(total, vectors[6:7, :], vectors[7:8, :])
@@ -1017,9 +1163,7 @@
         last_kernel,
         "last",
         [(place, "S")]
-        + placed_at("H", active, first_normed)
-        + [(vectors, "V")]
-        + placed_at("A", *in_order(pieces)),
+        + placed_at("V", active, first_normed, vectors, *in_order(pieces)),
         [
             ((tokens, D), bf16, "H"),
             ((tokens, D), f32, "V"),
@@ -1029,6 +1173,7 @@
         ],
         2.5e9,
         [pltpu.SemaphoreType.DMA],
+        total=16,
     )
 
 
@@ -1120,15 +1265,18 @@
     return jnp.concatenate([pick(place, kept, sent), pick(place, sent, kept)], axis=1)
 
 
-def slope_kernel(place, second_kept, second_sent, outer_mat, slope, kept, sent, sums):
-    second16 = both_halves(place[0], second_kept[...], second_sent[...])
-    half = kept.shape[1]
-    for at in range(0, 2 * half, D):
-        columns, inside = slice(at, at + D), slice(at % half, at % half + D)
-        grad = dot_nt(second16, outer_mat[columns, :]) * slope[:, columns].astype(jnp.float32)
+def slope_kernel(place, second_kept, second_sent, outer_mat, slope, kept, sent, sums, second16):
+    second16[...] = both_halves(place[0], second_kept[...], second_sent[...])
+    slope = slope.ready()
+    per_half = kept.shape[1] // D
+
+    def tile(at, carry):
+        columns = pl.ds(pl.multiple_of(at * D, D), D)
+        inside = pl.ds(pl.multiple_of((at % per_half) * D, D), D)
+        grad = dot_nt(second16[...], outer_mat[columns, :]) * slope[:, columns].astype(jnp.float32)
         sums[:, columns] = jnp.sum(grad, axis=0, keepdims=True)
         grad16 = grad.astype(jnp.bfloat16)
-        mine = place[0] == at // half
+        mine = place[0] == at // per_half
 
         @pl.when(mine)
         def keep():
@@ -1137,6 +1285,10 @@
         @pl.when(jnp.logical_not(mine))
         def send():
             sent[:, inside] = grad16
+
+        return carry
+
+    lax.fori_loop(0, 2 * per_half, tile, 0)
 
 
 def slope_back(place, second_kept, second_sent, outer_mat, slope):
@@ -1148,6 +1300,7 @@
         [(place, "S")] + placed_at("V", second_kept, second_sent, outer_mat) + [(slope, "H")],
         [half, half, ((1, ff), f32, "V")],
         2.5e9,
+        [pltpu.VMEM((tokens, D), bf16)],
     )
 
 
@@ -1210,35 +1363,22 @@
     place,
     preact_kept,
     preact_sent,
-    second_grad,
-    normed,
     factor,
     vectors,
-    restore,
-    l0,
-    l1,
-    l2,
-    l3,
-    r0,
-    r1,
-    r2,
-    r3,
-    residual_grad,
-    kept,
-    sent,
-    context_grad,
-    sums,
+    *refs,
 ):
-    left, right = (l0, l1, l2, l3), (r0, r1, r2, r3)
-    total = jnp.zeros(second_grad.shape, jnp.float32)
+    output_mat, inner_mats = refs[0], refs[1:7]
+    second_grad, normed, residual_grad, kept, sent, context_grad, sums = refs[7:]
+    restore = restore_from(place)
+    total = jnp.zeros((factor.shape[0], D), jnp.float32)
     half = preact_kept.shape[1]
-    for at, tile in second_tiles(left, right):
+    for at, tile in zip(range(0, 2 * half, FF_TILE), inner_mats):
         columns = slice(at % half, at % half + FF_TILE)
         kept_part, sent_part = preact_kept[:, columns], preact_sent[:, columns]
         if at >= half:
             kept_part, sent_part = sent_part, kept_part
-        total += dot_nt(pick(place[0], kept_part, sent_part), tile)
-    first_grad = second_grad[...] + whole_precision(total, restore[...])
+        total += dot_nt(pick(place[0], kept_part, sent_part), tile[...])
+    first_grad = second_grad[...] + whole_precision(total, restore)
     grad, gain_sum, shift_sum = normalize_back(first_grad, normed[...], factor[...], vectors[3:4, :])
     residual_grad[...] = grad
     sums[0:1, :] = jnp.sum(grad, axis=0, keepdims=True)
@@ -1247,21 +1387,19 @@
     grad16 = grad.astype(jnp.bfloat16)
     kept[...] = pick(place[0], grad16[:, : D // 2], grad16[:, D // 2 :])
     sent[...] = pick(place[0], grad16[:, D // 2 :], grad16[:, : D // 2])
-    moved = dot_nt(grad16, left_tile(left, slice(0, D))).astype(jnp.bfloat16)
-    context_grad[...] = dot_nt(moved, restore[...]).astype(jnp.bfloat16)
-
-
-def first_back(place, preact_kept, preact_sent, second_grad, normed, factor, vectors, restore, pieces):
+    moved = dot_nt(grad16, output_mat[...]).astype(jnp.bfloat16)
+    context_grad[...] = dot_nt(moved, restore).astype(jnp.bfloat16)
+
+
+def first_back(place, preact_kept, preact_sent, second_grad, normed, factor, vectors, mats):
     tokens = second_grad.shape[0]
     half = ((tokens, D // 2), bf16, "V")
     return run(
         first_kernel,
         "first_back",
         [(place, "S")]
-        + placed_at("V", preact_kept, preact_sent)
-        + placed_at("H", second_grad, normed)
-        + placed_at("V", factor, vectors)
-        + placed_at("H", restore, *in_order(pieces)),
+        + placed_at("V", preact_kept, preact_sent, factor, vectors)
+        + placed_at("H", *mats, second_grad, normed),
         [((tokens, D), f32, "H"), half, half, ((tokens, D), bf16, "V"), ((3, D), f32, "V")],
         4.9e9,
     )
@@ -1375,7 +1513,7 @@
 
 
 def attention_gradient_kernel(
-    arrange,
+    place,
     sums,
     other_sums,
     hidden_t,
@@ -1398,7 +1536,7 @@
     left_sent[:, :D] = grad[half:]
     total = (sums[...] + other_sums[...]).astype(jnp.bfloat16)
     total = jnp.concatenate([total, jnp.zeros((112, D), jnp.bfloat16)])
-    small = dot_nt(arrange[...], total).astype(jnp.bfloat16)
+    small = dot_nt(arrange_from(place), total).astype(jnp.bfloat16)
     left_kept[:, D:] = small[:half]
     left_sent[:, D:] = small[half:]
     value = dot(hidden_t[...], grads[:, D:]) + dot(other_hidden_t[...], other_grads[:, D:])
@@ -1409,7 +1547,7 @@
 
 def attention_gradient(*operands):
     left, right = ((D // 2, D + 128), bf16, "V"), ((D // 2, D), bf16, "V")
-    places = ["H"] + ["V"] * 2 + ["H"] * 4 + ["V"] * 4
+    places = ["S"] + ["V"] * 2 + ["H"] * 4 + ["V"] * 4
     return run(
         attention_gradient_kernel,
         "attention_gradient",
@@ -1419,29 +1557,31 @@
     )
 
 
-def input_kernel(place, residual_grad, kept, sent, restore, l0, l1, l2, l3, r0, r1, r2, r3, input_grad):
-    left, right = (l0, l1, l2, l3), (r0, r1, r2, r3)
+def input_kernel(
+    place, kept, sent, query_mat, low_key_mat, high_key_mat, value_mat, residual_grad, input_grad
+):
+    restore = restore_from(place)
     half = D // 2
     parts = []
     for at in range(3):
         columns = slice(at * half, (at + 1) * half)
         parts.append(both_halves(place[0], kept[:, columns], sent[:, columns]))
     query_grad, key_grad, value_grad = parts
-    total = dot_nt(query_grad, left_tile(left, slice(0, D)))
-    total += dot_nt(key_grad[:, :512], left_tile(left, slice(D, FIRST_HALF)))
-    total += dot_nt(key_grad[:, 512:], right_tile(right, slice(256, 512)))
-    total += dot_nt(value_grad, right_tile(right, slice(512, FIRST_HALF)))
-    total = residual_grad[...] + whole_precision(total, restore[...])
+    total = dot_nt(query_grad, query_mat[...])
+    total += dot_nt(key_grad[:, :512], low_key_mat[...])
+    total += dot_nt(key_grad[:, 512:], high_key_mat[...])
+    total += dot_nt(value_grad, value_mat[...])
+    total = residual_grad[...] + whole_precision(total, restore)
     input_grad[...] = total.astype(jnp.bfloat16)
 
 
-def input_back(place, residual_grad, kept, sent, restore, pieces):
+def input_back(place, residual_grad, kept, sent, mats):
     return run(
         input_kernel,
         "input_back",
-        [(place, "S"), (residual_grad, "H")]
+        [(place, "S")]
         + placed_at("V", kept, sent)
-        + placed_at("H", restore, *in_order(pieces)),
+        + placed_at("H", *mats, residual_grad),
         [(residual_grad.shape, bf16, "H")],
         3e9,
     )[0]
@@ -1498,9 +1638,55 @@
     )(left, left_in, right, right_in)
 
 
-def finish_kernel(place, own, first, second, third, mine, other):
+def add_join_kernel(left, left_in, right, right_in, kept, sent):
+    width = left.shape[-1]
+    for part, received, columns in (
+        (left, left_in, slice(0, width)),
+        (right, right_in, slice(width, width + right.shape[-1])),
+    ):
+        rows = part.shape[0] // 2
+        total = part[...].astype(jnp.float32) + received[...].astype(jnp.float32)
+        kept[..., columns] = total[:rows]
+        sent[..., columns] = total[rows:].astype(jnp.bfloat16)
+
+
+def add_join(left, left_in, right, right_in):
+    shape = (left.shape[0] // 2,) + left.shape[1:-1] + (left.shape[-1] + right.shape[-1],)
+    return pl.pallas_call(
+        add_join_kernel,
+        in_specs=[VMEM] * 4,
+        out_specs=[VMEM] * 2,
+        out_shape=[jax.ShapeDtypeStruct(shape, jnp.float32), jax.ShapeDtypeStruct(shape, jnp.bfloat16)],
+        compiler_params=params(),
+        cost_estimate=cost(1, 1),
+        name="add_join",
+    )(left, left_in, right, right_in)
+
+
+def add_half_kernel(own, received, kept, sent):
+    rows = own.shape[0] // 2
+    total = own[...] + received[...].astype(jnp.float32)
+    kept[...] = total[:rows]
+    sent[...] = total[rows:].astype(jnp.bfloat16)
+
+
+def add_half(own, received):
+    shape = (own.shape[0] // 2,) + own.shape[1:]
+    return pl.pallas_call(
+        add_half_kernel,
+        in_specs=[VMEM] * 2,
+        out_specs=[VMEM] * 2,
+        out_shape=[jax.ShapeDtypeStruct(shape, jnp.float32), jax.ShapeDtypeStruct(shape, jnp.bfloat16)],
+        compiler_params=params(),
+        cost_estimate=cost(1, 1),
+        name="add_half",
+    )(own, received)
+
+
+def finish_kernel(place, own, *refs):
+    received_all, (mine, other) = refs[:-2], refs[-2:]
     total = own[...]
-    for received in (first, second, third):
+    for received in received_all:
         total = total + received[...].astype(jnp.float32)
     if len(total.shape) == 3:
         low, high = total[0], total[1]
@@ -1514,7 +1700,7 @@
     rows = own.shape[1] if own.ndim == 3 else ROW
     return pl.pallas_call(
         finish_kernel,
-        in_specs=[SMEM] + [VMEM] * 4,
+        in_specs=[SMEM] + [VMEM] * (1 + len(received)),
         out_specs=[VMEM] * 2,
         out_shape=[jax.ShapeDtypeStruct((rows, own.shape[-1]), jnp.float32)] * 2,
         compiler_params=params(),
@@ -1574,6 +1760,10 @@
 
 def second_transfers(pieces):
     return [across(pieces[1], 2), mate(pieces[3])]
+
+
+def add_joined(pieces, received):
+    return add_join(pieces[0], received[0], pieces[2], received[1])
 
 
 def add_second(pieces, received):
@@ -1607,7 +1797,6 @@
 ):
     core, x_at, z_at, y_at = coordinates()
     place = jnp.stack([core, y_at, x_at, z_at]).astype(jnp.int32)
-    restore, arrange = permutations()
     first_block, second_block = pack(
         query_weight,
         key_weight,
@@ -1628,42 +1817,63 @@
     )
     ff = inner_weight.shape[1]
     first_z = z_exchange(first_block)
+    second_z = across(second_block, 4)
+    first_z = tied(first_z, second_z)
     first = stack_z(first_block, first_z, FIRST_HALF)
+    second = stack_two(after(second_block, *first), second_z, SECOND_HALF)
+    first, third_block = tied(first, *second), after(outer_weight, *second)
     first_in = near_exchange(first)
-    second_z = z_exchange(after(second_block, *first))
-    first = stack_near(first, first_in)
+    second_left_z = across(second[0], 8)
+    *first, first_both = stack_near(first, tied(first_in, second_left_z))
+    second_right = after(second[1], *first)
     first_far = far_exchange(first)
-    first_core = core_exchange(first)
-    second = stack_z(after(second_block, *first_far), second_z, SECOND_HALF)
+    second_right_z = across(second_right, 8)
+    first_core = across(first_both, 1)
+    second = stack_pair(
+        second[0], second_left_z, second_right, after(second_right_z, first_core, *first_far)
+    )[:2]
+    first_far, third_block = tied(first_far, *second), after(third_block, *second)
     second_in = near_exchange(second)
-    third_z = z_exchange(after(outer_weight, *second))
-    first_far_core = core_exchange(tied(first_far, *second))
-    second = stack_near(second, second_in)
+    first_far_core = core_exchange(first_far)
+    third_z = across(after(third_block, *first_far_core), 4)
+    third_two = stack_z_two(third_block, third_z)
+    left_rows, right_rows, vectors, hidden_t, *first_mats = project(
+        place, hidden_in, pieces_of(first, first_far, first_core, first_far_core)
+    )
+    *second, second_both = stack_near(second, tied(second_in, vectors, third_two))
+    third_two, left_rows = tied((third_two, left_rows), *second)
     second_far = far_exchange(second)
-    second_core = core_exchange(second)
-    first_pieces = pieces_of(first, first_far, first_core, tied(first_far_core, *second))
-    left_rows, right_rows, vectors, attention, context_arrived, hidden_t, context_t = front(
-        span_lengths, hidden_in, restore, arrange, first_pieces
-    )
-    third = stack_z(after(outer_weight, vectors, *second_far), third_z, D // 2)
+    third_z = across(third_two, 8)
+    second_core = across(second_both, 1)
+    attention, context_arrived, context_t = attention_forward(
+        place, span_lengths, left_rows, right_rows
+    )
+    third = stack_z(third_two, tied([third_z], context_arrived, second_core, *second_far), D // 2)
+    second_far = tied(second_far, *third)
     third_in = near_exchange(third)
-    second_far_core = core_exchange(tied(second_far, *third))
-    third = stack_near(third, third_in)
+    second_far_core = core_exchange(second_far)
+    second_pieces = pieces_of(second, second_far, second_core, second_far_core)
+    moved, first_normed, first_factor, first_t, output_mat = residual_forward(
+        place, hidden_in, context_arrived, vectors, second_pieces
+    )
+    *third, third_both = stack_near(third, tied(third_in, moved, *second_far_core))
+    moved = after(moved, *third)
     third_far = far_exchange(third)
-    third_core = core_exchange(third)
-    second_pieces = pieces_of(second, second_far, second_core, tied(second_far_core, *third))
-    active, active_t, slope, first_normed, first_factor, first_t = middle(
-        hidden_in, context_arrived, restore, arrange, vectors, ff, second_pieces
-    )
-    third_far_core = core_exchange(tied(third_far, first_factor))
+    third_core = across(third_both, 1)
+    active, active_t, slope, *inner_mats = feed_forward(moved, vectors, ff, second_pieces)
+    second_mats = [output_mat, *inner_mats]
+    third_far = tied(third_far, active, third_core)
+    third_far_core = core_exchange(third_far)
     third_pieces = pieces_of(third, third_far, third_core, third_far_core)
+    hidden_t, context_t, first_t, active_t, active = tied(
+        (hidden_t, context_t, first_t, active_t, active), *third_far_core
+    )
+    other_active_t, other_first_t = across(active_t, 1), across(first_t, 1)
+    other_hidden_t, other_context_t = across(hidden_t, 1), across(context_t, 1)
     layer_out, second_normed, second_factor, cls_rows, outer_mat = last(
         place, active, first_normed, vectors, third_pieces
     )
     other_rows = mate(cls_rows)
-    hidden_t, context_t, first_t, active_t = tied((hidden_t, context_t, first_t, active_t), cls_rows)
-    other_hidden_t, other_context_t = across(hidden_t, 1), across(context_t, 1)
-    other_first_t, other_active_t = across(first_t, 1), across(active_t, 1)
     second_grad, second_kept, second_sent, second_sums, span_loss = turn(
         place, partner_span, cotangent, second_normed, second_factor, vectors, cls_rows, other_rows
     )
@@ -1671,34 +1881,36 @@
     preact_kept, preact_sent, inner_sums = slope_back(
         place, second_kept, second_sent, outer_mat, slope
     )
+    second_received = after(second_received, preact_kept)
+    outer_parts = outer_gradient(place, active_t, other_active_t, second_kept, second_received)
+    preact_kept, preact_sent = tied((preact_kept, preact_sent), *outer_parts)
+    outer_in = first_transfers(outer_parts)
     preact_received = across(preact_sent, 1)
-    outer_parts = outer_gradient(
-        place, active_t, other_active_t, after(second_kept, preact_kept), second_received
-    )
-    outer_in = first_transfers(outer_parts)
     residual_grad, residual_kept, residual_sent, context_grad, first_sums = first_back(
         place,
-        after(preact_kept, outer_parts[0]),
+        preact_kept,
         preact_sent,
         second_grad,
         first_normed,
         first_factor,
         vectors,
-        restore,
-        second_pieces,
-    )
-    outer_parts = add_first(outer_parts, tied(outer_in, context_grad))
+        second_mats,
+    )
+    outer_parts = add_first(outer_parts, tied(outer_in, context_grad, preact_received))
+    residual_sent, preact_kept = tied((residual_sent, preact_kept), *outer_parts)
     outer_in = second_transfers(outer_parts)
-    residual_received = across(after(residual_sent, outer_parts[0]), 1)
-    inner_parts = inner_gradient(
-        first_t, other_first_t, after(preact_kept, outer_parts[0]), preact_received
-    )
-    outer_parts = add_second(outer_parts, tied(outer_in, inner_parts[0]))
-    outer_in = third_transfers(outer_parts)
-    inner_in = first_transfers(tied(inner_parts, outer_parts[0]))
+    residual_received = across(residual_sent, 1)
+    inner_parts = inner_gradient(first_t, other_first_t, preact_kept, preact_received)
+    outer_own, outer_sent = add_joined(
+        outer_parts, tied(outer_in, residual_received, *inner_parts)
+    )
+    inner_parts = tied(inner_parts, outer_own)
+    context_grad = after(context_grad, *inner_parts)
+    inner_in = first_transfers(inner_parts)
+    outer_in = across(outer_sent, 8)
     grads_kept, grads_sent, sums = attend_back(
         place,
-        after(context_grad, inner_parts[0], outer_parts[0]),
+        context_grad,
         left_rows,
         right_rows,
         attention,
@@ -1706,47 +1918,52 @@
         second_sums,
         inner_sums,
     )
-    inner_parts = add_first(inner_parts, tied(inner_in, sums))
+    inner_parts = add_first(inner_parts, tied(inner_in, sums, outer_in))
+    outer_own, outer_in = tied((outer_own, outer_in), *inner_parts)
+    grads_sent, sums = tied((grads_sent, sums), *inner_parts)
     inner_in = second_transfers(inner_parts)
-    grads_received = across(after(grads_sent, inner_parts[0]), 1)
-    other_sums = across(after(sums, inner_parts[0]), 1)
-    outer_mine, outer_other = finish(place, outer_parts[0], tied(outer_in, inner_parts[0]))
-    outer_other = across(outer_other, 1)
+    grads_received, other_sums = across(grads_sent, 1), across(sums, 1)
+    outer_own, outer_sent = add_half(outer_own, outer_in)
+    grads_received = after(grads_received, outer_own)
     rest_parts = attention_gradient(
-        arrange,
+        place,
         sums,
         other_sums,
         hidden_t,
         other_hidden_t,
         context_t,
         other_context_t,
-        after(grads_kept, outer_mine),
+        grads_kept,
         grads_received,
         residual_kept,
         residual_received,
     )
-    inner_parts = add_second(inner_parts, tied(inner_in, rest_parts[0]))
-    rest_in = first_transfers(tied(rest_parts, inner_parts[0]))
-    inner_in = third_transfers(inner_parts)
-    input_grad = input_back(
-        place,
-        residual_grad,
-        after(grads_kept, rest_parts[0], inner_parts[0]),
-        grads_sent,
-        restore,
-        first_pieces,
-    )
-    rest_parts = add_first(rest_parts, tied(rest_in, input_grad))
+    inner_own, inner_sent = add_joined(inner_parts, tied(inner_in, *rest_parts))
+    rest_parts = tied(rest_parts, inner_own)
+    outer_sent, grads_kept = tied((outer_sent, grads_kept), inner_own)
+    rest_in = first_transfers(rest_parts)
+    inner_in = across(inner_sent, 8)
+    outer_in = across(outer_sent, 4)
+    input_grad = input_back(place, residual_grad, grads_kept, grads_sent, first_mats)
+    rest_parts = add_first(rest_parts, tied(rest_in, input_grad, outer_in, inner_in))
+    inner_own, inner_in, outer_own, outer_in = tied(
+        (inner_own, inner_in, outer_own, outer_in), *rest_parts
+    )
     rest_in = second_transfers(rest_parts)
-    inner_mine, inner_other = finish(place, inner_parts[0], tied(inner_in, rest_parts[0]))
+    inner_own, inner_sent = add_half(inner_own, inner_in)
+    inner_in = across(inner_sent, 4)
+    outer_mine, outer_other = finish(place, outer_own, [outer_in])
+    outer_other = across(outer_other, 1)
+    rest_parts = add_second(rest_parts, tied(rest_in, inner_in, outer_other))
+    inner_in, outer_other = tied((inner_in, outer_other), *rest_parts)
+    rest_in = third_transfers(rest_parts)
+    inner_mine, inner_other = finish(place, inner_own, [inner_in])
     inner_other = across(inner_other, 1)
     (outer_grad,) = placed(
-        outer_out_kernel, "outer_out", place, outer_mine, after(outer_other, inner_mine), [(4 * ROW, D)]
-    )
-    rest_parts = add_second(rest_parts, tied(rest_in, outer_grad))
-    rest_in = third_transfers(rest_parts)
+        outer_out_kernel, "outer_out", place, outer_mine, outer_other, [(4 * ROW, D)]
+    )
     (inner_grad,) = placed(
-        inner_out_kernel, "inner_out", place, inner_mine, after(inner_other, rest_parts[0]), [(ROW, ff)]
+        inner_out_kernel, "inner_out", place, inner_mine, after(inner_other, outer_grad), [(ROW, ff)]
     )
     rest_mine, rest_other = finish(place, rest_parts[0], tied(rest_in, inner_grad))
     rest_other = across(rest_other, 1)

time: 268 us -> 251 us (0.937)
  waiting for transfers between devices: 100 us -> 75.9 us
  Pallas kernels: 100 us -> 114 us
  starting transfers between devices: 59.2 us -> 51.5 us
    ppermute x54 -> x48, waiting for transfers between devices: 87.8 us -> 65.7 us  [across(): return lax.ppermute(block, 'doc', [(at, at ^ mask) for at in range(count)])]
    pallas_call x12 -> x14, Pallas kernels: 91.9 us -> 103 us  [run(): pl.pallas_call(body, in_specs=[spaces[place] for place in in_places], out...]
    ppermute x54 -> x48, starting transfers between devices: 44.6 us -> 40.4 us  [across(): return lax.ppermute(block, 'doc', [(at, at ^ mask) for at in range(count)])]
    ppermute x13, starting transfers between devices: 14.6 us -> 11.1 us  [mate(): return lax.ppermute(block, 'pair', [(0, 1), (1, 0)])]
  transfers between devices with their start and end apart: 67 -> 61, of which waited for: 33 -> 35; matrix products, arithmetic and copies ran while one was open for 0% -> 0% of each run, Pallas kernels for 33% -> 40%
where the time goes in v1:
time: 251 us; the launch traced here: 246 us
  Pallas kernels  114 us (45%)
  waiting for transfers between devices  75.9 us (30%)
  starting transfers between devices  51.5 us (21%)
  local copies, waits for them, and re-layouts  3.18 us (1%)
    pallas_call x14, Pallas kernels, run(): pl.pallas_call(body, in_specs=[spaces[place] for place in in_places], out...  103 us
    ppermute x48, waiting for transfers between devices, across(): return lax.ppermute(block, 'doc', [(at, at ^ mask) for at in range(count)])  65.7 us
    ppermute x48, starting transfers between devices, across(): return lax.ppermute(block, 'doc', [(at, at ^ mask) for at in range(count)])  40.4 us
    ppermute x13, starting transfers between devices, mate(): return lax.ppermute(block, 'pair', [(0, 1), (1, 0)])  11.1 us
    ppermute x13, waiting for transfers between devices, mate(): return lax.ppermute(block, 'pair', [(0, 1), (1, 0)])  10.2 us
  transfers between devices with their start and end apart: 61, of which 35 were waited for; matrix products, arithmetic and copies ran while one was open for 0% of the time, Pallas kernels for 40%

profile of v1, /device:TPU:0, one launch (start us, length us, event | category | flops | bytes accessed | tf_op | source)
XLA Modules:
  0.0 246.1 jit_solution(10009645049949571705)
XLA Ops:
  0.7 2.0 pack.1
  2.6 3.1 %collective-permute-start.3 = (bf16[24,3840]{1,0:T(8,128)(2,1)}, bf16[24,3840]{1,0:T(8,128)(2,1)S(1)}, u32[]{:S(2)}, u32[]{:S(2)}) collective-permute-start(bf16[24,3840]{1,0:T(8,128)(2,1)} %get-tuple-element.220.first), channel_id=1, source_target_pairs={{0,8},{2,10},{4,12},{6,14},{8,0},{10,2},{12,4},{14,6},{16,24},{18,... | collective-permute-start | bytes 552968 | tf_op jit(solution)/shard_map/ppermute | solution.py:24
  5.7 2.5 %collective-permute-start.2 = (bf16[24,2560]{1,0:T(8,128)(2,1)}, bf16[24,2560]{1,0:T(8,128)(2,1)S(1)}, u32[]{:S(2)}, u32[]{:S(2)}) collective-permute-start(bf16[24,2560]{1,0:T(8,128)(2,1)} %get-tuple-element.213.refs_0_), channel_id=1, source_target_pairs={{0,24},{2,26},{4,28},{6,30},{8,16},{10,18},{12,20},{14,22},{16,8},... | collective-permute-start | bytes 368648 | tf_op jit(solution)/shard_map/ppermute | solution.py:24
  8.3 1.8 collective-permute-start
  10.1 6.5 %collective-permute-done.2.refs_3_ = bf16[24,2560]{1,0:T(8,128)(2,1)S(1)} collective-permute-done((bf16[24,2560]{1,0:T(8,128)(2,1)}, bf16[24,2560]{1,0:T(8,128)(2,1)S(1)}, u32[]{:S(2)}, u32[]{:S(2)}) %collective-permute-start.2) | collective-permute-done | bytes 122912 | tf_op jit(solution)/shard_map/ppermute | solution.py:24
  16.7 2.8 %collective-permute-done.1.refs_2_ = bf16[24,2560]{1,0:T(8,128)(2,1)S(1)} collective-permute-done((bf16[24,2560]{1,0:T(8,128)(2,1)}, bf16[24,2560]{1,0:T(8,128)(2,1)S(1)}, u32[]{:S(2)}, u32[]{:S(2)}) %collective-permute-start.1) | collective-permute-done | bytes 122912 | tf_op jit(solution)/shard_map/ppermute | solution.py:24
  21.4 1.6 collective-permute-start.4
  22.9 1.5 collective-permute-start.5
  24.5 1.8 collective-permute-start.6
  26.3 7.4 %collective-permute-done.6.left_in = bf16[48,1792]{1,0:T(8,128)(2,1)S(1)} collective-permute-done((bf16[48,1792]{1,0:T(8,128)(2,1)S(1)}, bf16[48,1792]{1,0:T(8,128)(2,1)S(1)}, u32[]{:S(2)}, u32[]{:S(2)}) %collective-permute-start.6) | collective-permute-done | bytes 172064 | tf_op jit(solution)/shard_map/ppermute | solution.py:24
  35.0 11.3 %collective-permute-done.10.right_in = bf16[48,2048]{1,0:T(8,128)(2,1)S(1)} collective-permute-done((bf16[48,2048]{1,0:T(8,128)(2,1)S(1)}, bf16[48,2048]{1,0:T(8,128)(2,1)S(1)}, u32[]{:S(2)}, u32[]{:S(2)}) %collective-permute-start.10) | collective-permute-done | bytes 196640 | tf_op jit(solution)/shard_map/ppermute | solution.py:24
  50.0 1.5 collective-permute-start.14
  51.6 8.0 %project.1 = (bf16[512,1280]{1,0:T(8,128)(2,1)}, bf16[512,1280]{1,0:T(8,128)(2,1)}, f32[16,768]{1,0:T(8,128)S(1)}, bf16[768,512]{1,0:T(8,128)(2,1)}, bf16[768,76...) custom-call(s32[4]{0:T(128)S(1)} %pad_add_fusion.refs_0_.place, ...), custom_call_target="tpu_custom_call" | custom-call | flops 1 | bytes 1 | tf_op jit(solution)/shard_map/project/pallas_call | solution.py:641
  60.8 1.5 stack_pair.6
  62.4 1.5 collective-permute-start.17
  64.6 2.5 %collective-permute-start.18 = (bf16[192,768]{1,0:T(8,128)(2,1)S(1)}, bf16[192,768]{1,0:T(8,128)(2,1)S(1)}, u32[]{:S(2)}, u32[]{:S(2)}) collective-permute-start(bf16[192,768]{1,0:T(8,128)(2,1)S(1)} %stack_z_two.1.refs_0_), channel_id=1, source_target_pairs={{0,16},{2,18},{4,20},{6,22},{8,24},{10,26},{12,28},{14,30},{16,0},... | collective-permute-start | bytes 884744 | tf_op jit(solution)/shard_map/ppermute | solution.py:24
  68.5 6.6 %attention_forward.1 = (bf16[512,1536]{1,0:T(8,128)(2,1)S(1)}, bf16[512,768]{1,0:T(8,128)(2,1)S(1)}, bf16[768,512]{1,0:T(8,128)(2,1)S(1)}) custom-call(s32[4]{0:T(128)S(1)} %pad_add_fusion.refs_0_.place, s32[4]{0:T(128)S(1)} %copy-done.12, bf16[512,1280]{1,0:T(8,128)(2,1)S(1)} %copy-done, bf16[512,1280]{1,0:T(8,128)(2,1)S(1)} %copy-done.1), custom_call_target="tpu_custom_call" | custom-call | flops 1 | bytes 1 | tf_op jit(solution)/shard_map/attention_forward/pallas_call | solution.py:641
  75.1 5.5 %collective-permute-done.18.refs_1_ = bf16[192,768]{1,0:T(8,128)(2,1)S(1)} collective-permute-done((bf16[192,768]{1,0:T(8,128)(2,1)S(1)}, bf16[192,768]{1,0:T(8,128)(2,1)S(1)}, u32[]{:S(2)}, u32[]{:S(2)}) %collective-permute-start.18) | collective-permute-done | bytes 294944 | tf_op jit(solution)/shard_map/ppermute | solution.py:24
  83.0 1.5 collective-permute-start.21
  85.7 4.0 %residual.1 = (bf16[512,768]{1,0:T(8,128)(2,1)S(1)}, f32[512,768]{1,0:T(8,128)S(1)}, f32[512,1]{1,0:T(8,128)S(1)}, bf16[768,512]{1,0:T(8,128)(2,1)S(1)}, bf16[768,768]{1,0:T(8,128)(2,1)S(1)}) custom-call(s32[4]{0:T(128)S(1)} %pad_add_fusion.refs_0_.place, f32[16,768]{1,0:T(8,128)S(1)} %get-tuple-element.241.refs_1_.refs_0_.refs_3_.refs_5_.refs_4_, ...), custom_call_target="tpu_custom_call" | custom-call | flops 1 | bytes 1 | tf_op jit(solution)/shard_map/residual/pallas_call | solution.py:641
  89.8 2.2 collective-permute-done.21.left_in
  95.5 23.1 %feed_forward.1 = (bf16[512,3072]{1,0:T(8,128)(2,1)S(1)}, bf16[3072,512]{1,0:T(8,128)(2,1)S(1)}, bf16[512,3072]{1,0:T(8,128)(2,1)S(1)}, bf16[768,512]{1,0:T(8,12...) custom-call(f32[16,768]{1,0:T(8,128)S(1)} %get-tuple-element.241.ref, ...), custom_call_target="tpu_custom_call" | custom-call | flops 1 | bytes 1 | tf_op jit(solution)/shard_map/feed_forward/pallas_call | solution.py:641
  119.3 1.5 collective-permute-done.27.refs_6_
  121.8 5.8 %last.1 = (bf16[512,768]{1,0:T(8,128)(2,1)}, f32[512,768]{1,0:T(8,128)S(1)}, f32[512,1]{1,0:T(8,128)S(1)}, bf16[4,768]{1,0:T(4,128)(2,1)S(1)}, bf16[3072,768]{1,0:T(8,128)(2,1)S(1)}) custom-call(s32[4]{0:T(128)S(1)} %pad_add_fusion.refs_0_.place, bf16[512,3072]{1,0:T(8,128)(2,1)S(1)} %get-tuple-element.269.refs_1_, ...), custom_call_target="tpu_custom_call" | custom-call | flops 1 | bytes 1 | tf_op jit(solution)/shard_map/last/pallas_call | solution.py:641
  128.2 3.1 %collective-permute-done.30.refs_7_ = bf16[4,768]{1,0:T(4,128)(2,1)S(1)} collective-permute-done((bf16[4,768]{1,0:T(4,128)(2,1)S(1)}, bf16[4,768]{1,0:T(4,128)(2,1)S(1)}, u32[]{:S(2)}, u32[]{:S(2)}) %collective-permute-start.30) | collective-permute-done | bytes 6176 | tf_op jit(solution)/shard_map/ppermute | solution.py:28
  131.2 2.8 %turn.1 = (f32[512,768]{1,0:T(8,128)S(1)}, bf16[512,384]{1,0:T(8,128)(2,1)S(1)}, bf16[512,384]{1,0:T(8,128)(2,1)S(1)}, f32[3,768]{1,0:T(4,128)S(1)}, f32[1,4]{1,0:T(1,128)}) custom-call(s32[4]{0:T(128)S(1)} %pad_add_fusion.refs_0_.place, s32[1,4]{1,0:T(1,128)S(1)} %copy-done.13, bf16[512,768]{1,0:T(8,128)(2,1)S(1)} %copy-done.8, ...), custom_call_target="tpu_custom_call" | custom-call | flops 1 | bytes 1 | tf_op jit(solution)/shard_map/turn/pallas_call | solution.py:641
  134.1 4.5 %slope_back.1 = (bf16[512,1536]{1,0:T(8,128)(2,1)S(1)}, bf16[512,1536]{1,0:T(8,128)(2,1)S(1)}, f32[1,3072]{1,0:T(1,128)S(1)}) custom-call(s32[4]{0:T(128)S(1)} %pad_add_fusion.refs_0_.place, bf16[512,384]{1,0:T(8,128)(2,1)S(1)} %get-tuple-element.276.refs_1_.refs_3_, bf16[512,384]{1,0:T(8,128)(2,1)S(1)} %get-tuple-element.277.refs_2_, ...), custom_call_target="tpu_custom_call" | custom-call | flops 1 | bytes 1 | tf_op jit(solution)/shard_map/slope_back/pallas_call | solution.py:641
  138.7 6.4 %outer_gradient.1 = (bf16[16,48,384]{2,1,0:T(8,128)(2,1)S(1)}, bf16[16,48,384]{2,1,0:T(8,128)(2,1)S(1)}, bf16[16,48,384]{2,1,0:T(8,128)(2,1)S(1)}, bf16[16,48,384]{2,1,0:T(8,128)(2,1)S(1)}) custom-call(s32[4]{0:T(128)S(1)} %pad_add_fusion.refs_0_.place, bf16[3072,512]{1,0:T(8,128)(2,1)S(1)} %get-tuple-element.272.refs_1_, ...), custom_call_target="tpu_custom_call" | custom-call | flops 1 | bytes 1 | tf_op jit(solution)/shard_map/outer_gradient/pallas_call | solution.py:641
  146.2 1.5 collective-permute-start.33
  147.7 12.2 %first_back.1 = (f32[512,768]{1,0:T(8,128)S(1)}, bf16[512,384]{1,0:T(8,128)(2,1)S(1)}, bf16[512,384]{1,0:T(8,128)(2,1)S(1)}, bf16[512,768]{1,0:T(8,128)(2,1)S(1)}, f32[3,768]{1,0:T(4,128)S(1)}) custom-call(s32[4]{0:T(128)S(1)} %pad_add_fusion.refs_0_.place, bf16[512,1536]{1,0:T(8,128)(2,1)S(1)} %get-tuple-element.308.refs_1_.refs_2_, ...), custom_call_target="tpu_custom_call" | custom-call | flops 1 | bytes 1 | tf_op jit(solution)/shard_map/first_back/pallas_call | solution.py:641
  161.6 1.6 collective-permute-start.35
  163.9 2.9 %inner_gradient.1 = (bf16[384,768]{1,0:T(8,128)(2,1)S(1)}, bf16[384,768]{1,0:T(8,128)(2,1)S(1)}, bf16[384,768]{1,0:T(8,128)(2,1)S(1)}, bf16[384,768]{1,0:T(8,128)(2,1)S(1)}) custom-call(bf16[768,512]{1,0:T(8,128)(2,1)S(1)} %get-tuple-element.307.refs_0_, bf16[768,512]{1,0:T(8,128)(2,1)S(1)} %collective-permute-done.38.refs_1_, ...), custom_call_target="tpu_custom_call" | custom-call | flops 1 | bytes 1 | tf_op jit(solution)/shard_map/inner_gradient/pallas_call | solution.py:641
  166.8 4.2 %collective-permute-done.35.left_in = bf16[8,48,384]{2,1,0:T(8,128)(2,1)S(1)} collective-permute-done((bf16[8,48,384]{2,1,0:T(8,128)(2,1)S(1)}, bf16[8,48,384]{2,1,0:T(8,128)(2,1)S(1)}, u32[]{:S(2)}, u32[]{:S(2)}) %collective-permute-start.35) | collective-permute-done | bytes 294944 | tf_op jit(solution)/shard_map/ppermute | solution.py:24
  174.5 2.7 %collective-permute-start.39 = (bf16[4,48,768]{2,1,0:T(8,128)(2,1)S(1)}, bf16[4,48,768]{2,1,0:T(8,128)(2,1)S(1)}, u32[]{:S(2)}, u32[]{:S(2)}) collective-permute-start(bf16[4,48,768]{2,1,0:T(8,128)(2,1)S(1)} %get-tuple-element.316), channel_id=1, source_target_pairs={{0,16},{2,18},{4,20},{6,22},{8,24},{10,26},{12,28},{14,30},{16,0},... | collective-permute-start | bytes 884744 | tf_op jit(solution)/shard_map/ppermute | solution.py:24
  177.1 10.1 %attend_back.1 = (bf16[512,1152]{1,0:T(8,128)(2,1)S(1)}, bf16[512,1152]{1,0:T(8,128)(2,1)S(1)}, f32[16,768]{1,0:T(8,128)S(1)}) custom-call(s32[4]{0:T(128)S(1)} %pad_add_fusion.refs_0_.place, bf16[512,768]{1,0:T(8,128)(2,1)S(1)} %get-tuple-element.321.refs_1_, bf16[512,1280]{1,0:T(8,128)(2,1)S(1)} %copy-done, bf16[512,1280]{1,0:T(8,128)(2,1)S(1)} %copy-done.2, ...), custom_call_target="tpu_custom_call" | custom-call | flops 1 | bytes 1 | tf_op jit(solution)/shard_map/attend_back/pallas_call | solution.py:641
  187.2 2.2 collective-permute-done.39.received
  194.9 4.6 %attention_gradient.1 = (bf16[384,896]{1,0:T(8,128)(2,1)S(1)}, bf16[384,896]{1,0:T(8,128)(2,1)S(1)}, bf16[384,768]{1,0:T(8,128)(2,1)S(1)}, bf16[384,768]{1,0:T(8,128)(2,1)S(1)}) custom-call(s32[4]{0:T(128)S(1)} %pad_add_fusion.refs_0_.place, f32[16,768]{1,0:T(8,128)S(1)} %get-tuple-element.338.refs_1_, f32[16,768]{1,0:T(8,128)S(1)} %collective-permute-done.44.refs_2_, ...), custom_call_target="tpu_custom_call" | custom-call | flops 1 | bytes 1 | tf_op jit(solution)/shard_map/attention_gradient/pallas_call | solution.py:641
  200.3 1.4 collective-permute-start.48
  202.3 1.4 collective-permute-start.51
  205.0 9.7 %input_back.1 = bf16[512,768]{1,0:T(8,128)(2,1)} custom-call(s32[4]{0:T(128)S(1)} %pad_add_fusion.refs_0_.place, bf16[512,1152]{1,0:T(8,128)(2,1)S(1)} %get-tuple-element.352.refs_7_.refs_1_, bf16[512,1152]{1,0:T(8,128)(2,1)S(1)} %get-tuple-element.341.refs_2_, bf16[768,768]{1,0:T(8,128)(2,1)S(1)} %copy-done.4, bf16[768,512]{1,0:T(8,128)(2,1)S(1)} %copy-done.6, ...), custom_call_target="tpu_custom_call" | custom-call | flops 1 | bytes 1 | tf_op jit(solution)/shard_map/input_back/pallas_call | solution.py:641
  214.7 2.6 %collective-permute-done.51.received = bf16[96,1536]{1,0:T(8,128)(2,1)S(1)} collective-permute-done((bf16[96,1536]{1,0:T(8,128)(2,1)S(1)}, bf16[96,1536]{1,0:T(8,128)(2,1)S(1)}, u32[]{:S(2)}, u32[]{:S(2)}) %collective-permute-start.51) | collective-permute-done | bytes 294944 | tf_op jit(solution)/shard_map/ppermute | solution.py:24
  220.8 4.3 %collective-permute-done.54.refs_0_ = bf16[48,1536]{1,0:T(8,128)(2,1)S(1)} collective-permute-done((bf16[48,1536]{1,0:T(8,128)(2,1)S(1)}, bf16[48,1536]{1,0:T(8,128)(2,1)S(1)}, u32[]{:S(2)}, u32[]{:S(2)}) %collective-permute-start.54) | collective-permute-done | bytes 147488 | tf_op jit(solution)/shard_map/ppermute | solution.py:24
  225.1 2.2 collective-permute-done.53.right_in
  227.9 2.7 %collective-permute-start.57 = (bf16[48,1664]{1,0:T(8,128)(2,1)S(1)}, bf16[48,1664]{1,0:T(8,128)(2,1)S(1)}, u32[]{:S(2)}, u32[]{:S(2)}) collective-permute-start(bf16[48,1664]{1,0:T(8,128)(2,1)S(1)} %get-tuple-element.381), channel_id=1, source_target_pairs={{0,16},{2,18},{4,20},{6,22},{8,24},{10,26},{12,28},{14,30},{16,0},... | collective-permute-start | bytes 479240 | tf_op jit(solution)/shard_map/ppermute | solution.py:24
  230.6 1.7 collective-permute-start.58
  235.6 6.9 %collective-permute-done.57.refs_1_ = bf16[48,1664]{1,0:T(8,128)(2,1)S(1)} collective-permute-done((bf16[48,1664]{1,0:T(8,128)(2,1)S(1)}, bf16[48,1664]{1,0:T(8,128)(2,1)S(1)}, u32[]{:S(2)}, u32[]{:S(2)}) %collective-permute-start.57) | collective-permute-done | bytes 159776 | tf_op jit(solution)/shard_map/ppermute | solution.py:24
  243.2 1.4 collective-permute-done.60.received
  244.6 1.4 rest_out.1
  (139 shorter events, 43.0 us)
Async XLA Ops:
  2.6 16.8 %collective-permute-start.3 = (bf16[24,3840]{1,0:T(8,128)(2,1)}, bf16[24,3840]{1,0:T(8,128)(2,1)S(1)}, u32[]{:S(2)}, u32[]{:S(2)}) collective-permute-start(bf16[24,3840]{1,0:T(8,128)(2,1)} %get-tuple-element.220.first), channel_id=1, source_target_pairs={{0,8},{2,10},{4,12},{6,14},{8,0},{10,2},{12,4},{14,6},{16,24},{18,... | collective-permute-start | bytes 552968 | tf_op jit(solution)/shard_map/ppermute | solution.py:24
  5.7 10.9 %collective-permute-start.2 = (bf16[24,2560]{1,0:T(8,128)(2,1)}, bf16[24,2560]{1,0:T(8,128)(2,1)S(1)}, u32[]{:S(2)}, u32[]{:S(2)}) collective-permute-start(bf16[24,2560]{1,0:T(8,128)(2,1)} %get-tuple-element.213.refs_0_), channel_id=1, source_target_pairs={{0,24},{2,26},{4,28},{6,30},{8,16},{10,18},{12,20},{14,22},{16,8},... | collective-permute-start | bytes 368648 | tf_op jit(solution)/shard_map/ppermute | solution.py:24
  8.2 11.3 %collective-permute-start.1 = (bf16[24,2560]{1,0:T(8,128)(2,1)}, bf16[24,2560]{1,0:T(8,128)(2,1)S(1)}, u32[]{:S(2)}, u32[]{:S(2)}) collective-permute-start(bf16[24,2560]{1,0:T(8,128)(2,1)} %get-tuple-element.213.refs_0_), channel_id=1, source_target_pairs={{0,16},{2,18},{4,20},{6,22},{8,24},{10,26},{12,28},{14,30},{16,0},... | collective-permute-start | bytes 368648 | tf_op jit(solution)/shard_map/ppermute | solution.py:24
  8.3 11.1 %collective-permute-start = (bf16[24,2560]{1,0:T(8,128)(2,1)}, bf16[24,2560]{1,0:T(8,128)(2,1)S(1)}, u32[]{:S(2)}, u32[]{:S(2)}) collective-permute-start(bf16[24,2560]{1,0:T(8,128)(2,1)} %get-tuple-element.213.refs_0_), channel_id=1, source_target_pairs={{0,8},{2,10},{4,12},{6,14},{8,0},{10,2},{12,4},{14,6},{16,24},{18,... | collective-permute-start | bytes 368648 | tf_op jit(solution)/shard_map/ppermute | solution.py:24
  21.4 12.2 %collective-permute-start.4 = (bf16[96,1280]{1,0:T(8,128)(2,1)S(1)}, bf16[96,1280]{1,0:T(8,128)(2,1)S(1)}, u32[]{:S(2)}, u32[]{:S(2)}) collective-permute-start(bf16[96,1280]{1,0:T(8,128)(2,1)S(1)} %get-tuple-element.223.left), channel_id=1, source_target_pairs={{0,4},{2,6},{4,0},{6,2},{8,12},{10,14},{12,8},{14,10},{16,20},{18,... | collective-permute-start | bytes 737288 | tf_op jit(solution)/shard_map/ppermute | solution.py:24
  22.9 10.7 %collective-permute-start.5 = (bf16[96,1280]{1,0:T(8,128)(2,1)S(1)}, bf16[96,1280]{1,0:T(8,128)(2,1)S(1)}, u32[]{:S(2)}, u32[]{:S(2)}) collective-permute-start(bf16[96,1280]{1,0:T(8,128)(2,1)S(1)} %get-tuple-element.224.right), channel_id=1, source_target_pairs={{0,1},{1,0},{2,3},{3,2},{4,5},{5,4},{6,7},{7,6},{8,9},{9,8},{10,11... | collective-permute-start | bytes 737288 | tf_op jit(solution)/shard_map/ppermute | solution.py:28
  24.5 9.2 %collective-permute-start.6 = (bf16[48,1792]{1,0:T(8,128)(2,1)S(1)}, bf16[48,1792]{1,0:T(8,128)(2,1)S(1)}, u32[]{:S(2)}, u32[]{:S(2)}) collective-permute-start(bf16[48,1792]{1,0:T(8,128)(2,1)S(1)} %get-tuple-element.221.left), channel_id=1, source_target_pairs={{0,16},{2,18},{4,20},{6,22},{8,24},{10,26},{12,28},{14,30},{16,0},... | collective-permute-start | bytes 516104 | tf_op jit(solution)/shard_map/ppermute | solution.py:24
  33.8 14.0 %collective-permute-start.7 = (bf16[192,2560]{1,0:T(8,128)(2,1)S(1)}, bf16[192,2560]{1,0:T(8,128)(2,1)}, u32[]{:S(2)}, u32[]{:S(2)}) collective-permute-start(bf16[192,2560]{1,0:T(8,128)(2,1)S(1)} %get-tuple-element.227), channel_id=1, source_target_pairs={{0,2},{2,0},{4,6},{6,4},{8,10},{10,8},{12,14},{14,12},{16,18},{18,... | collective-permute-start | bytes 2949128 | tf_op jit(solution)/shard_map/ppermute | solution.py:24
  33.8 13.6 %collective-permute-start.9 = (bf16[192,1280]{1,0:T(8,128)(2,1)S(1)}, bf16[192,1280]{1,0:T(8,128)(2,1)S(1)}, u32[]{:S(2)}, u32[]{:S(2)}) collective-permute-start(bf16[192,1280]{1,0:T(8,128)(2,1)S(1)} %get-tuple-element.228.refs_3_), channel_id=1, source_target_pairs={{0,4},{2,6},{4,0},{6,2},{8,12},{10,14},{12,8},{14,10},{16,20},{18,... | collective-permute-start | bytes 1474568 | tf_op jit(solution)/shard_map/ppermute | solution.py:24
  34.4 13.3 %collective-permute-start.8 = (bf16[192,1280]{1,0:T(8,128)(2,1)S(1)}, bf16[192,1280]{1,0:T(8,128)(2,1)S(1)}, u32[]{:S(2)}, u32[]{:S(2)}) collective-permute-start(bf16[192,1280]{1,0:T(8,128)(2,1)S(1)} %get-tuple-element.229.refs_6_), channel_id=1, source_target_pairs={{0,1},{1,0},{2,3},{3,2},{4,5},{5,4},{6,7},{7,6},{8,9},{9,8},{10,11... | collective-permute-start | bytes 1474568 | tf_op jit(solution)/shard_map/ppermute | solution.py:28
  34.9 11.3 %collective-permute-start.10 = (bf16[48,2048]{1,0:T(8,128)(2,1)S(1)}, bf16[48,2048]{1,0:T(8,128)(2,1)S(1)}, u32[]{:S(2)}, u32[]{:S(2)}) collective-permute-start(bf16[48,2048]{1,0:T(8,128)(2,1)S(1)} %get-tuple-element.230.right), channel_id=1, source_target_pairs={{0,16},{2,18},{4,20},{6,22},{8,24},{10,26},{12,28},{14,30},{16,0},... | collective-permute-start | bytes 589832 | tf_op jit(solution)/shard_map/ppermute | solution.py:24
  49.5 11.3 %collective-permute-start.15 = (bf16[96,2048]{1,0:T(8,128)(2,1)}, bf16[96,2048]{1,0:T(8,128)(2,1)}, u32[]{:S(2)}, u32[]{:S(2)}) collective-permute-start(bf16[96,2048]{1,0:T(8,128)(2,1)} %get-tuple-element.233.right), channel_id=1, source_target_pairs={{0,1},{1,0},{2,3},{3,2},{4,5},{5,4},{6,7},{7,6},{8,9},{9,8},{10,11... | collective-permute-start | bytes 1179656 | tf_op jit(solution)/shard_map/ppermute | solution.py:28
  50.0 10.8 %collective-permute-start.14 = (bf16[96,1792]{1,0:T(8,128)(2,1)}, bf16[96,1792]{1,0:T(8,128)(2,1)}, u32[]{:S(2)}, u32[]{:S(2)}) collective-permute-start(bf16[96,1792]{1,0:T(8,128)(2,1)} %get-tuple-element.232.left), channel_id=1, source_target_pairs={{0,4},{2,6},{4,0},{6,2},{8,12},{10,14},{12,8},{14,10},{16,20},{18,... | collective-permute-start | bytes 1032200 | tf_op jit(solution)/shard_map/ppermute | solution.py:24
  51.5 8.2 %collective-permute-start.13 = (bf16[96,768]{1,0:T(8,128)(2,1)S(1)}, bf16[96,768]{1,0:T(8,128)(2,1)}, u32[]{:S(2)}, u32[]{:S(2)}) collective-permute-start(bf16[96,768]{1,0:T(8,128)(2,1)S(1)} %copy-done.10), channel_id=1, source_target_pairs={{0,8},{2,10},{4,12},{6,14},{8,0},{10,2},{12,4},{14,6},{16,24},{18,... | collective-permute-start | bytes 442376 | tf_op jit(solution)/shard_map/ppermute | solution.py:24
  62.3 20.0 %collective-permute-start.19 = (bf16[192,3840]{1,0:T(8,128)(2,1)S(1)}, bf16[192,3840]{1,0:T(8,128)(2,1)S(1)}, u32[]{:S(2)}, u32[]{:S(2)}) collective-permute-start(bf16[192,3840]{1,0:T(8,128)(2,1)S(1)} %get-tuple-element.251), channel_id=1, source_target_pairs={{0,2},{2,0},{4,6},{6,4},{8,10},{10,8},{12,14},{14,12},{16,18},{18,... | collective-permute-start | bytes 4423688 | tf_op jit(solution)/shard_map/ppermute | solution.py:24
  62.4 19.9 %collective-permute-start.17 = (bf16[192,2048]{1,0:T(8,128)(2,1)S(1)}, bf16[192,2048]{1,0:T(8,128)(2,1)S(1)}, u32[]{:S(2)}, u32[]{:S(2)}) collective-permute-start(bf16[192,2048]{1,0:T(8,128)(2,1)S(1)} %get-tuple-element.245.refs_6_), channel_id=1, source_target_pairs={{0,4},{2,6},{4,0},{6,2},{8,12},{10,14},{12,8},{14,10},{16,20},{18,... | collective-permute-start | bytes 2359304 | tf_op jit(solution)/shard_map/ppermute | solution.py:24
  63.9 17.5 %collective-permute-start.16 = (bf16[192,1792]{1,0:T(8,128)(2,1)S(1)}, bf16[192,1792]{1,0:T(8,128)(2,1)S(1)}, u32[]{:S(2)}, u32[]{:S(2)}) collective-permute-start(bf16[192,1792]{1,0:T(8,128)(2,1)S(1)} %get-tuple-element.244.refs_3_.refs_2_), channel_id=1, source_target_pairs={{0,1},{1,0},{2,3},{3,2},{4,5},{5,4},{6,7},{7,6},{8,9},{9,8},{10,11... | collective-permute-start | bytes 2064392 | tf_op jit(solution)/shard_map/ppermute | solution.py:28
  64.6 16.0 %collective-permute-start.18 = (bf16[192,768]{1,0:T(8,128)(2,1)S(1)}, bf16[192,768]{1,0:T(8,128)(2,1)S(1)}, u32[]{:S(2)}, u32[]{:S(2)}) collective-permute-start(bf16[192,768]{1,0:T(8,128)(2,1)S(1)} %stack_z_two.1.refs_0_), channel_id=1, source_target_pairs={{0,16},{2,18},{4,20},{6,22},{8,24},{10,26},{12,28},{14,30},{16,0},... | collective-permute-start | bytes 884744 | tf_op jit(solution)/shard_map/ppermute | solution.py:24
  82.4 10.8 %collective-permute-start.23 = (bf16[192,2048]{1,0:T(8,128)(2,1)S(1)}, bf16[192,2048]{1,0:T(8,128)(2,1)S(1)}, u32[]{:S(2)}, u32[]{:S(2)}) collective-permute-start(bf16[192,2048]{1,0:T(8,128)(2,1)S(1)} %collective-permute-done.17.refs_7_), channel_id=1, source_target_pairs={{0,2},{2,0},{4,6},{6,4},{8,10},{10,8},{12,14},{14,12},{16,18},{18,... | collective-permute-start | bytes 2359304 | tf_op jit(solution)/shard_map/ppermute | solution.py:24
  83.0 9.0 %collective-permute-start.21 = (bf16[384,384]{1,0:T(8,128)(2,1)S(1)}, bf16[384,384]{1,0:T(8,128)(2,1)S(1)}, u32[]{:S(2)}, u32[]{:S(2)}) collective-permute-start(bf16[384,384]{1,0:T(8,128)(2,1)S(1)} %get-tuple-element.253.left), channel_id=1, source_target_pairs={{0,4},{2,6},{4,0},{6,2},{8,12},{10,14},{12,8},{14,10},{16,20},{18,... | collective-permute-start | bytes 884744 | tf_op jit(solution)/shard_map/ppermute | solution.py:24
  84.5 8.7 %collective-permute-start.22 = (bf16[384,384]{1,0:T(8,128)(2,1)S(1)}, bf16[384,384]{1,0:T(8,128)(2,1)S(1)}, u32[]{:S(2)}, u32[]{:S(2)}) collective-permute-start(bf16[384,384]{1,0:T(8,128)(2,1)S(1)} %get-tuple-element.254.right), channel_id=1, source_target_pairs={{0,1},{1,0},{2,3},{3,2},{4,5},{5,4},{6,7},{7,6},{8,9},{9,8},{10,11... | collective-permute-start | bytes 884744 | tf_op jit(solution)/shard_map/ppermute | solution.py:28
  93.4 25.3 %collective-permute-start.26 = (bf16[768,768]{1,0:T(8,128)(2,1)S(1)}, bf16[768,768]{1,0:T(8,128)(2,1)S(1)}, u32[]{:S(2)}, u32[]{:S(2)}) collective-permute-start(bf16[768,768]{1,0:T(8,128)(2,1)S(1)} %get-tuple-element.266), channel_id=1, source_target_pairs={{0,2},{2,0},{4,6},{6,4},{8,10},{10,8},{12,14},{14,12},{16,18},{18,... | collective-permute-start | bytes 3538952 | tf_op jit(solution)/shard_map/ppermute | solution.py:24
  93.5 25.2 %collective-permute-start.24 = (bf16[768,384]{1,0:T(8,128)(2,1)S(1)}, bf16[768,384]{1,0:T(8,128)(2,1)S(1)}, u32[]{:S(2)}, u32[]{:S(2)}) collective-permute-start(bf16[768,384]{1,0:T(8,128)(2,1)S(1)} %get-tuple-element.261.refs_4_), channel_id=1, source_target_pairs={{0,1},{1,0},{2,3},{3,2},{4,5},{5,4},{6,7},{7,6},{8,9},{9,8},{10,11... | collective-permute-start | bytes 1769480 | tf_op jit(solution)/shard_map/ppermute | solution.py:28
  94.2 24.4 %collective-permute-start.25 = (bf16[768,384]{1,0:T(8,128)(2,1)S(1)}, bf16[768,384]{1,0:T(8,128)(2,1)S(1)}, u32[]{:S(2)}, u32[]{:S(2)}) collective-permute-start(bf16[768,384]{1,0:T(8,128)(2,1)S(1)} %get-tuple-element.262.refs_8_), channel_id=1, source_target_pairs={{0,4},{2,6},{4,0},{6,2},{8,12},{10,14},{12,8},{14,10},{16,20},{18,... | collective-permute-start | bytes 1769480 | tf_op jit(solution)/shard_map/ppermute | solution.py:24
  121.6 17.1 %collective-permute-start.29 = (bf16[3072,512]{1,0:T(8,128)(2,1)S(1)}, bf16[3072,512]{1,0:T(8,128)(2,1)S(1)}, u32[]{:S(2)}, u32[]{:S(2)}) collective-permute-start(bf16[3072,512]{1,0:T(8,128)(2,1)S(1)} %get-tuple-element.272.refs_1_), channel_id=1, source_target_pairs={{0,2},{2,0},{4,6},{6,4},{8,10},{10,8},{12,14},{14,12},{16,18},{18,... | collective-permute-start | bytes 9437192 | tf_op jit(solution)/shard_map/ppermute | solution.py:24
  134.1 4.6 %collective-permute-start.31 = (bf16[512,384]{1,0:T(8,128)(2,1)S(1)}, bf16[512,384]{1,0:T(8,128)(2,1)S(1)}, u32[]{:S(2)}, u32[]{:S(2)}) collective-permute-start(bf16[512,384]{1,0:T(8,128)(2,1)S(1)} %get-tuple-element.277.refs_2_), channel_id=1, source_target_pairs={{0,2},{2,0},{4,6},{6,4},{8,10},{10,8},{12,14},{14,12},{16,18},{18,... | collective-permute-start | bytes 1179656 | tf_op jit(solution)/shard_map/ppermute | solution.py:24
  145.1 16.1 %collective-permute-start.34 = (bf16[512,1536]{1,0:T(8,128)(2,1)S(1)}, bf16[512,1536]{1,0:T(8,128)(2,1)S(1)}, u32[]{:S(2)}, u32[]{:S(2)}) collective-permute-start(bf16[512,1536]{1,0:T(8,128)(2,1)S(1)} %get-tuple-element.288.refs_2_), channel_id=1, source_target_pairs={{0,2},{2,0},{4,6},{6,4},{8,10},{10,8},{12,14},{14,12},{16,18},{18,... | collective-permute-start | bytes 4718600 | tf_op jit(solution)/shard_map/ppermute | solution.py:24
  145.6 15.3 %collective-permute-start.32 = (bf16[16,48,384]{2,1,0:T(8,128)(2,1)S(1)}, bf16[16,48,384]{2,1,0:T(8,128)(2,1)S(1)}, u32[]{:S(2)}, u32[]{:S(2)}) collective-permute-start(bf16[16,48,384]{2,1,0:T(8,128)(2,1)S(1)} %get-tuple-element.283), channel_id=1, source_target_pairs={{0,1},{1,0},{2,3},{3,2},{4,5},{5,4},{6,7},{7,6},{8,9},{9,8},{10,11... | collective-permute-start | bytes 1769480 | tf_op jit(solution)/shard_map/ppermute | solution.py:28
  146.2 15.0 %collective-permute-start.33 = (bf16[16,48,384]{2,1,0:T(8,128)(2,1)S(1)}, bf16[16,48,384]{2,1,0:T(8,128)(2,1)S(1)}, u32[]{:S(2)}, u32[]{:S(2)}) collective-permute-start(bf16[16,48,384]{2,1,0:T(8,128)(2,1)S(1)} %get-tuple-element.284), channel_id=1, source_target_pairs={{0,4},{2,6},{4,0},{6,2},{8,12},{10,14},{12,8},{14,10},{16,20},{18,... | collective-permute-start | bytes 1769480 | tf_op jit(solution)/shard_map/ppermute | solution.py:24
  147.7 16.2 %collective-permute-start.38 = (bf16[768,512]{1,0:T(8,128)(2,1)S(1)}, bf16[768,512]{1,0:T(8,128)(2,1)S(1)}, u32[]{:S(2)}, u32[]{:S(2)}) collective-permute-start(bf16[768,512]{1,0:T(8,128)(2,1)S(1)} %get-tuple-element.307.refs_0_), channel_id=1, source_target_pairs={{0,2},{2,0},{4,6},{6,4},{8,10},{10,8},{12,14},{14,12},{16,18},{18,... | collective-permute-start | bytes 2359304 | tf_op jit(solution)/shard_map/ppermute | solution.py:24
  161.5 10.7 %collective-permute-start.37 = (bf16[512,384]{1,0:T(8,128)(2,1)S(1)}, bf16[512,384]{1,0:T(8,128)(2,1)S(1)}, u32[]{:S(2)}, u32[]{:S(2)}) collective-permute-start(bf16[512,384]{1,0:T(8,128)(2,1)S(1)} %get-tuple-element.306), channel_id=1, source_target_pairs={{0,2},{2,0},{4,6},{6,4},{8,10},{10,8},{12,14},{14,12},{16,18},{18,... | collective-permute-start | bytes 1179656 | tf_op jit(solution)/shard_map/ppermute | solution.py:24
  161.6 9.4 %collective-permute-start.35 = (bf16[8,48,384]{2,1,0:T(8,128)(2,1)S(1)}, bf16[8,48,384]{2,1,0:T(8,128)(2,1)S(1)}, u32[]{:S(2)}, u32[]{:S(2)}) collective-permute-start(bf16[8,48,384]{2,1,0:T(8,128)(2,1)S(1)} %get-tuple-element.302), channel_id=1, source_target_pairs={{0,4},{2,6},{4,0},{6,2},{8,12},{10,14},{12,8},{14,10},{16,20},{18,... | collective-permute-start | bytes 884744 | tf_op jit(solution)/shard_map/ppermute | solution.py:24
  163.2 9.1 %collective-permute-start.36 = (bf16[8,48,384]{2,1,0:T(8,128)(2,1)S(1)}, bf16[8,48,384]{2,1,0:T(8,128)(2,1)S(1)}, u32[]{:S(2)}, u32[]{:S(2)}) collective-permute-start(bf16[8,48,384]{2,1,0:T(8,128)(2,1)S(1)} %get-tuple-element.303), channel_id=1, source_target_pairs={{0,1},{1,0},{2,3},{3,2},{4,5},{5,4},{6,7},{7,6},{8,9},{9,8},{10,11... | collective-permute-start | bytes 884744 | tf_op jit(solution)/shard_map/ppermute | solution.py:28
  172.4 17.0 %collective-permute-start.40 = (bf16[384,768]{1,0:T(8,128)(2,1)S(1)}, bf16[384,768]{1,0:T(8,128)(2,1)S(1)}, u32[]{:S(2)}, u32[]{:S(2)}) collective-permute-start(bf16[384,768]{1,0:T(8,128)(2,1)S(1)} %get-tuple-element.318), channel_id=1, source_target_pairs={{0,1},{1,0},{2,3},{3,2},{4,5},{5,4},{6,7},{7,6},{8,9},{9,8},{10,11... | collective-permute-start | bytes 1769480 | tf_op jit(solution)/shard_map/ppermute | solution.py:28
  173.2 16.3 %collective-permute-start.41 = (bf16[384,768]{1,0:T(8,128)(2,1)S(1)}, bf16[384,768]{1,0:T(8,128)(2,1)S(1)}, u32[]{:S(2)}, u32[]{:S(2)}) collective-permute-start(bf16[384,768]{1,0:T(8,128)(2,1)S(1)} %get-tuple-element.319), channel_id=1, source_target_pairs={{0,4},{2,6},{4,0},{6,2},{8,12},{10,14},{12,8},{14,10},{16,20},{18,... | collective-permute-start | bytes 1769480 | tf_op jit(solution)/shard_map/ppermute | solution.py:24
  174.5 14.9 %collective-permute-start.39 = (bf16[4,48,768]{2,1,0:T(8,128)(2,1)S(1)}, bf16[4,48,768]{2,1,0:T(8,128)(2,1)S(1)}, u32[]{:S(2)}, u32[]{:S(2)}) collective-permute-start(bf16[4,48,768]{2,1,0:T(8,128)(2,1)S(1)} %get-tuple-element.316), channel_id=1, source_target_pairs={{0,16},{2,18},{4,20},{6,22},{8,24},{10,26},{12,28},{14,30},{16,0},... | collective-permute-start | bytes 884744 | tf_op jit(solution)/shard_map/ppermute | solution.py:24
  190.4 9.4 %collective-permute-start.42 = (bf16[192,768]{1,0:T(8,128)(2,1)S(1)}, bf16[192,768]{1,0:T(8,128)(2,1)S(1)}, u32[]{:S(2)}, u32[]{:S(2)}) collective-permute-start(bf16[192,768]{1,0:T(8,128)(2,1)S(1)} %get-tuple-element.330), channel_id=1, source_target_pairs={{0,4},{2,6},{4,0},{6,2},{8,12},{10,14},{12,8},{14,10},{16,20},{18,... | collective-permute-start | bytes 884744 | tf_op jit(solution)/shard_map/ppermute | solution.py:24
  191.1 9.1 %collective-permute-start.43 = (bf16[192,768]{1,0:T(8,128)(2,1)S(1)}, bf16[192,768]{1,0:T(8,128)(2,1)S(1)}, u32[]{:S(2)}, u32[]{:S(2)}) collective-permute-start(bf16[192,768]{1,0:T(8,128)(2,1)S(1)} %get-tuple-element.332), channel_id=1, source_target_pairs={{0,1},{1,0},{2,3},{3,2},{4,5},{5,4},{6,7},{7,6},{8,9},{9,8},{10,11... | collective-permute-start | bytes 884744 | tf_op jit(solution)/shard_map/ppermute | solution.py:28
  200.3 17.0 %collective-permute-start.48 = (bf16[384,896]{1,0:T(8,128)(2,1)S(1)}, bf16[384,896]{1,0:T(8,128)(2,1)S(1)}, u32[]{:S(2)}, u32[]{:S(2)}) collective-permute-start(bf16[384,896]{1,0:T(8,128)(2,1)S(1)} %get-tuple-element.360), channel_id=1, source_target_pairs={{0,1},{1,0},{2,3},{3,2},{4,5},{5,4},{6,7},{7,6},{8,9},{9,8},{10,11... | collective-permute-start | bytes 2064392 | tf_op jit(solution)/shard_map/ppermute | solution.py:28
  201.6 15.6 %collective-permute-start.49 = (bf16[384,768]{1,0:T(8,128)(2,1)S(1)}, bf16[384,768]{1,0:T(8,128)(2,1)S(1)}, u32[]{:S(2)}, u32[]{:S(2)}) collective-permute-start(bf16[384,768]{1,0:T(8,128)(2,1)S(1)} %get-tuple-element.361), channel_id=1, source_target_pairs={{0,4},{2,6},{4,0},{6,2},{8,12},{10,14},{12,8},{14,10},{16,20},{18,... | collective-permute-start | bytes 1769480 | tf_op jit(solution)/shard_map/ppermute | solution.py:24
  202.3 15.0 %collective-permute-start.51 = (bf16[96,1536]{1,0:T(8,128)(2,1)S(1)}, bf16[96,1536]{1,0:T(8,128)(2,1)S(1)}, u32[]{:S(2)}, u32[]{:S(2)}) collective-permute-start(bf16[96,1536]{1,0:T(8,128)(2,1)S(1)} %get-tuple-element.363), channel_id=1, source_target_pairs={{0,16},{2,18},{4,20},{6,22},{8,24},{10,26},{12,28},{14,30},{16,0},... | collective-permute-start | bytes 884744 | tf_op jit(solution)/shard_map/ppermute | solution.py:24
  203.6 11.1 %collective-permute-start.50 = (bf16[2,48,768]{2,1,0:T(8,128)(2,1)S(1)}, bf16[2,48,768]{2,1,0:T(8,128)(2,1)S(1)}, u32[]{:S(2)}, u32[]{:S(2)}) collective-permute-start(bf16[2,48,768]{2,1,0:T(8,128)(2,1)S(1)} %get-tuple-element.362), channel_id=1, source_target_pairs={{0,8},{2,10},{4,12},{6,14},{8,0},{10,2},{12,4},{14,6},{16,24},{18,... | collective-permute-start | bytes 442376 | tf_op jit(solution)/shard_map/ppermute | solution.py:24
  217.6 10.0 %collective-permute-start.52 = (bf16[192,896]{1,0:T(8,128)(2,1)S(1)}, bf16[192,896]{1,0:T(8,128)(2,1)S(1)}, u32[]{:S(2)}, u32[]{:S(2)}) collective-permute-start(bf16[192,896]{1,0:T(8,128)(2,1)S(1)} %get-tuple-element.368), channel_id=1, source_target_pairs={{0,4},{2,6},{4,0},{6,2},{8,12},{10,14},{12,8},{14,10},{16,20},{18,... | collective-permute-start | bytes 1032200 | tf_op jit(solution)/shard_map/ppermute | solution.py:24
  218.7 8.5 %collective-permute-start.53 = (bf16[192,768]{1,0:T(8,128)(2,1)S(1)}, bf16[192,768]{1,0:T(8,128)(2,1)S(1)}, u32[]{:S(2)}, u32[]{:S(2)}) collective-permute-start(bf16[192,768]{1,0:T(8,128)(2,1)S(1)} %get-tuple-element.369), channel_id=1, source_target_pairs={{0,1},{1,0},{2,3},{3,2},{4,5},{5,4},{6,7},{7,6},{8,9},{9,8},{10,11... | collective-permute-start | bytes 884744 | tf_op jit(solution)/shard_map/ppermute | solution.py:28
  219.8 5.3 %collective-permute-start.54 = (bf16[48,1536]{1,0:T(8,128)(2,1)S(1)}, bf16[48,1536]{1,0:T(8,128)(2,1)S(1)}, u32[]{:S(2)}, u32[]{:S(2)}) collective-permute-start(bf16[48,1536]{1,0:T(8,128)(2,1)S(1)} %get-tuple-element.373), channel_id=1, source_target_pairs={{0,8},{2,10},{4,12},{6,14},{8,0},{10,2},{12,4},{14,6},{16,24},{18,... | collective-permute-start | bytes 442376 | tf_op jit(solution)/shard_map/ppermute | solution.py:24
  227.8 7.8 %collective-permute-start.56 = (bf16[48,1664]{1,0:T(8,128)(2,1)S(1)}, bf16[48,1664]{1,0:T(8,128)(2,1)S(1)}, u32[]{:S(2)}, u32[]{:S(2)}) collective-permute-start(bf16[48,1664]{1,0:T(8,128)(2,1)S(1)} %get-tuple-element.380), channel_id=1, source_target_pairs={{0,8},{2,10},{4,12},{6,14},{8,0},{10,2},{12,4},{14,6},{16,24},{18,... | collective-permute-start | bytes 479240 | tf_op jit(solution)/shard_map/ppermute | solution.py:24
  227.9 14.6 %collective-permute-start.57 = (bf16[48,1664]{1,0:T(8,128)(2,1)S(1)}, bf16[48,1664]{1,0:T(8,128)(2,1)S(1)}, u32[]{:S(2)}, u32[]{:S(2)}) collective-permute-start(bf16[48,1664]{1,0:T(8,128)(2,1)S(1)} %get-tuple-element.381), channel_id=1, source_target_pairs={{0,16},{2,18},{4,20},{6,22},{8,24},{10,26},{12,28},{14,30},{16,0},... | collective-permute-start | bytes 479240 | tf_op jit(solution)/shard_map/ppermute | solution.py:24
  230.6 11.9 %collective-permute-start.58 = (bf16[48,1664]{1,0:T(8,128)(2,1)S(1)}, bf16[48,1664]{1,0:T(8,128)(2,1)S(1)}, u32[]{:S(2)}, u32[]{:S(2)}) collective-permute-start(bf16[48,1664]{1,0:T(8,128)(2,1)S(1)} %get-tuple-element.382), channel_id=1, source_target_pairs={{0,24},{2,26},{4,28},{6,30},{8,16},{10,18},{12,20},{14,22},{16,8},... | collective-permute-start | bytes 479240 | tf_op jit(solution)/shard_map/ppermute | solution.py:24
  (27 other events, 184.6 us)
